TPU v7x, 256 devices: a whole 4x4x8 slice. The times are simulated.
256 devices in a mesh: row: 16 (over x, z_hi, core), col: 4 (over z_lo), depth: 4 (over y).
Axes of the slice: x: 4, y: 4, z: 8 (z_hi: 2, z_lo: 4; z = z_hi * 4 + z_lo), core: 2. Of those that a mesh axis runs over, the one named last changes fastest.
Arguments:
- density: float32 [1024, 5, 128, 128], P('row', None, ('col', 'depth')), may hold values from -1 to 1
- mask_band: int32 [1024, 5], P('row'), may hold values 0 or 1
- mask_square: int32 [1024, 9], P('row'), may hold values 0 or 1
- mask_out: int32 [1024, 5], P('row'), may hold values 0 or 1
Outputs:
- purified: float32 [1024, 5, 128, 128], P('row', None, ('col', 'depth'))
All inputs are finite; a program needn't handle non-finite values. No bound on the sum of `mask_band` or of `mask_square` or of `mask_out` on one device may be relied on, other than what follows from the above.
Results may differ from a plain program's by a relative error of at most 0.0003.
Values sent between devices are 32-bit elements; how exact they have to be, the bound alone decides.
No kernel may reach another device: no remote copies, remote signals or barrier semaphores. Data moves between devices by JAX's collectives and lax.ppermute only.
A program may use at most 64 MiB of HBM per device.

v0:
```python
import jax
import jax.numpy as jnp
from jax import lax
from jax.sharding import PartitionSpec as P


def padded(value, sides, width):
    for axis, dim in sides:
        size, length = (lax.axis_size(axis), value.shape[dim])
        up = [(i, (i + 1) % size) for i in range(size - 1)]
        down = [(j, i) for i, j in up]
        last = lax.slice_in_dim(value, length - width, length, axis=dim)
        initial = lax.slice_in_dim(value, 0, width, axis=dim)
        before = lax.ppermute(last, axis, up)
        after = lax.ppermute(initial, axis, down)
        value = jnp.concatenate([before, value, after], axis=dim)
    return value


def square_band(left_band, widened, margin):
    span_rows = left_band.shape[0]
    square = jnp.zeros((span_rows, 9, left_band.shape[2], left_band.shape[3]), jnp.float32)
    for offset in range(5):
        lower = offset - 2 + margin
        product = jnp.einsum(
            "rab,rubc->ruac",
            left_band[:, offset],
            widened[lower : lower + span_rows],
            precision=lax.Precision.HIGHEST,
        )
        square = square.at[:, offset : offset + 5].add(product)
    return square


def cube_left(square, widened):
    span_rows = square.shape[0]
    result = jnp.zeros((span_rows, 5, square.shape[2], square.shape[3]), jnp.float32)
    for column in range(9):
        lowest = max(0, 4 - column)
        highest = min(4, 8 - column)
        product = jnp.einsum(
            "rab,rubc->ruac",
            square[:, column],
            widened[column : column + span_rows, lowest : highest + 1],
            precision=lax.Precision.HIGHEST,
        )
        result = result.at[:, lowest + column - 4 : highest + column - 3].add(product)
    return result


def active_band(density, mask_band, first_row, total_rows):
    columns = (
        first_row
        + jnp.arange(density.shape[0], dtype=jnp.int32)[:, None]
        + jnp.arange(5, dtype=jnp.int32)[None, :]
        - 2
    )
    inside = ((columns >= 0) & (columns < total_rows)).astype(jnp.float32)
    return density * (mask_band.astype(jnp.float32) * inside)[:, :, None, None]


def gather_rows(stack):
    return lax.all_to_all(stack, ("col", "depth"), split_axis=0, concat_axis=2, tiled=True)


def on_device(density, mask_band, mask_square, mask_out):
    local_rows = density.shape[0]
    layer_count = lax.axis_size(("col", "depth"))
    whole_rows = local_rows // layer_count
    first_row = lax.axis_index("row") * local_rows
    active = active_band(density, mask_band, first_row, local_rows * lax.axis_size("row"))
    owned_rows = gather_rows(active)
    widened = padded(owned_rows, ((("row", "col", "depth"), 0),), 4)
    owned_rows = widened[4 : 4 + whole_rows]
    piece_start = lax.axis_index(("col", "depth")) * whole_rows
    square_gate = lax.dynamic_slice_in_dim(mask_square, piece_start, whole_rows, 0).astype(
        jnp.float32
    )[:, :, None, None]
    output_gate = lax.dynamic_slice_in_dim(mask_out, piece_start, whole_rows, 0).astype(
        jnp.float32
    )[:, :, None, None]
    square = square_band(owned_rows, widened, 4) * square_gate
    cube_part = cube_left(square, widened)
    purified = output_gate * (3.0 * square[:, 2:7] - 2.0 * cube_part)
    return lax.all_to_all(purified, ("col", "depth"), split_axis=2, concat_axis=0, tiled=True)


def solution(mesh):
    return jax.shard_map(
        on_device,
        mesh=mesh,
        in_specs=(
            P("row", None, ("col", "depth"), None),
            P("row", None),
            P("row", None),
            P("row", None),
        ),
        out_specs=P("row", None, ("col", "depth"), None),
        check_vma=False,
    )
```

profile of v0, /device:TPU:2, one launch (start us, length us, event | category | flops | bytes accessed | tf_op | source)
XLA Modules:
  0.0 152.9 jit_solution(2201040140150104544)
XLA Ops:
  0.0 0.0 copy-start
  0.0 0.7 convert_select_fusion
  0.7 0.1 copy.151
  0.8 1.7 %broadcast_multiply_fusion.1 = f32[64,5,8,128]{3,2,1,0:T(8,128)S(1)} fusion(f32[64,5,8,128]{3,2,1,0:T(8,128)} %param.34, f32[64,5]{1,0:T(8,128)S(1)} %copy.151), kind=kLoop, calls=%fused_computation.72 | loop fusion | flops 327680 | bytes 2622720 | tf_op jit(solution)/shard_map/mul | solution.py:59
  2.5 41.3 %all_to_all.36 = f32[64,5,8,128]{3,2,1,0:T(8,128)S(1)} all-to-all(f32[64,5,8,128]{3,2,1,0:T(8,128)S(1)} %broadcast_multiply_fusion.1), channel_id=1, replica_groups=mesh['row'=16,'col'=4,'depth'=4] {'col','depth'}, dimensions={0} | all-to-all | bytes 2621440 | tf_op jit(solution)/shard_map/all_to_all | solution.py:63
  43.8 0.0 copy-start.1
  43.8 0.0 copy-start.3
  43.8 0.1 copy.270
  43.9 0.9 copy-done.1
  44.9 2.1 %collective-permute-start = (f32[4,5,128,128]{3,2,0,1:T(8,128)S(1)}, f32[4,5,128,128]{3,2,0,1:T(8,128)}, u32[]{:S(2)}, u32[]{:S(2)}) collective-permute-start(f32[4,5,128,128]{3,2,0,1:T(8,128)S(1)} %bitcast.181), channel_id=1, source_target_pairs={{0,1},{1,2},{2,3},{3,4},{4,5},{5,6},{6,7},{7,8},{8,9},{9,10},{10,1... | collective-permute-start | bytes 3932168 | tf_op jit(solution)/shard_map/ppermute | solution.py:14
  47.0 7.6 %collective-permute-start.1 = (f32[4,5,128,128]{3,2,0,1:T(8,128)S(1)}, f32[4,5,128,128]{3,2,0,1:T(8,128)S(1)}, u32[]{:S(2)}, u32[]{:S(2)}) collective-permute-start(f32[4,5,128,128]{3,2,0,1:T(8,128)S(1)} %bitcast.182), channel_id=1, source_target_pairs={{1,0},{2,1},{3,2},{4,3},{5,4},{6,5},{7,6},{8,7},{9,8},{10,9},{11,1... | collective-permute-start | bytes 3932168 | tf_op jit(solution)/shard_map/ppermute | solution.py:15
  54.7 0.0 copy-done
  54.7 0.1 constant_dynamic-slice_fusion
  54.7 0.1 copy.234
  54.8 0.0 copy-done.3
  54.8 0.1 dynamic-slice_convert_fusion
  54.9 0.1 copy.150
  55.0 25.2 %collective-permute-done = f32[4,5,128,128]{3,2,0,1:T(8,128)} collective-permute-done((f32[4,5,128,128]{3,2,0,1:T(8,128)S(1)}, f32[4,5,128,128]{3,2,0,1:T(8,128)}, u32[]{:S(2)}, u32[]{:S(2)}) %collective-permute-start) | collective-permute-done | bytes 1310752 | tf_op jit(solution)/shard_map/ppermute | solution.py:14
  80.2 0.1 collective-permute-done.1
  80.3 1.8 %fusion.13 = (f32[4,5,128,128]{3,2,0,1:T(8,128)S(1)}, f32[4,5,128,128]{3,2,0,1:T(8,128)S(1)}, f32[4,5,128,128]{3,2,0,1:T(8,128)S(1)}, f32[4,5,128,128]{3,2,0,1:T(8,128)S(1)}) fusion(f32[4,5,128,128]{3,2,0,1:T(8,128)S(1)} %bitcast.183, f32[4,5,128,128]{3,2,0,1:T(8,128)S(1)} %collective-permute-done.1, f32[4,5,128,128]{3,2,0,1:T(8,128)} %collective-permute-done), kind=kLoop, calls=%fused_computation.37 | loop fusion | flops 1310720 | bytes 9175040 | tf_op jit(solution)/shard_map/concatenate | solution.py:16
  82.2 2.2 %convolution_bitcast_fusion.5 = f32[4,5,128,128]{2,3,1,0:T(8,128)S(1)} fusion(f32[4,5,128,128]{3,2,0,1:T(8,128)S(1)} %get-tuple-element.191, f32[4,5,128,128]{3,2,0,1:T(8,128)S(1)} %bitcast.184), kind=kOutput, calls=%fused_computation.30 | convolution fusion | flops 503316480 | bytes 2883584 | tf_op jit(solution)/shard_map/rab,rubc->ruac/dot_general | solution.py:25
  84.4 0.2 scatter-add.44
  84.7 2.4 %fusion.8 = f32[4,9,128,128]{2,3,1,0:T(8,128)S(1)} fusion(f32[4,9,128,128]{2,3,1,0:T(8,128)S(1)} %scatter-add.44, f32[4,5,128,128]{3,2,0,1:T(8,128)S(1)} %get-tuple-element.192, f32[4,5,128,128]{3,2,0,1:T(8,128)S(1)} %bitcast.185), kind=kOutput, calls=%fused_computation.29 | convolution fusion | flops 503644160 | bytes 4194304 | tf_op jit(solution)/shard_map/rab,rubc->ruac/dot_general | solution.py:25
  87.1 2.4 %fusion.6 = f32[4,9,128,128]{2,3,1,0:T(8,128)S(1)} fusion(f32[4,9,128,128]{2,3,1,0:T(8,128)S(1)} %fusion.8, f32[4,5,128,128]{3,2,0,1:T(8,128)S(1)} %bitcast.186), kind=kOutput, calls=%fused_computation.26 | convolution fusion | flops 503644160 | bytes 4194304 | tf_op jit(solution)/shard_map/rab,rubc->ruac/dot_general | solution.py:25
  89.5 2.4 %fusion.4 = f32[4,9,128,128]{2,3,1,0:T(8,128)S(1)} fusion(f32[4,9,128,128]{2,3,1,0:T(8,128)S(1)} %fusion.6, f32[4,5,128,128]{3,2,0,1:T(8,128)S(1)} %get-tuple-element.182, f32[4,5,128,128]{3,2,0,1:T(8,128)S(1)} %bitcast.187), kind=kOutput, calls=%fused_computation.23 | convolution fusion | flops 503644160 | bytes 4194304 | tf_op jit(solution)/shard_map/rab,rubc->ruac/dot_general | solution.py:25
  91.9 2.4 %fusion.2 = f32[4,9,128,128]{2,3,1,0:T(8,128)S(1)} fusion(f32[4,9,128,128]{2,3,1,0:T(8,128)S(1)} %fusion.4, f32[4,5,128,128]{3,2,0,1:T(8,128)S(1)} %get-tuple-element.181, f32[4,5,128,128]{3,2,0,1:T(8,128)S(1)} %bitcast.188), kind=kOutput, calls=%fused_computation.20 | convolution fusion | flops 503644160 | bytes 4194304 | tf_op jit(solution)/shard_map/rab,rubc->ruac/dot_general | solution.py:25
  94.4 0.2 broadcast_multiply_fusion
  94.6 1.7 %convolution_bitcast_fusion.13 = f32[4,1,128,128]{2,3,1,0:T(8,128)S(1)} fusion(f32[4,9,128,128]{2,3,1,0:T(8,128)S(1)} %broadcast_multiply_fusion, f32[4,5,128,128]{3,2,0,1:T(8,128)} %collective-permute-done), kind=kOutput, calls=%fused_computation.62 | convolution fusion | flops 100663296 | bytes 786432 | tf_op jit(solution)/shard_map/rab,rubc->ruac/dot_general | solution.py:41
  96.3 0.1 scatter-add.51
  96.5 1.1 pad_maximum_fusion.1
  97.5 1.0 fusion.25
  98.6 1.1 fusion.32
  99.7 1.5 fusion.23
  101.2 1.2 fusion.29
  102.4 0.0 copy-start.2
  102.5 1.9 %fusion.10 = f32[4,5,128,128]{2,3,1,0:T(8,128)S(1)} fusion(f32[4,5,128,128]{2,3,1,0:T(8,128)S(1)} %fusion.23, f32[4,4,128,128]{3,2,0,1:T(8,128)S(1)} %get-tuple-element.190, f32[4,9,128,128]{2,3,1,0:T(8,128)S(1)} %broadcast_multiply_fusion), kind=kOutput, calls=%fused_computation.34 | convolution fusion | flops 402915328 | bytes 3407872 | tf_op jit(solution)/shard_map/rab,rubc->ruac/dot_general | solution.py:41
  104.4 0.0 copy-done.2
  104.4 2.2 %fusion = f32[4,5,128,128]{2,3,1,0:T(8,128)S(1)} fusion(f32[4,5,128,128]{2,3,1,0:T(8,128)S(1)} %fusion.10, f32[4,9,128,128]{2,3,1,0:T(8,128)S(1)} %broadcast_multiply_fusion, f32[16,4,5,8,128]{4,3,2,1,0:T(8,128)S(1)} %bitcast.193), kind=kOutput, calls=%fused_computation.17 | convolution fusion | flops 503644160 | bytes 4194304 | tf_op jit(solution)/shard_map/rab,rubc->ruac/dot_general | solution.py:41
  106.6 1.8 %fusion.11 = f32[4,4,128,128]{2,3,1,0:T(8,128)S(1)} fusion(f32[4,5,128,128]{2,3,1,0:T(8,128)S(1)} %fusion, f32[4,4,128,128]{3,2,0,1:T(8,128)S(1)} %get-tuple-element.189, f32[4,9,128,128]{2,3,1,0:T(8,128)S(1)} %broadcast_multiply_fusion), kind=kOutput, calls=%fused_computation.35 | convolution fusion | flops 402915328 | bytes 3407872 | tf_op jit(solution)/shard_map/rab,rubc->ruac/dot_general | solution.py:41
  108.5 0.1 constant_dynamic-update-slice_fusion.2
  108.5 1.5 constant_dynamic-update-slice_fusion.1
  110.0 1.0 constant_dynamic-update-slice_fusion
  111.1 0.6 fusion.41
  111.7 0.3 fusion.17
  111.9 1.0 copy.177
  112.9 38.6 %all_to_all.37 = f32[4,5,128,128]{3,0,1,2:T(4,128)S(1)} all-to-all(f32[4,5,128,128]{3,0,1,2:T(4,128)S(1)} %copy.177), channel_id=1, replica_groups=mesh['row'=16,'col'=4,'depth'=4] {'col','depth'}, dimensions={2} | all-to-all | bytes 2621440 | tf_op jit(solution)/shard_map/all_to_all | solution.py:85
  151.5 0.1 copy.269
  151.7 1.2 copy.179
  (2 shorter events, 0.0 us)
Async XLA Ops:
  0.0 54.7 %copy-start = (s32[64,9]{0,1:T(8,128)S(1)}, s32[64,9]{0,1:T(8,128)}, u32[]{:S(2)}) copy-start(s32[64,9]{0,1:T(8,128)} %param.36) | copy-start | bytes 6916
  43.8 1.1 copy-start.1
  43.8 11.0 %copy-start.3 = (s32[64,5]{0,1:T(8,128)S(1)}, s32[64,5]{0,1:T(8,128)}, u32[]{:S(2)}) copy-start(s32[64,5]{0,1:T(8,128)} %param.37) | copy-start | bytes 3844
  44.9 35.4 %collective-permute-start = (f32[4,5,128,128]{3,2,0,1:T(8,128)S(1)}, f32[4,5,128,128]{3,2,0,1:T(8,128)}, u32[]{:S(2)}, u32[]{:S(2)}) collective-permute-start(f32[4,5,128,128]{3,2,0,1:T(8,128)S(1)} %bitcast.181), channel_id=1, source_target_pairs={{0,1},{1,2},{2,3},{3,4},{4,5},{5,6},{6,7},{7,8},{8,9},{9,10},{10,1... | collective-permute-start | bytes 3932168 | tf_op jit(solution)/shard_map/ppermute | solution.py:14
  47.0 33.3 %collective-permute-start.1 = (f32[4,5,128,128]{3,2,0,1:T(8,128)S(1)}, f32[4,5,128,128]{3,2,0,1:T(8,128)S(1)}, u32[]{:S(2)}, u32[]{:S(2)}) collective-permute-start(f32[4,5,128,128]{3,2,0,1:T(8,128)S(1)} %bitcast.182), channel_id=1, source_target_pairs={{1,0},{2,1},{3,2},{4,3},{5,4},{6,5},{7,6},{8,7},{9,8},{10,9},{11,1... | collective-permute-start | bytes 3932168 | tf_op jit(solution)/shard_map/ppermute | solution.py:15
  102.4 1.9 %copy-start.2 = (f32[64,5,8,128]{3,2,1,0:T(8,128)S(1)}, f32[64,5,8,128]{3,2,1,0:T(8,128)}, u32[]{:S(2)}) copy-start(f32[64,5,8,128]{3,2,1,0:T(8,128)} %copy-done.1) | copy-start | bytes 3932164
where the time goes:
time: 156 us; the launch traced here: 153 us
  blocking collectives  79.9 us (51%)
  waiting for transfers between devices  25.3 us (16%)
  matrix products  25.2 us (16%)
  starting transfers between devices  9.77 us (6%)
  other arithmetic  8.26 us (5%)
  local copies, waits for them, and re-layouts  4.15 us (3%)
    all_to_all x1, blocking collectives, gather_rows(): lax.all_to_all(stack, ('col', 'depth'), split_axis=0, concat_axis=2, tile...  41.3 us
    all_to_all x1, blocking collectives, on_device(): lax.all_to_all(purified, ('col', 'depth'), split_axis=2, concat_axis=0, t...  38.6 us
    ppermute x1, waiting for transfers between devices, padded(): before = lax.ppermute(last, axis, up)  25.2 us
    dot_general x9, matrix products, cube_left(): jnp.einsum('rab,rubc->ruac', square[:, column], widened[column:column + s...  13.3 us
    dot_general x5, matrix products, square_band(): jnp.einsum('rab,rubc->ruac', left_band[:, offset], widened[lower:lower +...  11.9 us
    ppermute x1, starting transfers between devices, padded(): after = lax.ppermute(initial, axis, down)  7.62 us
    concatenate x4, other arithmetic, padded(): value = jnp.concatenate([before, value, after], axis=dim)  5.26 us
  transfers between devices with their start and end apart: 2, of which 2 were waited for; matrix products, arithmetic and copies ran while one was open for 0% of the time, Pallas kernels for 0%

commit v1 on v0

v1 whole, which is shorter than its diff:
```python
import jax
import jax.numpy as jnp
from jax import lax
from jax.experimental import pallas as pl
from jax.experimental.pallas import tpu as pltpu
from jax.sharding import PartitionSpec as P

BLK = 128
OWN = 4
HALO = 4
PAIR = 2 * BLK
LAYERS = ("col", "depth")
EVERY = ("row", "col", "depth")

TO_BEFORE = [(0, s) for s in range(5)] + [(1, s) for s in range(5)] + [(2, 0), (2, 1), (3, 0)]
TO_AFTER = [(0, 4), (1, 3), (1, 4)] + [(2, s) for s in range(5)] + [(3, s) for s in range(5)]


def put_block(row, slot, value, high, low):
    top = row * BLK
    left = (row + slot - 2) * BLK
    rounded = value.astype(jnp.bfloat16)
    high[top : top + BLK, left : left + BLK] = rounded
    low[top : top + BLK, left : left + BLK] = (value - rounded.astype(jnp.float32)).astype(jnp.bfloat16)


def product(left_high, left_low, right_high, right_low):
    def dot(a, b):
        return jnp.dot(a, b, preferred_element_type=jnp.float32)

    return dot(left_high, right_high) + (dot(left_high, right_low) + dot(left_low, right_high))


def compute_kernel(own, after, before, square_mask, out_mask, out, high, low, square_high, square_low):
    first = lax.axis_index(LAYERS) * OWN
    zero = jnp.zeros((BLK, BLK), jnp.bfloat16)
    for pair in range(1, 5):
        for row, column in ((2 * pair + 1, 2 * pair - 2), (2 * pair, 2 * pair + 3)):
            high[row * BLK : (row + 1) * BLK, column * BLK : (column + 1) * BLK] = zero
            low[row * BLK : (row + 1) * BLK, column * BLK : (column + 1) * BLK] = zero
    for row, column in ((0, 3), (11, 8)):
        high[row * BLK : (row + 1) * BLK, column * BLK : (column + 1) * BLK] = zero
        low[row * BLK : (row + 1) * BLK, column * BLK : (column + 1) * BLK] = zero
    for place, (row, slot) in enumerate(TO_AFTER):
        put_block(row, slot, before[:, place].reshape(BLK, BLK), high, low)
    for row in range(OWN):
        for slot in range(5):
            put_block(HALO + row, slot, own[:, row * 5 + slot].reshape(BLK, BLK), high, low)
    for place, (row, slot) in enumerate(TO_BEFORE):
        put_block(HALO + OWN + row, slot, after[:, place].reshape(BLK, BLK), high, low)

    def tile(low_index, high_index):
        return slice(low_index * PAIR, high_index * PAIR)

    for pair in (2, 3):
        mine = tile(pair, pair + 1)
        kept = {}
        for column in range(pair - 2, pair + 3):
            inner = tile(max(pair, column) - 1, min(pair, column) + 2)
            outer = tile(column, column + 1)
            square = product(high[mine, inner], low[mine, inner], high[inner, outer], low[inner, outer])
            for half in range(2):
                for side in range(2):
                    slot = 2 * (column - pair) + side - half + 4
                    block = square[half * BLK : (half + 1) * BLK, side * BLK : (side + 1) * BLK]
                    row = 2 * (pair - 2) + half
                    if 0 <= slot < 9:
                        block = block * square_mask[first + row, slot].astype(jnp.float32)
                    if 2 <= slot < 7:
                        kept[row, slot - 2] = block
                    rounded = block.astype(jnp.bfloat16)
                    rows = slice(half * BLK, (half + 1) * BLK)
                    columns = slice(column * PAIR + side * BLK, column * PAIR + (side + 1) * BLK)
                    square_high[rows, columns] = rounded
                    square_low[rows, columns] = (block - rounded.astype(jnp.float32)).astype(jnp.bfloat16)
        for column in range(pair - 1, pair + 2):
            inner = tile(column - 1, column + 2)
            outer = tile(column, column + 1)
            cube = product(square_high[:, inner], square_low[:, inner], high[inner, outer], low[inner, outer])
            for half in range(2):
                for side in range(2):
                    slot = 2 * (column - pair) + side - half + 2
                    row = 2 * (pair - 2) + half
                    if 0 <= slot < 5:
                        block = cube[half * BLK : (half + 1) * BLK, side * BLK : (side + 1) * BLK]
                        gate = out_mask[first + row, slot].astype(jnp.float32)
                        block = gate * (3.0 * kept[row, slot] - 2.0 * block)
                        out[:, row * 5 + slot] = block.reshape(16, 8, BLK)


def compute(own, after, before, square_mask, out_mask):
    vmem = pl.BlockSpec(memory_space=pltpu.VMEM)
    smem = pl.BlockSpec(memory_space=pltpu.SMEM)
    window = (OWN + 2 * HALO) * BLK
    return pl.pallas_call(
        compute_kernel,
        out_shape=jax.ShapeDtypeStruct((16, 5 * OWN, 8, BLK), jnp.float32),
        in_specs=[vmem, vmem, vmem, smem, smem],
        out_specs=vmem,
        scratch_shapes=[
            pltpu.VMEM((window, window), jnp.bfloat16),
            pltpu.VMEM((window, window), jnp.bfloat16),
            pltpu.VMEM((PAIR, window), jnp.bfloat16),
            pltpu.VMEM((PAIR, window), jnp.bfloat16),
        ],
        compiler_params=pltpu.CompilerParams(vmem_limit_bytes=48 * 1024 * 1024),
        cost_estimate=pl.CostEstimate(flops=2 * 3 * 36 * 256**3, bytes_accessed=6 * 1024 * 1024, transcendentals=0),
    )(own, after, before, square_mask, out_mask)


def active_band(density, mask_band, first_row, total_rows):
    columns = (
        first_row
        + jnp.arange(density.shape[0], dtype=jnp.int32)[:, None]
        + jnp.arange(5, dtype=jnp.int32)[None, :]
        - 2
    )
    inside = ((columns >= 0) & (columns < total_rows)).astype(jnp.float32)
    return density * (mask_band.astype(jnp.float32) * inside)[:, :, None, None]


def on_device(density, mask_band, mask_square, mask_out):
    local_rows = density.shape[0]
    first_row = lax.axis_index("row") * local_rows
    active = active_band(density, mask_band, first_row, local_rows * lax.axis_size("row"))
    own = lax.all_to_all(active.reshape(16, 5 * OWN, 8, BLK), LAYERS, split_axis=0, concat_axis=0, tiled=True)
    up = [(i, i + 1) for i in range(255)]
    down = [(i + 1, i) for i in range(255)]
    to_before = jnp.concatenate([own[:, 0:12], own[:, 15:16]], axis=1)
    to_after = jnp.concatenate([own[:, 4:5], own[:, 8:20]], axis=1)
    before = lax.ppermute(to_after, EVERY, up)
    after = lax.ppermute(to_before, EVERY, down)
    purified = compute(own, after, before, mask_square, mask_out)
    result = lax.all_to_all(purified, LAYERS, split_axis=0, concat_axis=0, tiled=True)
    return result.reshape(density.shape)


def solution(mesh):
    return jax.shard_map(
        on_device,
        mesh=mesh,
        in_specs=(
            P("row", None, ("col", "depth"), None),
            P("row", None),
            P("row", None),
            P("row", None),
        ),
        out_specs=P("row", None, ("col", "depth"), None),
        check_vma=False,
    )
```

time: 156 us -> 120 us (0.77); the launches traced: 153 us -> 120 us
  matrix products: 25.2 us -> 0 us
  Pallas kernels: 0 us -> 5.96 us
  other arithmetic: 8.26 us -> 4.33 us
  starting transfers between devices: 9.77 us -> 6.15 us
  blocking collectives: 79.9 us -> 77 us
  local copies, waits for them, and re-layouts: 4.15 us -> 1.47 us
    dot_general x14 -> x0, matrix products: 25.2 us -> none  [the longest x9 13.3 us: cube_left(): jnp.einsum('rab,rubc->ruac', square[:, column], widened[column:column + s...]
    pallas_call x0 -> x1, Pallas kernels: none -> 5.96 us  [compute(): pl.pallas_call(compute_kernel, out_shape=jax.ShapeDtypeStruct((16, 5 * OW...]
    ppermute x2, starting transfers between devices: 9.77 us -> 6.15 us  [the longest x1 4.24 us: on_device(): after = lax.ppermute(to_before, EVERY, down)]
    concatenate x4 -> x2, other arithmetic: 5.26 us -> 1.92 us  [the longest x1 0.96 us: on_device(): to_before = jnp.concatenate([own[:, 0:12], own[:, 15:16]], axis=1)]
    all_to_all x2, blocking collectives: 79.9 us -> 77 us  [the longest x1 41.3 us: on_device(): lax.all_to_all(active.reshape(16, 5 * OWN, 8, BLK), LAYERS, split_axis=0,...]
  transfers between devices with their start and end apart: 2 -> 2, of which waited for: 2 -> 2; matrix products, arithmetic and copies ran while one was open for 0% -> 1% of each run, Pallas kernels for 0% -> 0%
where the time goes in v1:
time: 120 us
  blocking collectives  77 us (64%)
  waiting for transfers between devices  25.2 us (21%)
  starting transfers between devices  6.15 us (5%)
  Pallas kernels  5.96 us (5%)
  other arithmetic  4.33 us (4%)
  local copies, waits for them, and re-layouts  1.47 us (1%)
    all_to_all x1, blocking collectives, on_device(): lax.all_to_all(active.reshape(16, 5 * OWN, 8, BLK), LAYERS, split_axis=0,...  41.3 us
    all_to_all x1, blocking collectives, on_device(): lax.all_to_all(purified, LAYERS, split_axis=0, concat_axis=0, tiled=True)  35.7 us
    ppermute x1, waiting for transfers between devices, on_device(): after = lax.ppermute(to_before, EVERY, down)  13.8 us
    ppermute x1, waiting for transfers between devices, on_device(): before = lax.ppermute(to_after, EVERY, up)  11.4 us
    pallas_call x1, Pallas kernels, compute(): pl.pallas_call(compute_kernel, out_shape=jax.ShapeDtypeStruct((16, 5 * OW...  5.96 us
    ppermute x1, starting transfers between devices, on_device(): after = lax.ppermute(to_before, EVERY, down)  4.24 us
    mul x2, other arithmetic, active_band(): return density * (mask_band.astype(jnp.float32) * inside)[:, :, None, None]  2.41 us
  transfers between devices with their start and end apart: 2, of which 2 were waited for; matrix products, arithmetic and copies ran while one was open for 1% of the time, Pallas kernels for 0%

profile of v1, /device:TPU:2, one launch (start us, length us, event | category | flops | bytes accessed | tf_op | source)
XLA Modules:
  0.0 120.2 jit_solution(5358755095457681983)
XLA Ops:
  0.0 0.7 convert_select_fusion
  0.7 0.1 copy.5
  0.8 1.7 %broadcast_multiply_fusion = f32[64,5,8,128]{3,2,1,0:T(8,128)S(1)} fusion(f32[64,5,8,128]{3,2,1,0:T(8,128)} %param.4, f32[64,5]{1,0:T(8,128)S(1)} %copy.5), kind=kLoop, calls=%fused_computation.2 | loop fusion | flops 327680 | bytes 2622720 | tf_op jit(solution)/shard_map/mul | solution.py:119
  2.5 41.3 %all_to_all.10.own = f32[16,20,8,128]{3,2,1,0:T(8,128)S(1)} all-to-all(f32[16,20,8,128]{3,2,1,0:T(8,128)S(1)} %bitcast.2), channel_id=1, replica_groups=mesh['row'=16,'col'=4,'depth'=4] {'col','depth'}, dimensions={0} | all-to-all | bytes 2621440 | tf_op jit(solution)/shard_map/all_to_all | solution.py:126
  43.8 0.1 fusion.4
  43.9 0.0 copy-start
  43.9 0.0 copy-start.1
  43.9 1.0 pad_maximum_fusion
  44.9 4.2 %collective-permute-start = (f32[16,13,8,128]{3,2,1,0:T(8,128)}, f32[16,13,8,128]{3,2,1,0:T(8,128)S(1)}, u32[]{:S(2)}, u32[]{:S(2)}) collective-permute-start(f32[16,13,8,128]{3,2,1,0:T(8,128)} %pad_maximum_fusion), channel_id=1, source_target_pairs={{1,0},{2,1},{3,2},{4,3},{5,4},{6,5},{7,6},{8,7},{9,8},{10,9},{11,1... | collective-permute-start | bytes 2555912 | tf_op jit(solution)/shard_map/ppermute | solution.py:132
  49.1 1.0 pad_maximum_fusion.1
  50.1 1.9 %collective-permute-start.1 = (f32[16,13,8,128]{3,2,1,0:T(8,128)}, f32[16,13,8,128]{3,2,1,0:T(8,128)S(1)}, u32[]{:S(2)}, u32[]{:S(2)}) collective-permute-start(f32[16,13,8,128]{3,2,1,0:T(8,128)} %pad_maximum_fusion.1), channel_id=1, source_target_pairs={{0,1},{1,2},{2,3},{3,4},{4,5},{5,6},{6,7},{7,8},{8,9},{9,10},{10,1... | collective-permute-start | bytes 2555912 | tf_op jit(solution)/shard_map/ppermute | solution.py:131
  52.0 0.0 copy-done
  52.0 0.1 copy.6.square_mask
  52.1 0.0 copy-done.1
  52.1 0.1 copy.7.out_mask
  52.2 13.8 %collective-permute-done.after = f32[16,13,8,128]{3,2,1,0:T(8,128)S(1)} collective-permute-done((f32[16,13,8,128]{3,2,1,0:T(8,128)}, f32[16,13,8,128]{3,2,1,0:T(8,128)S(1)}, u32[]{:S(2)}, u32[]{:S(2)}) %collective-permute-start) | collective-permute-done | bytes 852000 | tf_op jit(solution)/shard_map/ppermute | solution.py:132
  66.1 11.4 %collective-permute-done.1.before = f32[16,13,8,128]{3,2,1,0:T(8,128)S(1)} collective-permute-done((f32[16,13,8,128]{3,2,1,0:T(8,128)}, f32[16,13,8,128]{3,2,1,0:T(8,128)S(1)}, u32[]{:S(2)}, u32[]{:S(2)}) %collective-permute-start.1) | collective-permute-done | bytes 852000 | tf_op jit(solution)/shard_map/ppermute | solution.py:131
  77.5 6.0 %shard_map.46 = f32[16,20,8,128]{3,2,1,0:T(8,128)S(1)} custom-call(f32[16,20,8,128]{3,2,1,0:T(8,128)S(1)} %all_to_all.10.own, f32[16,13,8,128]{3,2,1,0:T(8,128)S(1)} %collective-permute-done.after, f32[16,13,8,128]{3,2,1,0:T(8,128)S(1)} %collective-permute-done.1.before, s32[64,9]{1,0:T(8,128)S(1)} %copy.6.square_mask, s32[64,5]{1,0:T(8,128)S(1)} %copy.7.out_mask), custom_call_target="tpu_custom_call" | custom-call | flops 3623878656 | bytes 6291456 | tf_op jit(solution)/shard_map/pallas_call | solution.py:95
  83.4 35.7 %all_to_all.11 = f32[16,20,8,128]{3,2,1,0:T(8,128)S(1)} all-to-all(f32[16,20,8,128]{3,2,1,0:T(8,128)S(1)} %shard_map.46), channel_id=1, replica_groups=mesh['row'=16,'col'=4,'depth'=4] {'col','depth'}, dimensions={0} | all-to-all | bytes 2621440 | tf_op jit(solution)/shard_map/all_to_all | solution.py:134
  119.1 1.1 copy.9
  (2 shorter events, 0.0 us)
Async XLA Ops:
  43.9 8.1 %copy-start = (s32[64,9]{0,1:T(8,128)S(1)}, s32[64,9]{0,1:T(8,128)}, u32[]{:S(2)}) copy-start(s32[64,9]{0,1:T(8,128)} %param.6) | copy-start | bytes 6916
  43.9 8.2 %copy-start.1 = (s32[64,5]{0,1:T(8,128)S(1)}, s32[64,5]{0,1:T(8,128)}, u32[]{:S(2)}) copy-start(s32[64,5]{0,1:T(8,128)} %param.7) | copy-start | bytes 3844
  44.9 21.2 %collective-permute-start = (f32[16,13,8,128]{3,2,1,0:T(8,128)}, f32[16,13,8,128]{3,2,1,0:T(8,128)S(1)}, u32[]{:S(2)}, u32[]{:S(2)}) collective-permute-start(f32[16,13,8,128]{3,2,1,0:T(8,128)} %pad_maximum_fusion), channel_id=1, source_target_pairs={{1,0},{2,1},{3,2},{4,3},{5,4},{6,5},{7,6},{8,7},{9,8},{10,9},{11,1... | collective-permute-start | bytes 2555912 | tf_op jit(solution)/shard_map/ppermute | solution.py:132
  50.1 27.4 %collective-permute-start.1 = (f32[16,13,8,128]{3,2,1,0:T(8,128)}, f32[16,13,8,128]{3,2,1,0:T(8,128)S(1)}, u32[]{:S(2)}, u32[]{:S(2)}) collective-permute-start(f32[16,13,8,128]{3,2,1,0:T(8,128)} %pad_maximum_fusion.1), channel_id=1, source_target_pairs={{0,1},{1,2},{2,3},{3,4},{4,5},{5,6},{6,7},{7,8},{8,9},{9,10},{10,1... | collective-permute-start | bytes 2555912 | tf_op jit(solution)/shard_map/ppermute | solution.py:131

commit v2 on v1

--- a/solution.py
+++ b/solution.py
@@ -12,8 +12,10 @@
 LAYERS = ("col", "depth")
 EVERY = ("row", "col", "depth")
 
-TO_BEFORE = [(0, s) for s in range(5)] + [(1, s) for s in range(5)] + [(2, 0), (2, 1), (3, 0)]
-TO_AFTER = [(0, 4), (1, 3), (1, 4)] + [(2, s) for s in range(5)] + [(3, s) for s in range(5)]
+OUTER = [(row, slot) for row in (0, 3) for slot in range(5)]
+INNER = [(row, slot) for row in (1, 2) for slot in range(5)]
+OUTER_TO_BEFORE, OUTER_TO_AFTER = slice(0, 6), slice(4, 10)
+INNER_TO_BEFORE, INNER_TO_AFTER = slice(0, 7), slice(3, 10)
 
 
 def put_block(row, slot, value, high, low):
@@ -31,7 +33,9 @@
     return dot(left_high, right_high) + (dot(left_high, right_low) + dot(left_low, right_high))
 
 
-def compute_kernel(own, after, before, square_mask, out_mask, out, high, low, square_high, square_low):
+def compute_kernel(
+    outer, inner, outer_after, inner_after, outer_before, inner_before, weight, square_mask, out_mask, out, high, low, square_high, square_low
+):
     first = lax.axis_index(LAYERS) * OWN
     zero = jnp.zeros((BLK, BLK), jnp.bfloat16)
     for pair in range(1, 5):
@@ -41,13 +45,17 @@
     for row, column in ((0, 3), (11, 8)):
         high[row * BLK : (row + 1) * BLK, column * BLK : (column + 1) * BLK] = zero
         low[row * BLK : (row + 1) * BLK, column * BLK : (column + 1) * BLK] = zero
-    for place, (row, slot) in enumerate(TO_AFTER):
-        put_block(row, slot, before[:, place].reshape(BLK, BLK), high, low)
-    for row in range(OWN):
-        for slot in range(5):
-            put_block(HALO + row, slot, own[:, row * 5 + slot].reshape(BLK, BLK), high, low)
-    for place, (row, slot) in enumerate(TO_BEFORE):
-        put_block(HALO + OWN + row, slot, after[:, place].reshape(BLK, BLK), high, low)
+    for source, blocks, shift in (
+        (outer_before, OUTER[OUTER_TO_AFTER], 0),
+        (inner_before, INNER[INNER_TO_AFTER], 0),
+        (outer_after, OUTER[OUTER_TO_BEFORE], HALO + OWN),
+        (inner_after, INNER[INNER_TO_BEFORE], HALO + OWN),
+    ):
+        for place, (row, slot) in enumerate(blocks):
+            put_block(shift + row, slot, source[:, place].reshape(BLK, BLK), high, low)
+    for source, blocks in ((outer, OUTER), (inner, INNER)):
+        for place, (row, slot) in enumerate(blocks):
+            put_block(HALO + row, slot, source[:, place].reshape(BLK, BLK) * weight[row, slot], high, low)
 
     def tile(low_index, high_index):
         return slice(low_index * PAIR, high_index * PAIR)
@@ -88,14 +96,14 @@
                         out[:, row * 5 + slot] = block.reshape(16, 8, BLK)
 
 
-def compute(own, after, before, square_mask, out_mask):
+def compute(*operands):
     vmem = pl.BlockSpec(memory_space=pltpu.VMEM)
     smem = pl.BlockSpec(memory_space=pltpu.SMEM)
     window = (OWN + 2 * HALO) * BLK
     return pl.pallas_call(
         compute_kernel,
         out_shape=jax.ShapeDtypeStruct((16, 5 * OWN, 8, BLK), jnp.float32),
-        in_specs=[vmem, vmem, vmem, smem, smem],
+        in_specs=[vmem] * 6 + [smem] * 3,
         out_specs=vmem,
         scratch_shapes=[
             pltpu.VMEM((window, window), jnp.bfloat16),
@@ -103,35 +111,64 @@
             pltpu.VMEM((PAIR, window), jnp.bfloat16),
             pltpu.VMEM((PAIR, window), jnp.bfloat16),
         ],
-        compiler_params=pltpu.CompilerParams(vmem_limit_bytes=48 * 1024 * 1024),
+        compiler_params=pltpu.CompilerParams(vmem_limit_bytes=40 * 1024 * 1024),
         cost_estimate=pl.CostEstimate(flops=2 * 3 * 36 * 256**3, bytes_accessed=6 * 1024 * 1024, transcendentals=0),
-    )(own, after, before, square_mask, out_mask)
+    )(*operands)
 
 
-def active_band(density, mask_band, first_row, total_rows):
-    columns = (
-        first_row
-        + jnp.arange(density.shape[0], dtype=jnp.int32)[:, None]
-        + jnp.arange(5, dtype=jnp.int32)[None, :]
-        - 2
-    )
-    inside = ((columns >= 0) & (columns < total_rows)).astype(jnp.float32)
-    return density * (mask_band.astype(jnp.float32) * inside)[:, :, None, None]
+def swap(value, axis, dim):
+    me = lax.axis_index(axis)
+    size = lax.axis_size(axis)
+    pieces = [lax.dynamic_slice_in_dim(value, me, 1, dim)]
+    for k in range(1, size):
+        piece = lax.dynamic_slice_in_dim(value, me ^ k, 1, dim)
+        pieces.append(lax.ppermute(piece, axis, [(i, i ^ k) for i in range(size)]))
+    stack = jnp.concatenate(pieces, axis=dim)
+    return jnp.concatenate([lax.dynamic_slice_in_dim(stack, me ^ j, 1, dim) for j in range(size)], axis=dim)
+
+
+def exchange(col_first, depth_first):
+    one = swap(col_first, "col", 0)
+    other = swap(depth_first, "depth", 1)
+    other = swap(other, "col", 0)
+    one = swap(one, "depth", 1)
+    return one, other
+
+
+def shift(value):
+    return [(i, i + 1) for i in range(value)], [(i + 1, i) for i in range(value)]
 
 
 def on_device(density, mask_band, mask_square, mask_out):
     local_rows = density.shape[0]
-    first_row = lax.axis_index("row") * local_rows
-    active = active_band(density, mask_band, first_row, local_rows * lax.axis_size("row"))
-    own = lax.all_to_all(active.reshape(16, 5 * OWN, 8, BLK), LAYERS, split_axis=0, concat_axis=0, tiled=True)
-    up = [(i, i + 1) for i in range(255)]
-    down = [(i + 1, i) for i in range(255)]
-    to_before = jnp.concatenate([own[:, 0:12], own[:, 15:16]], axis=1)
-    to_after = jnp.concatenate([own[:, 4:5], own[:, 8:20]], axis=1)
-    before = lax.ppermute(to_after, EVERY, up)
-    after = lax.ppermute(to_before, EVERY, down)
-    purified = compute(own, after, before, mask_square, mask_out)
-    result = lax.all_to_all(purified, LAYERS, split_axis=0, concat_axis=0, tiled=True)
+    total_rows = local_rows * lax.axis_size("row")
+    begin = lax.axis_index(LAYERS) * OWN
+    rows = lax.axis_index("row") * local_rows + begin + jnp.arange(OWN, dtype=jnp.int32)
+    columns = rows[:, None] + jnp.arange(5, dtype=jnp.int32)[None, :] - 2
+    inside = ((columns >= 0) & (columns < total_rows)).astype(jnp.float32)
+    weight = lax.dynamic_slice_in_dim(mask_band, begin, OWN, 0).astype(jnp.float32) * inside
+    groups = density.reshape(4, 4, OWN, 5, 8, BLK)
+    inner, outer = exchange(
+        groups[:, :, 1:3].reshape(4, 4, 10, 8, BLK), groups[:, :, 0::3].reshape(4, 4, 10, 8, BLK)
+    )
+    inner = inner.reshape(16, 10, 8, BLK)
+    outer = outer.reshape(16, 10, 8, BLK)
+    up, down = shift(255)
+
+    def halo(group, group_weight, part, pairs):
+        gate = group_weight.reshape(10)[part][None, :, None, None]
+        return lax.ppermute(group[:, part] * gate, EVERY, pairs)
+
+    inner_after = halo(inner, weight[1:3], INNER_TO_BEFORE, down)
+    inner_before = halo(inner, weight[1:3], INNER_TO_AFTER, up)
+    outer_after = halo(outer, weight[0::3], OUTER_TO_BEFORE, down)
+    outer_before = halo(outer, weight[0::3], OUTER_TO_AFTER, up)
+    purified = compute(
+        outer, inner, outer_after, inner_after, outer_before, inner_before, weight, mask_square, mask_out
+    )
+    purified = purified.reshape(4, 4, 2, 10, 8, BLK)
+    lower, upper = exchange(purified[:, :, 0], purified[:, :, 1])
+    result = jnp.stack([lower, upper], axis=2)
     return result.reshape(density.shape)
 
 

time: 120 us -> 113 us (0.942); the launches traced: 120 us -> 112 us
  blocking collectives: 77 us -> 0 us
  starting transfers between devices: 6.15 us -> 51.1 us
  waiting for transfers between devices: 25.2 us -> 47.4 us
  local copies, waits for them, and re-layouts: 1.47 us -> 3.09 us
    all_to_all x2 -> x0, blocking collectives: 77 us -> none  [the longest x1 41.3 us: on_device(): lax.all_to_all(active.reshape(16, 5 * OWN, 8, BLK), LAYERS, split_axis=0,...]
    ppermute x2 -> x28, starting transfers between devices: 6.15 us -> 51.1 us  [the longest x24 31.4 us: swap(): pieces.append(lax.ppermute(piece, axis, [(i, i ^ k) for i in range(size)]))]
    ppermute x2 -> x28, waiting for transfers between devices: 25.2 us -> 47.4 us  [the longest x24 41 us: swap(): pieces.append(lax.ppermute(piece, axis, [(i, i ^ k) for i in range(size)]))]
    slice x2 -> x6, local copies, waits for them, and re-layouts: 0.11 us -> 1.68 us  [the longest x1 1.39 us: on_device(): groups[:, :, 1:3].reshape(4, 4, 10, 8, BLK)]
    concatenate x2 -> x14, other arithmetic: 1.92 us -> 0.63 us  [the longest x8 0.35 us: swap(): stack = jnp.concatenate(pieces, axis=dim)]
    another operation x0 -> x2, other arithmetic: none -> 1.27 us  [on_device(): result = jnp.stack([lower, upper], axis=2)]
    mul x2 -> x3, other arithmetic: 2.41 us -> 1.95 us  [the longest x2 1.88 us: halo(): return lax.ppermute(group[:, part] * gate, EVERY, pairs)]
  transfers between devices with their start and end apart: 2 -> 28, of which waited for: 2 -> 14; matrix products, arithmetic and copies ran while one was open for 1% -> 3% of each run, Pallas kernels for 0% -> 0%
where the time goes in v2:
time: 113 us; the launch traced here: 112 us
  starting transfers between devices  51.1 us (45%)
  waiting for transfers between devices  47.4 us (42%)
  Pallas kernels  6.02 us (5%)
  other arithmetic  3.85 us (3%)
  local copies, waits for them, and re-layouts  3.09 us (3%)
    ppermute x24, waiting for transfers between devices, swap(): pieces.append(lax.ppermute(piece, axis, [(i, i ^ k) for i in range(size)]))  41 us
    ppermute x24, starting transfers between devices, swap(): pieces.append(lax.ppermute(piece, axis, [(i, i ^ k) for i in range(size)]))  31.4 us
    ppermute x4, starting transfers between devices, halo(): return lax.ppermute(group[:, part] * gate, EVERY, pairs)  19.7 us
    ppermute x4, waiting for transfers between devices, halo(): return lax.ppermute(group[:, part] * gate, EVERY, pairs)  6.43 us
    pallas_call x1, Pallas kernels, compute(): pl.pallas_call(compute_kernel, out_shape=jax.ShapeDtypeStruct((16, 5 * OW...  6.02 us
  transfers between devices with their start and end apart: 28, of which 14 were waited for; matrix products, arithmetic and copies ran while one was open for 3% of the time, Pallas kernels for 0%

profile of v2, /device:TPU:2, one launch (start us, length us, event | category | flops | bytes accessed | tf_op | source)
XLA Modules:
  0.0 111.8 jit_solution(15151792473261186081)
XLA Ops:
  0.0 1.4 %fusion.4 = (f32[4,4,2,5,8,128]{5,4,3,2,1,0:T(8,128)S(1)}, f32[4,4,2,5,8,128]{5,4,3,2,1,0:T(8,128)S(1)}) fusion(f32[4,4,4,5,8,128]{5,4,3,2,1,0:T(8,128)} %bitcast.34), kind=kLoop, calls=%fused_computation.93 | loop fusion | bytes 2621440 | tf_op jit(solution)/shard_map/slice | solution.py:152
  1.5 4.7 %collective-permute-start.8 = (f32[1,4,10,8,128]{4,3,2,1,0:T(8,128)S(1)}, f32[1,4,10,8,128]{4,3,2,1,0:T(8,128)S(1)}, u32[]{:S(2)}, u32[]{:S(2)}) collective-permute-start(f32[1,4,10,8,128]{4,3,2,1,0:T(8,128)S(1)} %get-tuple-element.58), channel_id=1, source_target_pairs={{0,12},{4,8},{8,4},{12,0},{1,13},{5,9},{9,5},{13,1},{2,14},{6,10},... | collective-permute-start | bytes 491528 | tf_op jit(solution)/shard_map/ppermute | solution.py:125
  6.2 0.7 collective-permute-start.6
  6.9 3.1 %collective-permute-start.2 = (f32[4,1,10,8,128]{4,3,2,1,0:T(8,128)S(1)}, f32[4,1,10,8,128]{4,3,2,1,0:T(8,128)S(1)}, u32[]{:S(2)}, u32[]{:S(2)}) collective-permute-start(f32[4,1,10,8,128]{4,3,2,1,0:T(8,128)S(1)} %get-tuple-element.74), channel_id=1, source_target_pairs={{0,3},{1,2},{2,1},{3,0},{4,7},{5,6},{6,5},{7,4},{8,11},{9,10},{10,... | collective-permute-start | bytes 491528 | tf_op jit(solution)/shard_map/ppermute | solution.py:125
  10.0 0.6 collective-permute-start.1
  10.7 0.1 copy.8
  10.8 0.1 convert_select_fusion.weight
  10.9 0.1 reshape.51
  11.1 0.1 reshape.50
  11.2 0.1 collective-permute-done.8
  11.3 1.6 %collective-permute-start = (f32[4,1,10,8,128]{4,3,2,1,0:T(8,128)S(1)}, f32[4,1,10,8,128]{4,3,2,1,0:T(8,128)S(1)}, u32[]{:S(2)}, u32[]{:S(2)}) collective-permute-start(f32[4,1,10,8,128]{4,3,2,1,0:T(8,128)S(1)} %get-tuple-element.76), channel_id=1, source_target_pairs={{0,1},{1,0},{2,3},{3,2},{4,5},{5,4},{6,7},{7,6},{8,9},{9,8},{10,11... | collective-permute-start | bytes 491528 | tf_op jit(solution)/shard_map/ppermute | solution.py:125
  12.9 6.7 %collective-permute-done.7 = f32[1,4,10,8,128]{4,3,2,1,0:T(8,128)S(1)} collective-permute-done((f32[1,4,10,8,128]{4,3,2,1,0:T(8,128)S(1)}, f32[1,4,10,8,128]{4,3,2,1,0:T(8,128)S(1)}, u32[]{:S(2)}, u32[]{:S(2)}) %collective-permute-start.7) | collective-permute-done | bytes 163872 | tf_op jit(solution)/shard_map/ppermute | solution.py:125
  19.8 3.1 %collective-permute-start.11 = (f32[4,1,10,8,128]{4,3,2,1,0:T(8,128)S(1)}, f32[4,1,10,8,128]{4,3,2,1,0:T(8,128)S(1)}, u32[]{:S(2)}, u32[]{:S(2)}) collective-permute-start(f32[4,1,10,8,128]{4,3,2,1,0:T(8,128)S(1)} %get-tuple-element.50), channel_id=1, source_target_pairs={{0,3},{1,2},{2,1},{3,0},{4,7},{5,6},{6,5},{7,4},{8,11},{9,10},{10,... | collective-permute-start | bytes 491528 | tf_op jit(solution)/shard_map/ppermute | solution.py:125
  22.9 0.6 collective-permute-start.10
  23.5 0.5 collective-permute-start.9
  24.2 2.8 %collective-permute-start.5 = (f32[1,4,10,8,128]{4,3,2,1,0:T(8,128)S(1)}, f32[1,4,10,8,128]{4,3,2,1,0:T(8,128)S(1)}, u32[]{:S(2)}, u32[]{:S(2)}) collective-permute-start(f32[1,4,10,8,128]{4,3,2,1,0:T(8,128)S(1)} %get-tuple-element.66), channel_id=1, source_target_pairs={{0,12},{4,8},{8,4},{12,0},{1,13},{5,9},{9,5},{13,1},{2,14},{6,10},... | collective-permute-start | bytes 491528 | tf_op jit(solution)/shard_map/ppermute | solution.py:125
  27.0 2.2 %collective-permute-done.11 = f32[4,1,10,8,128]{4,3,2,1,0:T(8,128)S(1)} collective-permute-done((f32[4,1,10,8,128]{4,3,2,1,0:T(8,128)S(1)}, f32[4,1,10,8,128]{4,3,2,1,0:T(8,128)S(1)}, u32[]{:S(2)}, u32[]{:S(2)}) %collective-permute-start.11) | collective-permute-done | bytes 163872 | tf_op jit(solution)/shard_map/ppermute | solution.py:125
  29.2 2.0 %collective-permute-done.10 = f32[4,1,10,8,128]{4,3,2,1,0:T(8,128)S(1)} collective-permute-done((f32[4,1,10,8,128]{4,3,2,1,0:T(8,128)S(1)}, f32[4,1,10,8,128]{4,3,2,1,0:T(8,128)S(1)}, u32[]{:S(2)}, u32[]{:S(2)}) %collective-permute-start.10) | collective-permute-done | bytes 163872 | tf_op jit(solution)/shard_map/ppermute | solution.py:125
  31.3 1.7 %collective-permute-done.5 = f32[1,4,10,8,128]{4,3,2,1,0:T(8,128)S(1)} collective-permute-done((f32[1,4,10,8,128]{4,3,2,1,0:T(8,128)S(1)}, f32[1,4,10,8,128]{4,3,2,1,0:T(8,128)S(1)}, u32[]{:S(2)}, u32[]{:S(2)}) %collective-permute-start.5) | collective-permute-done | bytes 163872 | tf_op jit(solution)/shard_map/ppermute | solution.py:125
  33.0 6.5 %collective-permute-done.4 = f32[1,4,10,8,128]{4,3,2,1,0:T(8,128)S(1)} collective-permute-done((f32[1,4,10,8,128]{4,3,2,1,0:T(8,128)S(1)}, f32[1,4,10,8,128]{4,3,2,1,0:T(8,128)S(1)}, u32[]{:S(2)}, u32[]{:S(2)}) %collective-permute-start.4) | collective-permute-done | bytes 163872 | tf_op jit(solution)/shard_map/ppermute | solution.py:125
  39.7 0.9 slice_multiply_fusion
  40.5 3.3 %collective-permute-start.15 = (f32[16,7,8,128]{3,2,1,0:T(8,128)}, f32[16,7,8,128]{3,2,1,0:T(8,128)S(1)}, u32[]{:S(2)}, u32[]{:S(2)}) collective-permute-start(f32[16,7,8,128]{3,2,1,0:T(8,128)} %get-tuple-element.41), channel_id=1, source_target_pairs={{0,1},{1,2},{2,3},{3,4},{4,5},{5,6},{6,7},{7,8},{8,9},{9,10},{10,1... | collective-permute-start | bytes 1376264 | tf_op jit(solution)/shard_map/ppermute | solution.py:160
  43.8 6.5 %collective-permute-start.13 = (f32[16,7,8,128]{3,2,1,0:T(8,128)S(1)}, f32[16,7,8,128]{3,2,1,0:T(8,128)S(1)}, u32[]{:S(2)}, u32[]{:S(2)}) collective-permute-start(f32[16,7,8,128]{3,2,1,0:T(8,128)S(1)} %get-tuple-element.42), channel_id=1, source_target_pairs={{1,0},{2,1},{3,2},{4,3},{5,4},{6,5},{7,6},{8,7},{9,8},{10,9},{11,1... | collective-permute-start | bytes 1376264 | tf_op jit(solution)/shard_map/ppermute | solution.py:160
  50.4 1.0 slice_multiply_fusion.2
  51.4 1.9 %collective-permute-start.14 = (f32[16,6,8,128]{3,2,1,0:T(8,128)}, f32[16,6,8,128]{3,2,1,0:T(8,128)S(1)}, u32[]{:S(2)}, u32[]{:S(2)}) collective-permute-start(f32[16,6,8,128]{3,2,1,0:T(8,128)} %get-tuple-element.43), channel_id=1, source_target_pairs={{0,1},{1,2},{2,3},{3,4},{4,5},{5,6},{6,7},{7,8},{8,9},{9,10},{10,1... | collective-permute-start | bytes 1179656 | tf_op jit(solution)/shard_map/ppermute | solution.py:160
  53.3 8.0 %collective-permute-start.12 = (f32[16,6,8,128]{3,2,1,0:T(8,128)}, f32[16,6,8,128]{3,2,1,0:T(8,128)S(1)}, u32[]{:S(2)}, u32[]{:S(2)}) collective-permute-start(f32[16,6,8,128]{3,2,1,0:T(8,128)} %get-tuple-element.44), channel_id=1, source_target_pairs={{1,0},{2,1},{3,2},{4,3},{5,4},{6,5},{7,6},{8,7},{9,8},{10,9},{11,1... | collective-permute-start | bytes 1179656 | tf_op jit(solution)/shard_map/ppermute | solution.py:160
  61.4 0.1 copy.6.square_mask
  61.5 0.1 copy.7.out_mask
  61.6 6.4 %collective-permute-done.14.outer_before = f32[16,6,8,128]{3,2,1,0:T(8,128)S(1)} collective-permute-done((f32[16,6,8,128]{3,2,1,0:T(8,128)}, f32[16,6,8,128]{3,2,1,0:T(8,128)S(1)}, u32[]{:S(2)}, u32[]{:S(2)}) %collective-permute-start.14) | collective-permute-done | bytes 393248 | tf_op jit(solution)/shard_map/ppermute | solution.py:160
  68.0 6.0 %shard_map.46 = f32[16,20,8,128]{3,2,1,0:T(8,128)S(1)} custom-call(f32[16,10,8,128]{3,2,1,0:T(8,128)S(1)} %bitcast.30, f32[16,10,8,128]{3,2,1,0:T(8,128)S(1)} %bitcast.28, f32[16,6,8,128]{3,2,1,0:T(8,128)S(1)} %collective-permute-done.12.outer_after, f32[16,7,8,128]{3,2,1,0:T(8,128)S(1)} %collective-permute-done.13.inner_after, ...), custom_call_target="tpu_custom_call" | custom-call | flops 3623878656 | bytes 6291456 | tf_op jit(solution)/shard_map/pallas_call | solution.py:103
  74.0 0.1 fusion.3
  74.2 0.1 collective-permute-start.18
  74.3 0.1 collective-permute-start.17
  74.4 4.3 %collective-permute-start.16 = (f32[1,4,10,8,128]{4,3,2,1,0:T(8,128)S(1)}, f32[1,4,10,8,128]{4,3,2,1,0:T(8,128)S(1)}, u32[]{:S(2)}, u32[]{:S(2)}) collective-permute-start(f32[1,4,10,8,128]{4,3,2,1,0:T(8,128)S(1)} %get-tuple-element.24), channel_id=1, source_target_pairs={{0,4},{4,0},{8,12},{12,8},{1,5},{5,1},{9,13},{13,9},{2,6},{6,2},{1... | collective-permute-start | bytes 491528 | tf_op jit(solution)/shard_map/ppermute | solution.py:125
  78.7 1.5 %collective-permute-start.24 = (f32[4,1,10,8,128]{4,3,2,1,0:T(8,128)S(1)}, f32[4,1,10,8,128]{4,3,2,1,0:T(8,128)S(1)}, u32[]{:S(2)}, u32[]{:S(2)}) collective-permute-start(f32[4,1,10,8,128]{4,3,2,1,0:T(8,128)S(1)} %get-tuple-element.38), channel_id=1, source_target_pairs={{0,3},{1,2},{2,1},{3,0},{4,7},{5,6},{6,5},{7,4},{8,11},{9,10},{10,... | collective-permute-start | bytes 491528 | tf_op jit(solution)/shard_map/ppermute | solution.py:125
  80.2 3.1 %collective-permute-done.18 = f32[1,4,10,8,128]{4,3,2,1,0:T(8,128)S(1)} collective-permute-done((f32[1,4,10,8,128]{4,3,2,1,0:T(8,128)S(1)}, f32[1,4,10,8,128]{4,3,2,1,0:T(8,128)S(1)}, u32[]{:S(2)}, u32[]{:S(2)}) %collective-permute-start.18) | collective-permute-done | bytes 163872 | tf_op jit(solution)/shard_map/ppermute | solution.py:125
  83.3 3.9 %collective-permute-done.17 = f32[1,4,10,8,128]{4,3,2,1,0:T(8,128)S(1)} collective-permute-done((f32[1,4,10,8,128]{4,3,2,1,0:T(8,128)S(1)}, f32[1,4,10,8,128]{4,3,2,1,0:T(8,128)S(1)}, u32[]{:S(2)}, u32[]{:S(2)}) %collective-permute-start.17) | collective-permute-done | bytes 163872 | tf_op jit(solution)/shard_map/ppermute | solution.py:125
  87.4 4.3 %collective-permute-start.21 = (f32[4,1,10,8,128]{4,3,2,1,0:T(8,128)S(1)}, f32[4,1,10,8,128]{4,3,2,1,0:T(8,128)S(1)}, u32[]{:S(2)}, u32[]{:S(2)}) collective-permute-start(f32[4,1,10,8,128]{4,3,2,1,0:T(8,128)S(1)} %get-tuple-element.14), channel_id=1, source_target_pairs={{0,3},{1,2},{2,1},{3,0},{4,7},{5,6},{6,5},{7,4},{8,11},{9,10},{10,... | collective-permute-start | bytes 491528 | tf_op jit(solution)/shard_map/ppermute | solution.py:125
  91.8 1.0 collective-permute-start.19
  93.0 2.2 %collective-permute-start.27 = (f32[1,4,10,8,128]{4,3,2,1,0:T(8,128)S(1)}, f32[1,4,10,8,128]{4,3,2,1,0:T(8,128)S(1)}, u32[]{:S(2)}, u32[]{:S(2)}) collective-permute-start(f32[1,4,10,8,128]{4,3,2,1,0:T(8,128)S(1)} %get-tuple-element.30), channel_id=1, source_target_pairs={{0,12},{4,8},{8,4},{12,0},{1,13},{5,9},{9,5},{13,1},{2,14},{6,10},... | collective-permute-start | bytes 491528 | tf_op jit(solution)/shard_map/ppermute | solution.py:125
  95.1 4.5 %collective-permute-done.21 = f32[4,1,10,8,128]{4,3,2,1,0:T(8,128)S(1)} collective-permute-done((f32[4,1,10,8,128]{4,3,2,1,0:T(8,128)S(1)}, f32[4,1,10,8,128]{4,3,2,1,0:T(8,128)S(1)}, u32[]{:S(2)}, u32[]{:S(2)}) %collective-permute-start.21) | collective-permute-done | bytes 163872 | tf_op jit(solution)/shard_map/ppermute | solution.py:125
  99.6 0.3 collective-permute-start.25
  99.9 0.4 collective-permute-done.20
  100.4 0.3 collective-permute-done.19
  100.8 1.2 %collective-permute-done.27 = f32[1,4,10,8,128]{4,3,2,1,0:T(8,128)S(1)} collective-permute-done((f32[1,4,10,8,128]{4,3,2,1,0:T(8,128)S(1)}, f32[1,4,10,8,128]{4,3,2,1,0:T(8,128)S(1)}, u32[]{:S(2)}, u32[]{:S(2)}) %collective-permute-start.27) | collective-permute-done | bytes 163872 | tf_op jit(solution)/shard_map/ppermute | solution.py:125
  102.0 8.4 %collective-permute-done.26 = f32[1,4,10,8,128]{4,3,2,1,0:T(8,128)S(1)} collective-permute-done((f32[1,4,10,8,128]{4,3,2,1,0:T(8,128)S(1)}, f32[1,4,10,8,128]{4,3,2,1,0:T(8,128)S(1)}, u32[]{:S(2)}, u32[]{:S(2)}) %collective-permute-start.26) | collective-permute-done | bytes 163872 | tf_op jit(solution)/shard_map/ppermute | solution.py:125
  110.6 0.1 maximum_bitcast_fusion
  110.7 1.2 %pad_maximum_fusion = f32[4,4,2,10,8,128]{5,4,3,2,1,0:T(8,128)} fusion(f32[4,4,1,10,8,128]{5,4,3,2,1,0:T(8,128)S(1)} %get-tuple-element.82, f32[4,4,1,10,8,128]{5,4,3,2,1,0:T(8,128)S(1)} %get-tuple-element.81), kind=kLoop, calls=%fused_computation | loop fusion | flops 327680 | bytes 2621440 | tf_op jit(solution)/shard_map/stack | solution.py:171
  (63 shorter events, 1.8 us)
Async XLA Ops:
  0.0 10.6 %copy-start = (s32[64,5]{0,1:T(8,128)S(1)}, s32[64,5]{0,1:T(8,128)}, u32[]{:S(2)}) copy-start(s32[64,5]{0,1:T(8,128)} %param.5) | copy-start | bytes 3844
  1.5 9.8 %collective-permute-start.8 = (f32[1,4,10,8,128]{4,3,2,1,0:T(8,128)S(1)}, f32[1,4,10,8,128]{4,3,2,1,0:T(8,128)S(1)}, u32[]{:S(2)}, u32[]{:S(2)}) collective-permute-start(f32[1,4,10,8,128]{4,3,2,1,0:T(8,128)S(1)} %get-tuple-element.58), channel_id=1, source_target_pairs={{0,12},{4,8},{8,4},{12,0},{1,13},{5,9},{9,5},{13,1},{2,14},{6,10},... | collective-permute-start | bytes 491528 | tf_op jit(solution)/shard_map/ppermute | solution.py:125
  6.2 13.4 %collective-permute-start.7 = (f32[1,4,10,8,128]{4,3,2,1,0:T(8,128)S(1)}, f32[1,4,10,8,128]{4,3,2,1,0:T(8,128)S(1)}, u32[]{:S(2)}, u32[]{:S(2)}) collective-permute-start(f32[1,4,10,8,128]{4,3,2,1,0:T(8,128)S(1)} %get-tuple-element.59), channel_id=1, source_target_pairs={{0,8},{4,12},{8,0},{12,4},{1,9},{5,13},{9,1},{13,5},{2,10},{6,14},... | collective-permute-start | bytes 491528 | tf_op jit(solution)/shard_map/ppermute | solution.py:125
  6.2 13.4 %collective-permute-start.6 = (f32[1,4,10,8,128]{4,3,2,1,0:T(8,128)S(1)}, f32[1,4,10,8,128]{4,3,2,1,0:T(8,128)S(1)}, u32[]{:S(2)}, u32[]{:S(2)}) collective-permute-start(f32[1,4,10,8,128]{4,3,2,1,0:T(8,128)S(1)} %get-tuple-element.60), channel_id=1, source_target_pairs={{0,4},{4,0},{8,12},{12,8},{1,5},{5,1},{9,13},{13,9},{2,6},{6,2},{1... | collective-permute-start | bytes 491528 | tf_op jit(solution)/shard_map/ppermute | solution.py:125
  6.9 16.6 %collective-permute-start.2 = (f32[4,1,10,8,128]{4,3,2,1,0:T(8,128)S(1)}, f32[4,1,10,8,128]{4,3,2,1,0:T(8,128)S(1)}, u32[]{:S(2)}, u32[]{:S(2)}) collective-permute-start(f32[4,1,10,8,128]{4,3,2,1,0:T(8,128)S(1)} %get-tuple-element.74), channel_id=1, source_target_pairs={{0,3},{1,2},{2,1},{3,0},{4,7},{5,6},{6,5},{7,4},{8,11},{9,10},{10,... | collective-permute-start | bytes 491528 | tf_op jit(solution)/shard_map/ppermute | solution.py:125
  10.0 14.0 %collective-permute-start.1 = (f32[4,1,10,8,128]{4,3,2,1,0:T(8,128)S(1)}, f32[4,1,10,8,128]{4,3,2,1,0:T(8,128)S(1)}, u32[]{:S(2)}, u32[]{:S(2)}) collective-permute-start(f32[4,1,10,8,128]{4,3,2,1,0:T(8,128)S(1)} %get-tuple-element.75), channel_id=1, source_target_pairs={{0,2},{1,3},{2,0},{3,1},{4,6},{5,7},{6,4},{7,5},{8,10},{9,11},{10,... | collective-permute-start | bytes 491528 | tf_op jit(solution)/shard_map/ppermute | solution.py:125
  11.3 12.7 %collective-permute-start = (f32[4,1,10,8,128]{4,3,2,1,0:T(8,128)S(1)}, f32[4,1,10,8,128]{4,3,2,1,0:T(8,128)S(1)}, u32[]{:S(2)}, u32[]{:S(2)}) collective-permute-start(f32[4,1,10,8,128]{4,3,2,1,0:T(8,128)S(1)} %get-tuple-element.76), channel_id=1, source_target_pairs={{0,1},{1,0},{2,3},{3,2},{4,5},{5,4},{6,7},{7,6},{8,9},{9,8},{10,11... | collective-permute-start | bytes 491528 | tf_op jit(solution)/shard_map/ppermute | solution.py:125
  19.8 9.4 %collective-permute-start.11 = (f32[4,1,10,8,128]{4,3,2,1,0:T(8,128)S(1)}, f32[4,1,10,8,128]{4,3,2,1,0:T(8,128)S(1)}, u32[]{:S(2)}, u32[]{:S(2)}) collective-permute-start(f32[4,1,10,8,128]{4,3,2,1,0:T(8,128)S(1)} %get-tuple-element.50), channel_id=1, source_target_pairs={{0,3},{1,2},{2,1},{3,0},{4,7},{5,6},{6,5},{7,4},{8,11},{9,10},{10,... | collective-permute-start | bytes 491528 | tf_op jit(solution)/shard_map/ppermute | solution.py:125
  22.9 8.3 %collective-permute-start.10 = (f32[4,1,10,8,128]{4,3,2,1,0:T(8,128)S(1)}, f32[4,1,10,8,128]{4,3,2,1,0:T(8,128)S(1)}, u32[]{:S(2)}, u32[]{:S(2)}) collective-permute-start(f32[4,1,10,8,128]{4,3,2,1,0:T(8,128)S(1)} %get-tuple-element.51), channel_id=1, source_target_pairs={{0,2},{1,3},{2,0},{3,1},{4,6},{5,7},{6,4},{7,5},{8,10},{9,11},{10,... | collective-permute-start | bytes 491528 | tf_op jit(solution)/shard_map/ppermute | solution.py:125
  23.5 7.7 %collective-permute-start.9 = (f32[4,1,10,8,128]{4,3,2,1,0:T(8,128)S(1)}, f32[4,1,10,8,128]{4,3,2,1,0:T(8,128)S(1)}, u32[]{:S(2)}, u32[]{:S(2)}) collective-permute-start(f32[4,1,10,8,128]{4,3,2,1,0:T(8,128)S(1)} %get-tuple-element.52), channel_id=1, source_target_pairs={{0,1},{1,0},{2,3},{3,2},{4,5},{5,4},{6,7},{7,6},{8,9},{9,8},{10,11... | collective-permute-start | bytes 491528 | tf_op jit(solution)/shard_map/ppermute | solution.py:125
  24.2 8.8 %collective-permute-start.5 = (f32[1,4,10,8,128]{4,3,2,1,0:T(8,128)S(1)}, f32[1,4,10,8,128]{4,3,2,1,0:T(8,128)S(1)}, u32[]{:S(2)}, u32[]{:S(2)}) collective-permute-start(f32[1,4,10,8,128]{4,3,2,1,0:T(8,128)S(1)} %get-tuple-element.66), channel_id=1, source_target_pairs={{0,12},{4,8},{8,4},{12,0},{1,13},{5,9},{9,5},{13,1},{2,14},{6,10},... | collective-permute-start | bytes 491528 | tf_op jit(solution)/shard_map/ppermute | solution.py:125
  27.0 12.5 %collective-permute-start.4 = (f32[1,4,10,8,128]{4,3,2,1,0:T(8,128)S(1)}, f32[1,4,10,8,128]{4,3,2,1,0:T(8,128)S(1)}, u32[]{:S(2)}, u32[]{:S(2)}) collective-permute-start(f32[1,4,10,8,128]{4,3,2,1,0:T(8,128)S(1)} %get-tuple-element.67), channel_id=1, source_target_pairs={{0,8},{4,12},{8,0},{12,4},{1,9},{5,13},{9,1},{13,5},{2,10},{6,14},... | collective-permute-start | bytes 491528 | tf_op jit(solution)/shard_map/ppermute | solution.py:125
  29.2 10.3 %collective-permute-start.3 = (f32[1,4,10,8,128]{4,3,2,1,0:T(8,128)S(1)}, f32[1,4,10,8,128]{4,3,2,1,0:T(8,128)S(1)}, u32[]{:S(2)}, u32[]{:S(2)}) collective-permute-start(f32[1,4,10,8,128]{4,3,2,1,0:T(8,128)S(1)} %get-tuple-element.68), channel_id=1, source_target_pairs={{0,4},{4,0},{8,12},{12,8},{1,5},{5,1},{9,13},{13,9},{2,6},{6,2},{1... | collective-permute-start | bytes 491528 | tf_op jit(solution)/shard_map/ppermute | solution.py:125
  40.5 27.5 %collective-permute-start.15 = (f32[16,7,8,128]{3,2,1,0:T(8,128)}, f32[16,7,8,128]{3,2,1,0:T(8,128)S(1)}, u32[]{:S(2)}, u32[]{:S(2)}) collective-permute-start(f32[16,7,8,128]{3,2,1,0:T(8,128)} %get-tuple-element.41), channel_id=1, source_target_pairs={{0,1},{1,2},{2,3},{3,4},{4,5},{5,6},{6,7},{7,8},{8,9},{9,10},{10,1... | collective-permute-start | bytes 1376264 | tf_op jit(solution)/shard_map/ppermute | solution.py:160
  43.8 24.1 %collective-permute-start.13 = (f32[16,7,8,128]{3,2,1,0:T(8,128)S(1)}, f32[16,7,8,128]{3,2,1,0:T(8,128)S(1)}, u32[]{:S(2)}, u32[]{:S(2)}) collective-permute-start(f32[16,7,8,128]{3,2,1,0:T(8,128)S(1)} %get-tuple-element.42), channel_id=1, source_target_pairs={{1,0},{2,1},{3,2},{4,3},{5,4},{6,5},{7,6},{8,7},{9,8},{10,9},{11,1... | collective-permute-start | bytes 1376264 | tf_op jit(solution)/shard_map/ppermute | solution.py:160
  50.3 11.0 %copy-start.1 = (s32[64,9]{0,1:T(8,128)S(1)}, s32[64,9]{0,1:T(8,128)}, u32[]{:S(2)}) copy-start(s32[64,9]{0,1:T(8,128)} %param.6) | copy-start | bytes 6916
  50.3 11.1 %copy-start.2 = (s32[64,5]{0,1:T(8,128)S(1)}, s32[64,5]{0,1:T(8,128)}, u32[]{:S(2)}) copy-start(s32[64,5]{0,1:T(8,128)} %param.7) | copy-start | bytes 3844
  51.4 16.6 %collective-permute-start.14 = (f32[16,6,8,128]{3,2,1,0:T(8,128)}, f32[16,6,8,128]{3,2,1,0:T(8,128)S(1)}, u32[]{:S(2)}, u32[]{:S(2)}) collective-permute-start(f32[16,6,8,128]{3,2,1,0:T(8,128)} %get-tuple-element.43), channel_id=1, source_target_pairs={{0,1},{1,2},{2,3},{3,4},{4,5},{5,6},{6,7},{7,8},{8,9},{9,10},{10,1... | collective-permute-start | bytes 1179656 | tf_op jit(solution)/shard_map/ppermute | solution.py:160
  53.3 14.7 %collective-permute-start.12 = (f32[16,6,8,128]{3,2,1,0:T(8,128)}, f32[16,6,8,128]{3,2,1,0:T(8,128)S(1)}, u32[]{:S(2)}, u32[]{:S(2)}) collective-permute-start(f32[16,6,8,128]{3,2,1,0:T(8,128)} %get-tuple-element.44), channel_id=1, source_target_pairs={{1,0},{2,1},{3,2},{4,3},{5,4},{6,5},{7,6},{8,7},{9,8},{10,9},{11,1... | collective-permute-start | bytes 1179656 | tf_op jit(solution)/shard_map/ppermute | solution.py:160
  74.2 9.1 %collective-permute-start.18 = (f32[1,4,10,8,128]{4,3,2,1,0:T(8,128)S(1)}, f32[1,4,10,8,128]{4,3,2,1,0:T(8,128)S(1)}, u32[]{:S(2)}, u32[]{:S(2)}) collective-permute-start(f32[1,4,10,8,128]{4,3,2,1,0:T(8,128)S(1)} %get-tuple-element.22), channel_id=1, source_target_pairs={{0,12},{4,8},{8,4},{12,0},{1,13},{5,9},{9,5},{13,1},{2,14},{6,10},... | collective-permute-start | bytes 491528 | tf_op jit(solution)/shard_map/ppermute | solution.py:125
  74.3 12.9 %collective-permute-start.17 = (f32[1,4,10,8,128]{4,3,2,1,0:T(8,128)S(1)}, f32[1,4,10,8,128]{4,3,2,1,0:T(8,128)S(1)}, u32[]{:S(2)}, u32[]{:S(2)}) collective-permute-start(f32[1,4,10,8,128]{4,3,2,1,0:T(8,128)S(1)} %get-tuple-element.23), channel_id=1, source_target_pairs={{0,8},{4,12},{8,0},{12,4},{1,9},{5,13},{9,1},{13,5},{2,10},{6,14},... | collective-permute-start | bytes 491528 | tf_op jit(solution)/shard_map/ppermute | solution.py:125
  74.4 12.8 %collective-permute-start.16 = (f32[1,4,10,8,128]{4,3,2,1,0:T(8,128)S(1)}, f32[1,4,10,8,128]{4,3,2,1,0:T(8,128)S(1)}, u32[]{:S(2)}, u32[]{:S(2)}) collective-permute-start(f32[1,4,10,8,128]{4,3,2,1,0:T(8,128)S(1)} %get-tuple-element.24), channel_id=1, source_target_pairs={{0,4},{4,0},{8,12},{12,8},{1,5},{5,1},{9,13},{13,9},{2,6},{6,2},{1... | collective-permute-start | bytes 491528 | tf_op jit(solution)/shard_map/ppermute | solution.py:125
  78.7 13.1 %collective-permute-start.24 = (f32[4,1,10,8,128]{4,3,2,1,0:T(8,128)S(1)}, f32[4,1,10,8,128]{4,3,2,1,0:T(8,128)S(1)}, u32[]{:S(2)}, u32[]{:S(2)}) collective-permute-start(f32[4,1,10,8,128]{4,3,2,1,0:T(8,128)S(1)} %get-tuple-element.38), channel_id=1, source_target_pairs={{0,3},{1,2},{2,1},{3,0},{4,7},{5,6},{6,5},{7,4},{8,11},{9,10},{10,... | collective-permute-start | bytes 491528 | tf_op jit(solution)/shard_map/ppermute | solution.py:125
  80.2 12.5 %collective-permute-start.23 = (f32[4,1,10,8,128]{4,3,2,1,0:T(8,128)S(1)}, f32[4,1,10,8,128]{4,3,2,1,0:T(8,128)S(1)}, u32[]{:S(2)}, u32[]{:S(2)}) collective-permute-start(f32[4,1,10,8,128]{4,3,2,1,0:T(8,128)S(1)} %get-tuple-element.39), channel_id=1, source_target_pairs={{0,2},{1,3},{2,0},{3,1},{4,6},{5,7},{6,4},{7,5},{8,10},{9,11},{10,... | collective-permute-start | bytes 491528 | tf_op jit(solution)/shard_map/ppermute | solution.py:125
  83.3 9.4 %collective-permute-start.22 = (f32[4,1,10,8,128]{4,3,2,1,0:T(8,128)S(1)}, f32[4,1,10,8,128]{4,3,2,1,0:T(8,128)S(1)}, u32[]{:S(2)}, u32[]{:S(2)}) collective-permute-start(f32[4,1,10,8,128]{4,3,2,1,0:T(8,128)S(1)} %get-tuple-element.40), channel_id=1, source_target_pairs={{0,1},{1,0},{2,3},{3,2},{4,5},{5,4},{6,7},{7,6},{8,9},{9,8},{10,11... | collective-permute-start | bytes 491528 | tf_op jit(solution)/shard_map/ppermute | solution.py:125
  87.4 12.2 %collective-permute-start.21 = (f32[4,1,10,8,128]{4,3,2,1,0:T(8,128)S(1)}, f32[4,1,10,8,128]{4,3,2,1,0:T(8,128)S(1)}, u32[]{:S(2)}, u32[]{:S(2)}) collective-permute-start(f32[4,1,10,8,128]{4,3,2,1,0:T(8,128)S(1)} %get-tuple-element.14), channel_id=1, source_target_pairs={{0,3},{1,2},{2,1},{3,0},{4,7},{5,6},{6,5},{7,4},{8,11},{9,10},{10,... | collective-permute-start | bytes 491528 | tf_op jit(solution)/shard_map/ppermute | solution.py:125
  91.8 8.6 %collective-permute-start.20 = (f32[4,1,10,8,128]{4,3,2,1,0:T(8,128)S(1)}, f32[4,1,10,8,128]{4,3,2,1,0:T(8,128)S(1)}, u32[]{:S(2)}, u32[]{:S(2)}) collective-permute-start(f32[4,1,10,8,128]{4,3,2,1,0:T(8,128)S(1)} %get-tuple-element.15), channel_id=1, source_target_pairs={{0,2},{1,3},{2,0},{3,1},{4,6},{5,7},{6,4},{7,5},{8,10},{9,11},{10,... | collective-permute-start | bytes 491528 | tf_op jit(solution)/shard_map/ppermute | solution.py:125
  91.8 8.9 %collective-permute-start.19 = (f32[4,1,10,8,128]{4,3,2,1,0:T(8,128)S(1)}, f32[4,1,10,8,128]{4,3,2,1,0:T(8,128)S(1)}, u32[]{:S(2)}, u32[]{:S(2)}) collective-permute-start(f32[4,1,10,8,128]{4,3,2,1,0:T(8,128)S(1)} %get-tuple-element.16), channel_id=1, source_target_pairs={{0,1},{1,0},{2,3},{3,2},{4,5},{5,4},{6,7},{7,6},{8,9},{9,8},{10,11... | collective-permute-start | bytes 491528 | tf_op jit(solution)/shard_map/ppermute | solution.py:125
  93.0 9.0 %collective-permute-start.27 = (f32[1,4,10,8,128]{4,3,2,1,0:T(8,128)S(1)}, f32[1,4,10,8,128]{4,3,2,1,0:T(8,128)S(1)}, u32[]{:S(2)}, u32[]{:S(2)}) collective-permute-start(f32[1,4,10,8,128]{4,3,2,1,0:T(8,128)S(1)} %get-tuple-element.30), channel_id=1, source_target_pairs={{0,12},{4,8},{8,4},{12,0},{1,13},{5,9},{9,5},{13,1},{2,14},{6,10},... | collective-permute-start | bytes 491528 | tf_op jit(solution)/shard_map/ppermute | solution.py:125
  95.1 15.3 %collective-permute-start.26 = (f32[1,4,10,8,128]{4,3,2,1,0:T(8,128)S(1)}, f32[1,4,10,8,128]{4,3,2,1,0:T(8,128)S(1)}, u32[]{:S(2)}, u32[]{:S(2)}) collective-permute-start(f32[1,4,10,8,128]{4,3,2,1,0:T(8,128)S(1)} %get-tuple-element.31), channel_id=1, source_target_pairs={{0,8},{4,12},{8,0},{12,4},{1,9},{5,13},{9,1},{13,5},{2,10},{6,14},... | collective-permute-start | bytes 491528 | tf_op jit(solution)/shard_map/ppermute | solution.py:125
  99.6 10.8 %collective-permute-start.25 = (f32[1,4,10,8,128]{4,3,2,1,0:T(8,128)S(1)}, f32[1,4,10,8,128]{4,3,2,1,0:T(8,128)S(1)}, u32[]{:S(2)}, u32[]{:S(2)}) collective-permute-start(f32[1,4,10,8,128]{4,3,2,1,0:T(8,128)S(1)} %get-tuple-element.32), channel_id=1, source_target_pairs={{0,4},{4,0},{8,12},{12,8},{1,5},{5,1},{9,13},{13,9},{2,6},{6,2},{1... | collective-permute-start | bytes 491528 | tf_op jit(solution)/shard_map/ppermute | solution.py:125

commit v3 on v1

v3 whole, which is shorter than its diff:
```python
import functools

import jax
import jax.numpy as jnp
from jax import lax
from jax.experimental import pallas as pl
from jax.experimental.pallas import tpu as pltpu
from jax.sharding import PartitionSpec as P

BLK = 128
OWN = 4
HALO = 4
PAIR = 2 * BLK
FIRST_OUT = 8
EVERY = ("row", "col", "depth")

BEFORE_ONLY = [(0, s) for s in range(4)] + [(1, s) for s in range(3)]
BOTH = [(0, 4), (1, 3), (1, 4), (2, 0), (2, 1), (3, 0)]
AFTER_ONLY = [(2, s) for s in range(2, 5)] + [(3, s) for s in range(1, 5)]
EARLY_SIDE = 1
INNER = BEFORE_ONLY[7 - EARLY_SIDE :] + BOTH + AFTER_ONLY[:EARLY_SIDE]
OUTER = BEFORE_ONLY[: 7 - EARLY_SIDE] + AFTER_ONLY[EARLY_SIDE:]
INNER_TO_BEFORE, INNER_TO_AFTER = slice(0, 6 + EARLY_SIDE), slice(EARLY_SIDE, 6 + 2 * EARLY_SIDE)
OUTER_TO_BEFORE, OUTER_TO_AFTER = slice(0, 7 - EARLY_SIDE), slice(7 - EARLY_SIDE, 14 - 2 * EARLY_SIDE)


def ranks(row, col, depth):
    core, z_half = row & 1, (row >> 1) & 1
    return col ^ (3 * (core ^ z_half)), depth ^ (3 * core)


def place():
    return tuple(lax.axis_index(axis) for axis in EVERY)


def pack_kernel(last_row, density, mask, *outs):
    row, col, depth = place()
    col_rank, depth_rank = ranks(row, col, depth)

    def weight(rank, block_row, slot):
        value = mask[slot, rank * OWN + block_row].astype(jnp.float32)
        if block_row + slot < 2:
            value = jnp.where((row == 0) & (rank == 0), 0.0, value)
        if block_row + slot > OWN + 1:
            value = jnp.where((row == last_row) & (rank == 15), 0.0, value)
        return value

    for k in range(4):
        for other in range(4):
            rank = (col_rank ^ k) * 4 + other
            for index, (block_row, slot) in enumerate(INNER):
                outs[k][0, other, index] = density[rank * OWN + block_row, slot] * weight(rank, block_row, slot)
            rank = other * 4 + (depth_rank ^ k)
            for index, (block_row, slot) in enumerate(OUTER):
                outs[4 + k][other, 0, index] = density[rank * OWN + block_row, slot] * weight(rank, block_row, slot)


def pack(density, mask):
    vmem = pl.BlockSpec(memory_space=pltpu.VMEM)
    smem = pl.BlockSpec(memory_space=pltpu.SMEM)
    inner = jax.ShapeDtypeStruct((1, 4, len(INNER), 8, BLK), jnp.float32)
    outer = jax.ShapeDtypeStruct((4, 1, len(OUTER), 8, BLK), jnp.float32)
    outs = pl.pallas_call(
        functools.partial(pack_kernel, lax.axis_size("row") - 1),
        out_shape=[inner] * 4 + [outer] * 4,
        in_specs=[vmem, smem],
        out_specs=[vmem] * 8,
        compiler_params=pltpu.CompilerParams(vmem_limit_bytes=16 * 1024 * 1024),
        cost_estimate=pl.CostEstimate(flops=10**6, bytes_accessed=4 * 1024 * 1024, transcendentals=0),
    )(density, mask)
    return list(outs[:4]), list(outs[4:])


EARLY = (
    [(row, slot) for row, slot in OUTER]
    + [(row, slot) for row, slot in INNER]
    + [(row + OWN, slot) for row, slot in INNER[INNER_TO_BEFORE]]
    + [(row - OWN, slot) for row, slot in INNER[INNER_TO_AFTER]]
)
LATE_AFTER = [(row + OWN, slot) for row, slot in OUTER[OUTER_TO_BEFORE]]
LATE_BEFORE = [(row - OWN, slot) for row, slot in OUTER[OUTER_TO_AFTER]]


def split_block(value):
    rounded = value.astype(jnp.bfloat16)
    return rounded, (value - rounded.astype(jnp.float32)).astype(jnp.bfloat16)


def split_kernel(outer, inner, inner_after, inner_before, high, low):
    index = 0
    for source in (outer, inner, inner_after, inner_before):
        for at in range(source.shape[1]):
            high[index], low[index] = split_block(source[:, at].reshape(BLK, BLK))
            index += 1


def split(*operands):
    vmem = pl.BlockSpec(memory_space=pltpu.VMEM)
    part = jax.ShapeDtypeStruct((len(EARLY), BLK, BLK), jnp.bfloat16)
    return pl.pallas_call(
        split_kernel,
        out_shape=(part, part),
        in_specs=[vmem] * 4,
        out_specs=(vmem, vmem),
        cost_estimate=pl.CostEstimate(flops=0, bytes_accessed=16 * 1024 * 1024, transcendentals=0),
        compiler_params=pltpu.CompilerParams(vmem_limit_bytes=16 * 1024 * 1024),
    )(*operands)


def put_block(row, column, parts, high, low):
    rows, columns = slice(row * BLK, (row + 1) * BLK), slice(column * BLK, (column + 1) * BLK)
    high[rows, columns], low[rows, columns] = parts


def product(left_high, left_low, right_high, right_low):
    def dot(a, b):
        return jnp.dot(a, b, preferred_element_type=jnp.float32)

    return dot(left_high, right_high) + (dot(left_high, right_low) + dot(left_low, right_high))


def tile(first, end):
    return slice(first * PAIR, end * PAIR)


def compute_kernel(top, early_high, early_low, late_after, late_before, square_mask, out_mask, *refs):
    *outs, high, low, square_high, square_low = refs
    col_rank, depth_rank = ranks(*place())
    first = (col_rank * 4 + depth_rank) * OWN + top
    zero = jnp.zeros((BLK, BLK), jnp.bfloat16)
    for row, column in ((3, 0), (2, 5), (5, 2), (4, 7), (7, 4), (6, 9), (0, 3), (9, 6)):
        high[row * BLK : (row + 1) * BLK, column * BLK : (column + 1) * BLK] = zero
        low[row * BLK : (row + 1) * BLK, column * BLK : (column + 1) * BLK] = zero
    def needed(blocks):
        for index, (row, slot) in enumerate(blocks):
            at = row - top + 4
            column = at + slot - 2
            if 2 <= at < 8 or (0 <= at < 2 and 2 <= column < 4) or (8 <= at < 10 and 6 <= column < 8):
                yield index, at, column

    for index, row, column in needed(EARLY):
        put_block(row, column, (early_high[index], early_low[index]), high, low)
    for source, blocks in ((late_after, LATE_AFTER), (late_before, LATE_BEFORE)):
        for index, row, column in needed(blocks):
            put_block(row, column, split_block(source[:, index].reshape(BLK, BLK)), high, low)

    kept = {}
    for column in range(5):
        inside, outside = tile(max(2, column) - 1, min(2, column) + 2), tile(column, column + 1)
        square = product(high[tile(2, 3), inside], low[tile(2, 3), inside], high[inside, outside], low[inside, outside])
        for half in range(2):
            for side in range(2):
                slot = 2 * column + side - half
                block = square[half * BLK : (half + 1) * BLK, side * BLK : (side + 1) * BLK]
                if 0 <= slot < 9:
                    block = block * square_mask[slot, first + half].astype(jnp.float32)
                if 2 <= slot < 7:
                    kept[half, slot - 2] = block
                put_block(half, 2 * column + side, split_block(block), square_high, square_low)
    for column in range(1, 4):
        inside, outside = tile(column - 1, column + 2), tile(column, column + 1)
        cube = product(square_high[:, inside], square_low[:, inside], high[inside, outside], low[inside, outside])
        for half in range(2):
            for side in range(2):
                slot = 2 * column + side - half - 2
                if 0 <= slot < 5:
                    block = cube[half * BLK : (half + 1) * BLK, side * BLK : (side + 1) * BLK]
                    gate = out_mask[slot, first + half].astype(jnp.float32)
                    value = (gate * (3.0 * kept[half, slot] - 2.0 * block)).reshape(16, 8, BLK)
                    index = half * 5 + slot
                    if index < outs[0].shape[1]:
                        outs[0][:, index] = value
                    else:
                        outs[1][:, index - outs[0].shape[1]] = value


def compute(top, counts, *operands):
    vmem = pl.BlockSpec(memory_space=pltpu.VMEM)
    smem = pl.BlockSpec(memory_space=pltpu.SMEM)
    window = 10 * BLK
    return pl.pallas_call(
        functools.partial(compute_kernel, top),
        out_shape=[jax.ShapeDtypeStruct((16, count, 8, BLK), jnp.float32) for count in counts],
        in_specs=[vmem] * 4 + [smem] * 2,
        out_specs=[vmem] * len(counts),
        scratch_shapes=[
            pltpu.VMEM((window, window), jnp.bfloat16),
            pltpu.VMEM((window, window), jnp.bfloat16),
            pltpu.VMEM((PAIR, window), jnp.bfloat16),
            pltpu.VMEM((PAIR, window), jnp.bfloat16),
        ],
        compiler_params=pltpu.CompilerParams(vmem_limit_bytes=32 * 1024 * 1024),
        cost_estimate=pl.CostEstimate(flops=2 * 3 * 18 * 256**3, bytes_accessed=4 * 1024 * 1024, transcendentals=0),
    )(*operands)


def send(pieces, axis):
    size = lax.axis_size(axis)
    return pieces[:1] + [lax.ppermute(pieces[k], axis, [(i, i ^ k) for i in range(size)]) for k in range(1, size)]


def cut(value, dim, far):
    return [lax.dynamic_slice_in_dim(value, far ^ k, 1, dim) for k in range(value.shape[dim])]


def join(pieces, dim, near):
    stack = jnp.concatenate(pieces, axis=dim)
    return jnp.concatenate([lax.dynamic_slice_in_dim(stack, near ^ j, 1, dim) for j in range(len(pieces))], axis=dim)


def swap(value, axis, dim, near, far):
    return join(send(cut(value, dim, far), axis), dim, near)


def chain(rows):
    places = [(row, col, depth) for row in range(rows) for col in range(4) for depth in range(4)]
    places.sort(key=lambda at: (at[0], *ranks(*at)))
    return [row * 16 + col * 4 + depth for row, col, depth in places]


def on_device(density, mask_band, mask_square, mask_out):
    row, col, depth = place()
    col_rank, depth_rank = ranks(row, col, depth)
    order = chain(lax.axis_size("row"))
    up = list(zip(order[:-1], order[1:]))
    down = list(zip(order[1:], order[:-1]))

    def halo(group, before_part, after_part):
        after = lax.ppermute(group[:, before_part], EVERY, down)
        before = lax.ppermute(group[:, after_part], EVERY, up)
        return after, before

    inner, outer = pack(density, mask_band.T)
    inner = join(send(inner, "col"), 0, col)
    outer = join(send(outer, "depth"), 1, depth)
    outer = swap(outer, "col", 0, col, col_rank)
    inner = swap(inner, "depth", 1, depth, depth_rank)
    inner = inner.reshape(16, len(INNER), 8, BLK)
    outer = outer.reshape(16, len(OUTER), 8, BLK)
    early = split(outer, inner, *halo(inner, INNER_TO_BEFORE, INNER_TO_AFTER))
    operands = (*early, *halo(outer, OUTER_TO_BEFORE, OUTER_TO_AFTER), mask_square.T, mask_out.T)
    lower, middle = compute(0, (FIRST_OUT, 10 - FIRST_OUT), *operands)
    lower, operands = lax.optimization_barrier((lower, operands))
    (upper,) = compute(2, (10,), *operands)
    upper = jnp.concatenate([middle, upper], axis=1)
    lower = lower.reshape(4, 4, FIRST_OUT, 8, BLK)
    upper = upper.reshape(4, 4, 20 - FIRST_OUT, 8, BLK)
    lower = swap(lower, "col", 0, col_rank, col)
    upper = swap(upper, "depth", 1, depth_rank, depth)
    upper = send(cut(upper, 0, col), "col")
    upper[1], lower = lax.optimization_barrier((upper[1], lower))
    upper = join(upper, 0, col_rank)
    lower = swap(lower, "depth", 1, depth_rank, depth)
    return jnp.concatenate([lower, upper], axis=2).reshape(density.shape)


def solution(mesh):
    return jax.shard_map(
        on_device,
        mesh=mesh,
        in_specs=(
            P("row", None, ("col", "depth"), None),
            P("row", None),
            P("row", None),
            P("row", None),
        ),
        out_specs=P("row", None, ("col", "depth"), None),
        check_vma=False,
    )
```

time: 120 us -> 107 us (0.89)
  blocking collectives: 77 us -> 0 us
  starting transfers between devices: 6.15 us -> 53.2 us
  waiting for transfers between devices: 25.2 us -> 40.3 us
  other arithmetic: 4.33 us -> 1.8 us
  Pallas kernels: 5.96 us -> 7.81 us
  local copies, waits for them, and re-layouts: 1.47 us -> 3.01 us
    all_to_all x2 -> x0, blocking collectives: 77 us -> none  [the longest x1 41.3 us: on_device(): lax.all_to_all(active.reshape(16, 5 * OWN, 8, BLK), LAYERS, split_axis=0,...]
    ppermute x2 -> x28, starting transfers between devices: 6.15 us -> 53.2 us  [the longest x24 41.5 us: send(): lax.ppermute(pieces[k], axis, [(i, i ^ k) for i in range(size)])]
    ppermute x2 -> x28, waiting for transfers between devices: 25.2 us -> 40.3 us  [the longest x24 32.2 us: send(): lax.ppermute(pieces[k], axis, [(i, i ^ k) for i in range(size)])]
    mul x2 -> x0, other arithmetic: 2.41 us -> none  [active_band(): return density * (mask_band.astype(jnp.float32) * inside)[:, :, None, None]]
    pallas_call x1 -> x4, Pallas kernels: 5.96 us -> 7.81 us  [the longest x2 6.49 us: compute(): pl.pallas_call(functools.partial(compute_kernel, top), out_shape=[jax.Sha...]
  transfers between devices with their start and end apart: 2 -> 28, of which waited for: 2 -> 12; matrix products, arithmetic and copies ran while one was open for 1% -> 1% of each run, Pallas kernels for 0% -> 3%
where the time goes in v3:
time: 107 us
  starting transfers between devices  53.2 us (50%)
  waiting for transfers between devices  40.3 us (38%)
  Pallas kernels  7.81 us (7%)
  local copies, waits for them, and re-layouts  3.01 us (3%)
  other arithmetic  1.8 us (2%)
    ppermute x24, starting transfers between devices, send(): lax.ppermute(pieces[k], axis, [(i, i ^ k) for i in range(size)])  41.5 us
    ppermute x24, waiting for transfers between devices, send(): lax.ppermute(pieces[k], axis, [(i, i ^ k) for i in range(size)])  32.2 us
    ppermute x2, starting transfers between devices, halo(): before = lax.ppermute(group[:, after_part], EVERY, up)  7.84 us
    pallas_call x2, Pallas kernels, compute(): pl.pallas_call(functools.partial(compute_kernel, top), out_shape=[jax.Sha...  6.49 us
    ppermute x2, waiting for transfers between devices, halo(): after = lax.ppermute(group[:, before_part], EVERY, down)  5.18 us
    ppermute x2, starting transfers between devices, halo(): after = lax.ppermute(group[:, before_part], EVERY, down)  3.84 us
    ppermute x2, waiting for transfers between devices, halo(): before = lax.ppermute(group[:, after_part], EVERY, up)  2.97 us
  transfers between devices with their start and end apart: 28, of which 12 were waited for; matrix products, arithmetic and copies ran while one was open for 1% of the time, Pallas kernels for 3%

profile of v3, /device:TPU:2, one launch (start us, length us, event | category | flops | bytes accessed | tf_op | source)
XLA Modules:
  0.0 106.7 jit_solution(13271675786812474419)
XLA Ops:
  0.0 1.3 %copy-done = f32[64,5,8,128]{3,2,1,0:T(8,128)S(1)} copy-done((f32[64,5,8,128]{3,2,1,0:T(8,128)S(1)}, f32[64,5,8,128]{3,2,1,0:T(8,128)}, u32[]{:S(2)}) %copy-start) | copy-done | bytes 1310744
  1.3 0.7 copy-done.1
  2.0 1.1 %shard_map.46 = (f32[1,4,8,8,128]{4,3,2,1,0:T(8,128)S(1)}, f32[1,4,8,8,128]{4,3,2,1,0:T(8,128)S(1)}, f32[1,4,8,8,128]{4,3,2,1,0:T(8,128)S(1)}, f32[1,4,8,8,128]{...) custom-call(f32[64,5,8,128]{3,2,1,0:T(8,128)S(1)} %copy-done, ...), custom_call_target="tpu_custom_call" | custom-call | flops 1000000 | bytes 4194304 | tf_op jit(solution)/shard_map/pallas_call | solution.py:63
  3.1 2.0 %collective-permute-start.6 = (f32[1,4,8,8,128]{4,3,2,1,0:T(8,128)S(1)}, f32[1,4,8,8,128]{4,3,2,1,0:T(8,128)S(1)}, u32[]{:S(2)}, u32[]{:S(2)}) collective-permute-start(f32[1,4,8,8,128]{4,3,2,1,0:T(8,128)S(1)} %get-tuple-element.31), channel_id=1, source_target_pairs={{0,4},{4,0},{8,12},{12,8},{1,5},{5,1},{9,13},{13,9},{2,6},{6,2},{1... | collective-permute-start | bytes 393224 | tf_op jit(solution)/shard_map/ppermute | solution.py:199
  5.1 3.3 %collective-permute-start.7 = (f32[1,4,8,8,128]{4,3,2,1,0:T(8,128)S(1)}, f32[1,4,8,8,128]{4,3,2,1,0:T(8,128)S(1)}, u32[]{:S(2)}, u32[]{:S(2)}) collective-permute-start(f32[1,4,8,8,128]{4,3,2,1,0:T(8,128)S(1)} %get-tuple-element.32), channel_id=1, source_target_pairs={{0,8},{4,12},{8,0},{12,4},{1,9},{5,13},{9,1},{13,5},{2,10},{6,14},... | collective-permute-start | bytes 393224 | tf_op jit(solution)/shard_map/ppermute | solution.py:199
  8.4 1.6 %collective-permute-start = (f32[4,1,12,8,128]{4,3,2,1,0:T(8,128)S(1)}, f32[4,1,12,8,128]{4,3,2,1,0:T(8,128)S(1)}, u32[]{:S(2)}, u32[]{:S(2)}) collective-permute-start(f32[4,1,12,8,128]{4,3,2,1,0:T(8,128)S(1)} %get-tuple-element.27), channel_id=1, source_target_pairs={{0,1},{1,0},{2,3},{3,2},{4,5},{5,4},{6,7},{7,6},{8,9},{9,8},{10,11... | collective-permute-start | bytes 589832 | tf_op jit(solution)/shard_map/ppermute | solution.py:199
  10.0 2.9 %collective-permute-start.1 = (f32[4,1,12,8,128]{4,3,2,1,0:T(8,128)S(1)}, f32[4,1,12,8,128]{4,3,2,1,0:T(8,128)S(1)}, u32[]{:S(2)}, u32[]{:S(2)}) collective-permute-start(f32[4,1,12,8,128]{4,3,2,1,0:T(8,128)S(1)} %get-tuple-element.28), channel_id=1, source_target_pairs={{0,2},{1,3},{2,0},{3,1},{4,6},{5,7},{6,4},{7,5},{8,10},{9,11},{10,... | collective-permute-start | bytes 589832 | tf_op jit(solution)/shard_map/ppermute | solution.py:199
  13.0 0.3 collective-permute-start.2
  13.3 5.0 %collective-permute-done.7 = f32[1,4,8,8,128]{4,3,2,1,0:T(8,128)S(1)} collective-permute-done((f32[1,4,8,8,128]{4,3,2,1,0:T(8,128)S(1)}, f32[1,4,8,8,128]{4,3,2,1,0:T(8,128)S(1)}, u32[]{:S(2)}, u32[]{:S(2)}) %collective-permute-start.7) | collective-permute-done | bytes 131104 | tf_op jit(solution)/shard_map/ppermute | solution.py:199
  18.6 3.3 %collective-permute-start.10 = (f32[4,1,8,8,128]{4,3,2,1,0:T(8,128)S(1)}, f32[4,1,8,8,128]{4,3,2,1,0:T(8,128)S(1)}, u32[]{:S(2)}, u32[]{:S(2)}) collective-permute-start(f32[4,1,8,8,128]{4,3,2,1,0:T(8,128)S(1)} %get-tuple-element.101), channel_id=1, source_target_pairs={{0,2},{1,3},{2,0},{3,1},{4,6},{5,7},{6,4},{7,5},{8,10},{9,11},{10,... | collective-permute-start | bytes 393224 | tf_op jit(solution)/shard_map/ppermute | solution.py:199
  21.9 1.1 collective-permute-start.11
  23.0 4.8 %collective-permute-done.2 = f32[4,1,12,8,128]{4,3,2,1,0:T(8,128)S(1)} collective-permute-done((f32[4,1,12,8,128]{4,3,2,1,0:T(8,128)S(1)}, f32[4,1,12,8,128]{4,3,2,1,0:T(8,128)S(1)}, u32[]{:S(2)}, u32[]{:S(2)}) %collective-permute-start.2) | collective-permute-done | bytes 196640 | tf_op jit(solution)/shard_map/ppermute | solution.py:199
  28.0 0.1 constant_dynamic-slice_fusion.51
  28.0 0.1 collective-permute-start.3
  28.1 4.1 %collective-permute-start.4 = (f32[1,4,12,8,128]{4,3,2,1,0:T(8,128)S(1)}, f32[1,4,12,8,128]{4,3,2,1,0:T(8,128)S(1)}, u32[]{:S(2)}, u32[]{:S(2)}) collective-permute-start(f32[1,4,12,8,128]{4,3,2,1,0:T(8,128)S(1)} %get-tuple-element.71), channel_id=1, source_target_pairs={{0,8},{4,12},{8,0},{12,4},{1,9},{5,13},{9,1},{13,5},{2,10},{6,14},... | collective-permute-start | bytes 589832 | tf_op jit(solution)/shard_map/ppermute | solution.py:199
  32.2 0.3 collective-permute-start.5
  32.7 1.9 %collective-permute-start.12 = (f32[16,7,8,128]{3,2,1,0:T(8,128)S(1)}, f32[16,7,8,128]{3,2,1,0:T(8,128)S(1)}, u32[]{:S(2)}, u32[]{:S(2)}) collective-permute-start(f32[16,7,8,128]{3,2,1,0:T(8,128)S(1)} %get-tuple-element.94), channel_id=1, source_target_pairs={{1,0},{2,1},{3,2},{4,3},{5,4},{6,5},{7,6},{8,7},{9,8},{10,9},{11,1... | collective-permute-start | bytes 1376264 | tf_op jit(solution)/shard_map/ppermute | solution.py:229
  34.7 3.9 %collective-permute-start.13 = (f32[16,7,8,128]{3,2,1,0:T(8,128)S(1)}, f32[16,7,8,128]{3,2,1,0:T(8,128)S(1)}, u32[]{:S(2)}, u32[]{:S(2)}) collective-permute-start(f32[16,7,8,128]{3,2,1,0:T(8,128)S(1)} %get-tuple-element.93), channel_id=1, source_target_pairs={{0,1},{1,2},{2,3},{3,4},{4,5},{5,6},{6,7},{7,8},{8,9},{9,10},{10,1... | collective-permute-start | bytes 1376264 | tf_op jit(solution)/shard_map/ppermute | solution.py:230
  38.6 6.4 %collective-permute-done.4 = f32[1,4,12,8,128]{4,3,2,1,0:T(8,128)S(1)} collective-permute-done((f32[1,4,12,8,128]{4,3,2,1,0:T(8,128)S(1)}, f32[1,4,12,8,128]{4,3,2,1,0:T(8,128)S(1)}, u32[]{:S(2)}, u32[]{:S(2)}) %collective-permute-start.4) | collective-permute-done | bytes 196640 | tf_op jit(solution)/shard_map/ppermute | solution.py:199
  45.1 0.1 constant_dynamic-slice_fusion.47
  45.3 1.9 %collective-permute-start.14 = (f32[16,6,8,128]{3,2,1,0:T(8,128)S(1)}, f32[16,6,8,128]{3,2,1,0:T(8,128)S(1)}, u32[]{:S(2)}, u32[]{:S(2)}) collective-permute-start(f32[16,6,8,128]{3,2,1,0:T(8,128)S(1)} %get-tuple-element.64), channel_id=1, source_target_pairs={{1,0},{2,1},{3,2},{4,3},{5,4},{6,5},{7,6},{8,7},{9,8},{10,9},{11,1... | collective-permute-start | bytes 1179656 | tf_op jit(solution)/shard_map/ppermute | solution.py:229
  47.3 3.9 %collective-permute-start.15 = (f32[16,6,8,128]{3,2,1,0:T(8,128)S(1)}, f32[16,6,8,128]{3,2,1,0:T(8,128)S(1)}, u32[]{:S(2)}, u32[]{:S(2)}) collective-permute-start(f32[16,6,8,128]{3,2,1,0:T(8,128)S(1)} %get-tuple-element.63), channel_id=1, source_target_pairs={{0,1},{1,2},{2,3},{3,4},{4,5},{5,6},{6,7},{7,8},{8,9},{9,10},{10,1... | collective-permute-start | bytes 1179656 | tf_op jit(solution)/shard_map/ppermute | solution.py:230
  51.2 0.2 shard_map.47
  51.5 5.2 %collective-permute-done.14.late_after = f32[16,6,8,128]{3,2,1,0:T(8,128)S(1)} collective-permute-done((f32[16,6,8,128]{3,2,1,0:T(8,128)S(1)}, f32[16,6,8,128]{3,2,1,0:T(8,128)S(1)}, u32[]{:S(2)}, u32[]{:S(2)}) %collective-permute-start.14) | collective-permute-done | bytes 393248 | tf_op jit(solution)/shard_map/ppermute | solution.py:229
  56.6 3.0 %collective-permute-done.15.late_before = f32[16,6,8,128]{3,2,1,0:T(8,128)S(1)} collective-permute-done((f32[16,6,8,128]{3,2,1,0:T(8,128)S(1)}, f32[16,6,8,128]{3,2,1,0:T(8,128)S(1)}, u32[]{:S(2)}, u32[]{:S(2)}) %collective-permute-start.15) | collective-permute-done | bytes 393248 | tf_op jit(solution)/shard_map/ppermute | solution.py:230
  59.6 3.2 %shard_map.48 = (f32[16,8,8,128]{3,2,1,0:T(8,128)S(1)}, f32[16,2,8,128]{3,2,1,0:T(8,128)S(1)}) custom-call(bf16[34,128,128]{2,1,0:T(8,128)(2,1)S(1)} %get-tuple-element.38.early_high, bf16[34,128,128]{2,1,0:T(8,128)(2,1)S(1)} %get-tuple-element.39.early_low, f32[16,6,8,128]{3,2,1,0:T(8,128)S(1)} %collective-permute-done.14.late_after, ...), custom_call_target="tpu_custom_call" | custom-call | flops 1811939328 | bytes 4194304 | tf_op jit(solution)/shard_map/pallas_call | solution.py:181
  62.9 4.3 %collective-permute-start.20 = (f32[1,4,8,8,128]{4,3,2,1,0:T(8,128)S(1)}, f32[1,4,8,8,128]{4,3,2,1,0:T(8,128)S(1)}, u32[]{:S(2)}, u32[]{:S(2)}) collective-permute-start(f32[1,4,8,8,128]{4,3,2,1,0:T(8,128)S(1)} %get-tuple-element.92), channel_id=1, source_target_pairs={{0,4},{4,0},{8,12},{12,8},{1,5},{5,1},{9,13},{13,9},{2,6},{6,2},{1... | collective-permute-start | bytes 393224 | tf_op jit(solution)/shard_map/ppermute | solution.py:199
  67.2 2.6 %collective-permute-start.21 = (f32[1,4,8,8,128]{4,3,2,1,0:T(8,128)S(1)}, f32[1,4,8,8,128]{4,3,2,1,0:T(8,128)S(1)}, u32[]{:S(2)}, u32[]{:S(2)}) collective-permute-start(f32[1,4,8,8,128]{4,3,2,1,0:T(8,128)S(1)} %get-tuple-element.91), channel_id=1, source_target_pairs={{0,8},{4,12},{8,0},{12,4},{1,9},{5,13},{9,1},{13,5},{2,10},{6,14},... | collective-permute-start | bytes 393224 | tf_op jit(solution)/shard_map/ppermute | solution.py:199
  69.8 0.8 collective-permute-start.22
  70.7 3.2 %shard_map.49 = f32[16,10,8,128]{3,2,1,0:T(8,128)S(1)} custom-call(bf16[34,128,128]{2,1,0:T(8,128)(2,1)S(1)} %get-tuple-element.38.early_high, bf16[34,128,128]{2,1,0:T(8,128)(2,1)S(1)} %get-tuple-element.39.early_low, f32[16,6,8,128]{3,2,1,0:T(8,128)S(1)} %collective-permute-done.14.late_after, f32[16,6,8,128]{3,2,1,0:T(8,128)S(1)} %collective-permute-done.15.late_before, ...), custom_call_target="tpu_custom_call" | custom-call | flops 1811939328 | bytes 4194304 | tf_op jit(solution)/shard_map/pallas_call | solution.py:181
  73.9 0.1 pad_maximum_fusion.3
  74.1 0.1 collective-permute-start.16
  74.2 5.4 %collective-permute-start.17 = (f32[4,1,12,8,128]{4,3,2,1,0:T(8,128)S(1)}, f32[4,1,12,8,128]{4,3,2,1,0:T(8,128)S(1)}, u32[]{:S(2)}, u32[]{:S(2)}) collective-permute-start(f32[4,1,12,8,128]{4,3,2,1,0:T(8,128)S(1)} %get-tuple-element.61), channel_id=1, source_target_pairs={{0,2},{1,3},{2,0},{3,1},{4,6},{5,7},{6,4},{7,5},{8,10},{9,11},{10,... | collective-permute-start | bytes 589832 | tf_op jit(solution)/shard_map/ppermute | solution.py:199
  79.7 1.9 %collective-permute-done.16 = f32[4,1,12,8,128]{4,3,2,1,0:T(8,128)S(1)} collective-permute-done((f32[4,1,12,8,128]{4,3,2,1,0:T(8,128)S(1)}, f32[4,1,12,8,128]{4,3,2,1,0:T(8,128)S(1)}, u32[]{:S(2)}, u32[]{:S(2)}) %collective-permute-start.16) | collective-permute-done | bytes 196640 | tf_op jit(solution)/shard_map/ppermute | solution.py:199
  81.6 4.8 %collective-permute-done.17 = f32[4,1,12,8,128]{4,3,2,1,0:T(8,128)S(1)} collective-permute-done((f32[4,1,12,8,128]{4,3,2,1,0:T(8,128)S(1)}, f32[4,1,12,8,128]{4,3,2,1,0:T(8,128)S(1)}, u32[]{:S(2)}, u32[]{:S(2)}) %collective-permute-start.17) | collective-permute-done | bytes 196640 | tf_op jit(solution)/shard_map/ppermute | solution.py:199
  86.4 2.0 %collective-permute-done.18 = f32[4,1,12,8,128]{4,3,2,1,0:T(8,128)S(1)} collective-permute-done((f32[4,1,12,8,128]{4,3,2,1,0:T(8,128)S(1)}, f32[4,1,12,8,128]{4,3,2,1,0:T(8,128)S(1)}, u32[]{:S(2)}, u32[]{:S(2)}) %collective-permute-start.18) | collective-permute-done | bytes 196640 | tf_op jit(solution)/shard_map/ppermute | solution.py:199
  88.5 0.1 constant_dynamic-slice_fusion.27
  88.7 0.7 collective-permute-start.19
  89.4 1.3 %collective-permute-start.26 = (f32[1,4,12,8,128]{4,3,2,1,0:T(8,128)S(1)}, f32[1,4,12,8,128]{4,3,2,1,0:T(8,128)S(1)}, u32[]{:S(2)}, u32[]{:S(2)}) collective-permute-start(f32[1,4,12,8,128]{4,3,2,1,0:T(8,128)S(1)} %get-tuple-element.53), channel_id=1, source_target_pairs={{0,8},{4,12},{8,0},{12,4},{1,9},{5,13},{9,1},{13,5},{2,10},{6,14},... | collective-permute-start | bytes 589832 | tf_op jit(solution)/shard_map/ppermute | solution.py:199
  90.6 2.6 %collective-permute-start.27 = (f32[1,4,12,8,128]{4,3,2,1,0:T(8,128)S(1)}, f32[1,4,12,8,128]{4,3,2,1,0:T(8,128)S(1)}, u32[]{:S(2)}, u32[]{:S(2)}) collective-permute-start(f32[1,4,12,8,128]{4,3,2,1,0:T(8,128)S(1)} %get-tuple-element.52), channel_id=1, source_target_pairs={{0,12},{4,8},{8,4},{12,0},{1,13},{5,9},{9,5},{13,1},{2,14},{6,10},... | collective-permute-start | bytes 589832 | tf_op jit(solution)/shard_map/ppermute | solution.py:199
  93.3 4.0 %collective-permute-done.19 = f32[1,4,12,8,128]{4,3,2,1,0:T(8,128)S(1)} collective-permute-done((f32[1,4,12,8,128]{4,3,2,1,0:T(8,128)S(1)}, f32[1,4,12,8,128]{4,3,2,1,0:T(8,128)S(1)}, u32[]{:S(2)}, u32[]{:S(2)}) %collective-permute-start.19) | collective-permute-done | bytes 196640 | tf_op jit(solution)/shard_map/ppermute | solution.py:199
  97.3 0.1 collective-permute-start.23
  97.4 1.2 %collective-permute-start.24 = (f32[4,1,8,8,128]{4,3,2,1,0:T(8,128)S(1)}, f32[4,1,8,8,128]{4,3,2,1,0:T(8,128)S(1)}, u32[]{:S(2)}, u32[]{:S(2)}) collective-permute-start(f32[4,1,8,8,128]{4,3,2,1,0:T(8,128)S(1)} %get-tuple-element.83), channel_id=1, source_target_pairs={{0,2},{1,3},{2,0},{3,1},{4,6},{5,7},{6,4},{7,5},{8,10},{9,11},{10,... | collective-permute-start | bytes 393224 | tf_op jit(solution)/shard_map/ppermute | solution.py:199
  98.7 3.5 %collective-permute-start.25 = (f32[4,1,8,8,128]{4,3,2,1,0:T(8,128)S(1)}, f32[4,1,8,8,128]{4,3,2,1,0:T(8,128)S(1)}, u32[]{:S(2)}, u32[]{:S(2)}) collective-permute-start(f32[4,1,8,8,128]{4,3,2,1,0:T(8,128)S(1)} %get-tuple-element.82), channel_id=1, source_target_pairs={{0,3},{1,2},{2,1},{3,0},{4,7},{5,6},{6,5},{7,4},{8,11},{9,10},{10,... | collective-permute-start | bytes 393224 | tf_op jit(solution)/shard_map/ppermute | solution.py:199
  102.1 0.7 collective-permute-done.26
  103.0 1.0 collective-permute-done.24
  104.0 1.4 %collective-permute-done.25 = f32[4,1,8,8,128]{4,3,2,1,0:T(8,128)S(1)} collective-permute-done((f32[4,1,8,8,128]{4,3,2,1,0:T(8,128)S(1)}, f32[4,1,8,8,128]{4,3,2,1,0:T(8,128)S(1)}, u32[]{:S(2)}, u32[]{:S(2)}) %collective-permute-start.25) | collective-permute-done | bytes 131104 | tf_op jit(solution)/shard_map/ppermute | solution.py:199
  105.5 1.2 %maximum_maximum_fusion = f32[4,4,20,8,128]{4,3,2,1,0:T(8,128)} fusion(f32[1,4,12,8,128]{4,3,2,1,0:T(8,128)S(1)} %get-tuple-element.48, f32[1,4,12,8,128]{4,3,2,1,0:T(8,128)S(1)} %get-tuple-element.49, f32[1,4,12,8,128]{4,3,2,1,0:T(8,128)S(1)} %get-tuple-element.50, f32[1,4,12,8,128]{4,3,2,1,0:T(8,128)S(1)} %get-tuple-element.47, ...), kind=kLoop, calls=%fused_computation | loop fusion | flops 2293760 | bytes 2621440 | tf_op jit(solution)/shard_map/concatenate | solution.py:254
  (58 shorter events, 1.4 us)
Async XLA Ops:
  0.0 1.3 %copy-start = (f32[64,5,8,128]{3,2,1,0:T(8,128)S(1)}, f32[64,5,8,128]{3,2,1,0:T(8,128)}, u32[]{:S(2)}) copy-start(f32[64,5,8,128]{3,2,1,0:T(8,128)} %density.1) | copy-start | bytes 3932164
  1.3 0.7 copy-start.1
  3.1 9.9 %collective-permute-start.6 = (f32[1,4,8,8,128]{4,3,2,1,0:T(8,128)S(1)}, f32[1,4,8,8,128]{4,3,2,1,0:T(8,128)S(1)}, u32[]{:S(2)}, u32[]{:S(2)}) collective-permute-start(f32[1,4,8,8,128]{4,3,2,1,0:T(8,128)S(1)} %get-tuple-element.31), channel_id=1, source_target_pairs={{0,4},{4,0},{8,12},{12,8},{1,5},{5,1},{9,13},{13,9},{2,6},{6,2},{1... | collective-permute-start | bytes 393224 | tf_op jit(solution)/shard_map/ppermute | solution.py:199
  5.1 13.2 %collective-permute-start.7 = (f32[1,4,8,8,128]{4,3,2,1,0:T(8,128)S(1)}, f32[1,4,8,8,128]{4,3,2,1,0:T(8,128)S(1)}, u32[]{:S(2)}, u32[]{:S(2)}) collective-permute-start(f32[1,4,8,8,128]{4,3,2,1,0:T(8,128)S(1)} %get-tuple-element.32), channel_id=1, source_target_pairs={{0,8},{4,12},{8,0},{12,4},{1,9},{5,13},{9,1},{13,5},{2,10},{6,14},... | collective-permute-start | bytes 393224 | tf_op jit(solution)/shard_map/ppermute | solution.py:199
  8.4 10.0 %collective-permute-start.8 = (f32[1,4,8,8,128]{4,3,2,1,0:T(8,128)S(1)}, f32[1,4,8,8,128]{4,3,2,1,0:T(8,128)S(1)}, u32[]{:S(2)}, u32[]{:S(2)}) collective-permute-start(f32[1,4,8,8,128]{4,3,2,1,0:T(8,128)S(1)} %get-tuple-element.33), channel_id=1, source_target_pairs={{0,12},{4,8},{8,4},{12,0},{1,13},{5,9},{9,5},{13,1},{2,14},{6,10},... | collective-permute-start | bytes 393224 | tf_op jit(solution)/shard_map/ppermute | solution.py:199
  8.4 14.5 %collective-permute-start = (f32[4,1,12,8,128]{4,3,2,1,0:T(8,128)S(1)}, f32[4,1,12,8,128]{4,3,2,1,0:T(8,128)S(1)}, u32[]{:S(2)}, u32[]{:S(2)}) collective-permute-start(f32[4,1,12,8,128]{4,3,2,1,0:T(8,128)S(1)} %get-tuple-element.27), channel_id=1, source_target_pairs={{0,1},{1,0},{2,3},{3,2},{4,5},{5,4},{6,7},{7,6},{8,9},{9,8},{10,11... | collective-permute-start | bytes 589832 | tf_op jit(solution)/shard_map/ppermute | solution.py:199
  10.0 13.0 %collective-permute-start.1 = (f32[4,1,12,8,128]{4,3,2,1,0:T(8,128)S(1)}, f32[4,1,12,8,128]{4,3,2,1,0:T(8,128)S(1)}, u32[]{:S(2)}, u32[]{:S(2)}) collective-permute-start(f32[4,1,12,8,128]{4,3,2,1,0:T(8,128)S(1)} %get-tuple-element.28), channel_id=1, source_target_pairs={{0,2},{1,3},{2,0},{3,1},{4,6},{5,7},{6,4},{7,5},{8,10},{9,11},{10,... | collective-permute-start | bytes 589832 | tf_op jit(solution)/shard_map/ppermute | solution.py:199
  13.0 14.8 %collective-permute-start.2 = (f32[4,1,12,8,128]{4,3,2,1,0:T(8,128)S(1)}, f32[4,1,12,8,128]{4,3,2,1,0:T(8,128)S(1)}, u32[]{:S(2)}, u32[]{:S(2)}) collective-permute-start(f32[4,1,12,8,128]{4,3,2,1,0:T(8,128)S(1)} %get-tuple-element.29), channel_id=1, source_target_pairs={{0,3},{1,2},{2,1},{3,0},{4,7},{5,6},{6,5},{7,4},{8,11},{9,10},{10,... | collective-permute-start | bytes 589832 | tf_op jit(solution)/shard_map/ppermute | solution.py:199
  18.6 13.7 %collective-permute-start.10 = (f32[4,1,8,8,128]{4,3,2,1,0:T(8,128)S(1)}, f32[4,1,8,8,128]{4,3,2,1,0:T(8,128)S(1)}, u32[]{:S(2)}, u32[]{:S(2)}) collective-permute-start(f32[4,1,8,8,128]{4,3,2,1,0:T(8,128)S(1)} %get-tuple-element.101), channel_id=1, source_target_pairs={{0,2},{1,3},{2,0},{3,1},{4,6},{5,7},{6,4},{7,5},{8,10},{9,11},{10,... | collective-permute-start | bytes 393224 | tf_op jit(solution)/shard_map/ppermute | solution.py:199
  21.9 10.7 %collective-permute-start.11 = (f32[4,1,8,8,128]{4,3,2,1,0:T(8,128)S(1)}, f32[4,1,8,8,128]{4,3,2,1,0:T(8,128)S(1)}, u32[]{:S(2)}, u32[]{:S(2)}) collective-permute-start(f32[4,1,8,8,128]{4,3,2,1,0:T(8,128)S(1)} %get-tuple-element.100), channel_id=1, source_target_pairs={{0,3},{1,2},{2,1},{3,0},{4,7},{5,6},{6,5},{7,4},{8,11},{9,10},{10,... | collective-permute-start | bytes 393224 | tf_op jit(solution)/shard_map/ppermute | solution.py:199
  22.9 9.6 %collective-permute-start.9 = (f32[4,1,8,8,128]{4,3,2,1,0:T(8,128)S(1)}, f32[4,1,8,8,128]{4,3,2,1,0:T(8,128)S(1)}, u32[]{:S(2)}, u32[]{:S(2)}) collective-permute-start(f32[4,1,8,8,128]{4,3,2,1,0:T(8,128)S(1)} %get-tuple-element.102), channel_id=1, source_target_pairs={{0,1},{1,0},{2,3},{3,2},{4,5},{5,4},{6,7},{7,6},{8,9},{9,8},{10,11... | collective-permute-start | bytes 393224 | tf_op jit(solution)/shard_map/ppermute | solution.py:199
  28.0 10.6 %collective-permute-start.3 = (f32[1,4,12,8,128]{4,3,2,1,0:T(8,128)S(1)}, f32[1,4,12,8,128]{4,3,2,1,0:T(8,128)S(1)}, u32[]{:S(2)}, u32[]{:S(2)}) collective-permute-start(f32[1,4,12,8,128]{4,3,2,1,0:T(8,128)S(1)} %get-tuple-element.72), channel_id=1, source_target_pairs={{0,4},{4,0},{8,12},{12,8},{1,5},{5,1},{9,13},{13,9},{2,6},{6,2},{1... | collective-permute-start | bytes 589832 | tf_op jit(solution)/shard_map/ppermute | solution.py:199
  28.1 16.9 %collective-permute-start.4 = (f32[1,4,12,8,128]{4,3,2,1,0:T(8,128)S(1)}, f32[1,4,12,8,128]{4,3,2,1,0:T(8,128)S(1)}, u32[]{:S(2)}, u32[]{:S(2)}) collective-permute-start(f32[1,4,12,8,128]{4,3,2,1,0:T(8,128)S(1)} %get-tuple-element.71), channel_id=1, source_target_pairs={{0,8},{4,12},{8,0},{12,4},{1,9},{5,13},{9,1},{13,5},{2,10},{6,14},... | collective-permute-start | bytes 589832 | tf_op jit(solution)/shard_map/ppermute | solution.py:199
  32.2 12.8 %collective-permute-start.5 = (f32[1,4,12,8,128]{4,3,2,1,0:T(8,128)S(1)}, f32[1,4,12,8,128]{4,3,2,1,0:T(8,128)S(1)}, u32[]{:S(2)}, u32[]{:S(2)}) collective-permute-start(f32[1,4,12,8,128]{4,3,2,1,0:T(8,128)S(1)} %get-tuple-element.70), channel_id=1, source_target_pairs={{0,12},{4,8},{8,4},{12,0},{1,13},{5,9},{9,5},{13,1},{2,14},{6,10},... | collective-permute-start | bytes 589832 | tf_op jit(solution)/shard_map/ppermute | solution.py:199
  32.7 18.5 %collective-permute-start.12 = (f32[16,7,8,128]{3,2,1,0:T(8,128)S(1)}, f32[16,7,8,128]{3,2,1,0:T(8,128)S(1)}, u32[]{:S(2)}, u32[]{:S(2)}) collective-permute-start(f32[16,7,8,128]{3,2,1,0:T(8,128)S(1)} %get-tuple-element.94), channel_id=1, source_target_pairs={{1,0},{2,1},{3,2},{4,3},{5,4},{6,5},{7,6},{8,7},{9,8},{10,9},{11,1... | collective-permute-start | bytes 1376264 | tf_op jit(solution)/shard_map/ppermute | solution.py:229
  34.7 16.5 %collective-permute-start.13 = (f32[16,7,8,128]{3,2,1,0:T(8,128)S(1)}, f32[16,7,8,128]{3,2,1,0:T(8,128)S(1)}, u32[]{:S(2)}, u32[]{:S(2)}) collective-permute-start(f32[16,7,8,128]{3,2,1,0:T(8,128)S(1)} %get-tuple-element.93), channel_id=1, source_target_pairs={{0,1},{1,2},{2,3},{3,4},{4,5},{5,6},{6,7},{7,8},{8,9},{9,10},{10,1... | collective-permute-start | bytes 1376264 | tf_op jit(solution)/shard_map/ppermute | solution.py:230
  45.3 14.3 %copy-start.2 = (s32[64,9]{0,1:T(8,128)S(1)}, s32[64,9]{0,1:T(8,128)}, u32[]{:S(2)}) copy-start(s32[64,9]{0,1:T(8,128)} %param.6) | copy-start | bytes 6916
  45.3 14.3 %copy-start.3 = (s32[64,5]{0,1:T(8,128)S(1)}, s32[64,5]{0,1:T(8,128)}, u32[]{:S(2)}) copy-start(s32[64,5]{0,1:T(8,128)} %param.7) | copy-start | bytes 3844
  45.3 11.3 %collective-permute-start.14 = (f32[16,6,8,128]{3,2,1,0:T(8,128)S(1)}, f32[16,6,8,128]{3,2,1,0:T(8,128)S(1)}, u32[]{:S(2)}, u32[]{:S(2)}) collective-permute-start(f32[16,6,8,128]{3,2,1,0:T(8,128)S(1)} %get-tuple-element.64), channel_id=1, source_target_pairs={{1,0},{2,1},{3,2},{4,3},{5,4},{6,5},{7,6},{8,7},{9,8},{10,9},{11,1... | collective-permute-start | bytes 1179656 | tf_op jit(solution)/shard_map/ppermute | solution.py:229
  47.3 12.3 %collective-permute-start.15 = (f32[16,6,8,128]{3,2,1,0:T(8,128)S(1)}, f32[16,6,8,128]{3,2,1,0:T(8,128)S(1)}, u32[]{:S(2)}, u32[]{:S(2)}) collective-permute-start(f32[16,6,8,128]{3,2,1,0:T(8,128)S(1)} %get-tuple-element.63), channel_id=1, source_target_pairs={{0,1},{1,2},{2,3},{3,4},{4,5},{5,6},{6,7},{7,8},{8,9},{9,10},{10,1... | collective-permute-start | bytes 1179656 | tf_op jit(solution)/shard_map/ppermute | solution.py:230
  62.9 16.7 %collective-permute-start.20 = (f32[1,4,8,8,128]{4,3,2,1,0:T(8,128)S(1)}, f32[1,4,8,8,128]{4,3,2,1,0:T(8,128)S(1)}, u32[]{:S(2)}, u32[]{:S(2)}) collective-permute-start(f32[1,4,8,8,128]{4,3,2,1,0:T(8,128)S(1)} %get-tuple-element.92), channel_id=1, source_target_pairs={{0,4},{4,0},{8,12},{12,8},{1,5},{5,1},{9,13},{13,9},{2,6},{6,2},{1... | collective-permute-start | bytes 393224 | tf_op jit(solution)/shard_map/ppermute | solution.py:199
  67.2 12.4 %collective-permute-start.21 = (f32[1,4,8,8,128]{4,3,2,1,0:T(8,128)S(1)}, f32[1,4,8,8,128]{4,3,2,1,0:T(8,128)S(1)}, u32[]{:S(2)}, u32[]{:S(2)}) collective-permute-start(f32[1,4,8,8,128]{4,3,2,1,0:T(8,128)S(1)} %get-tuple-element.91), channel_id=1, source_target_pairs={{0,8},{4,12},{8,0},{12,4},{1,9},{5,13},{9,1},{13,5},{2,10},{6,14},... | collective-permute-start | bytes 393224 | tf_op jit(solution)/shard_map/ppermute | solution.py:199
  69.8 9.8 %collective-permute-start.22 = (f32[1,4,8,8,128]{4,3,2,1,0:T(8,128)S(1)}, f32[1,4,8,8,128]{4,3,2,1,0:T(8,128)S(1)}, u32[]{:S(2)}, u32[]{:S(2)}) collective-permute-start(f32[1,4,8,8,128]{4,3,2,1,0:T(8,128)S(1)} %get-tuple-element.90), channel_id=1, source_target_pairs={{0,12},{4,8},{8,4},{12,0},{1,13},{5,9},{9,5},{13,1},{2,14},{6,10},... | collective-permute-start | bytes 393224 | tf_op jit(solution)/shard_map/ppermute | solution.py:199
  74.1 7.5 %collective-permute-start.16 = (f32[4,1,12,8,128]{4,3,2,1,0:T(8,128)S(1)}, f32[4,1,12,8,128]{4,3,2,1,0:T(8,128)S(1)}, u32[]{:S(2)}, u32[]{:S(2)}) collective-permute-start(f32[4,1,12,8,128]{4,3,2,1,0:T(8,128)S(1)} %get-tuple-element.62), channel_id=1, source_target_pairs={{0,1},{1,0},{2,3},{3,2},{4,5},{5,4},{6,7},{7,6},{8,9},{9,8},{10,11... | collective-permute-start | bytes 589832 | tf_op jit(solution)/shard_map/ppermute | solution.py:199
  74.2 12.2 %collective-permute-start.17 = (f32[4,1,12,8,128]{4,3,2,1,0:T(8,128)S(1)}, f32[4,1,12,8,128]{4,3,2,1,0:T(8,128)S(1)}, u32[]{:S(2)}, u32[]{:S(2)}) collective-permute-start(f32[4,1,12,8,128]{4,3,2,1,0:T(8,128)S(1)} %get-tuple-element.61), channel_id=1, source_target_pairs={{0,2},{1,3},{2,0},{3,1},{4,6},{5,7},{6,4},{7,5},{8,10},{9,11},{10,... | collective-permute-start | bytes 589832 | tf_op jit(solution)/shard_map/ppermute | solution.py:199
  79.6 8.8 %collective-permute-start.18 = (f32[4,1,12,8,128]{4,3,2,1,0:T(8,128)S(1)}, f32[4,1,12,8,128]{4,3,2,1,0:T(8,128)S(1)}, u32[]{:S(2)}, u32[]{:S(2)}) collective-permute-start(f32[4,1,12,8,128]{4,3,2,1,0:T(8,128)S(1)} %get-tuple-element.60), channel_id=1, source_target_pairs={{0,3},{1,2},{2,1},{3,0},{4,7},{5,6},{6,5},{7,4},{8,11},{9,10},{10,... | collective-permute-start | bytes 589832 | tf_op jit(solution)/shard_map/ppermute | solution.py:199
  88.7 8.6 %collective-permute-start.19 = (f32[1,4,12,8,128]{4,3,2,1,0:T(8,128)S(1)}, f32[1,4,12,8,128]{4,3,2,1,0:T(8,128)S(1)}, u32[]{:S(2)}, u32[]{:S(2)}) collective-permute-start(f32[1,4,12,8,128]{4,3,2,1,0:T(8,128)S(1)} %get-tuple-element.54), channel_id=1, source_target_pairs={{0,4},{4,0},{8,12},{12,8},{1,5},{5,1},{9,13},{13,9},{2,6},{6,2},{1... | collective-permute-start | bytes 589832 | tf_op jit(solution)/shard_map/ppermute | solution.py:199
  89.4 13.5 %collective-permute-start.26 = (f32[1,4,12,8,128]{4,3,2,1,0:T(8,128)S(1)}, f32[1,4,12,8,128]{4,3,2,1,0:T(8,128)S(1)}, u32[]{:S(2)}, u32[]{:S(2)}) collective-permute-start(f32[1,4,12,8,128]{4,3,2,1,0:T(8,128)S(1)} %get-tuple-element.53), channel_id=1, source_target_pairs={{0,8},{4,12},{8,0},{12,4},{1,9},{5,13},{9,1},{13,5},{2,10},{6,14},... | collective-permute-start | bytes 589832 | tf_op jit(solution)/shard_map/ppermute | solution.py:199
  90.6 12.2 %collective-permute-start.27 = (f32[1,4,12,8,128]{4,3,2,1,0:T(8,128)S(1)}, f32[1,4,12,8,128]{4,3,2,1,0:T(8,128)S(1)}, u32[]{:S(2)}, u32[]{:S(2)}) collective-permute-start(f32[1,4,12,8,128]{4,3,2,1,0:T(8,128)S(1)} %get-tuple-element.52), channel_id=1, source_target_pairs={{0,12},{4,8},{8,4},{12,0},{1,13},{5,9},{9,5},{13,1},{2,14},{6,10},... | collective-permute-start | bytes 589832 | tf_op jit(solution)/shard_map/ppermute | solution.py:199
  97.3 5.7 %collective-permute-start.23 = (f32[4,1,8,8,128]{4,3,2,1,0:T(8,128)S(1)}, f32[4,1,8,8,128]{4,3,2,1,0:T(8,128)S(1)}, u32[]{:S(2)}, u32[]{:S(2)}) collective-permute-start(f32[4,1,8,8,128]{4,3,2,1,0:T(8,128)S(1)} %get-tuple-element.84), channel_id=1, source_target_pairs={{0,1},{1,0},{2,3},{3,2},{4,5},{5,4},{6,7},{7,6},{8,9},{9,8},{10,11... | collective-permute-start | bytes 393224 | tf_op jit(solution)/shard_map/ppermute | solution.py:199
  97.4 6.6 %collective-permute-start.24 = (f32[4,1,8,8,128]{4,3,2,1,0:T(8,128)S(1)}, f32[4,1,8,8,128]{4,3,2,1,0:T(8,128)S(1)}, u32[]{:S(2)}, u32[]{:S(2)}) collective-permute-start(f32[4,1,8,8,128]{4,3,2,1,0:T(8,128)S(1)} %get-tuple-element.83), channel_id=1, source_target_pairs={{0,2},{1,3},{2,0},{3,1},{4,6},{5,7},{6,4},{7,5},{8,10},{9,11},{10,... | collective-permute-start | bytes 393224 | tf_op jit(solution)/shard_map/ppermute | solution.py:199
  98.7 6.7 %collective-permute-start.25 = (f32[4,1,8,8,128]{4,3,2,1,0:T(8,128)S(1)}, f32[4,1,8,8,128]{4,3,2,1,0:T(8,128)S(1)}, u32[]{:S(2)}, u32[]{:S(2)}) collective-permute-start(f32[4,1,8,8,128]{4,3,2,1,0:T(8,128)S(1)} %get-tuple-element.82), channel_id=1, source_target_pairs={{0,3},{1,2},{2,1},{3,0},{4,7},{5,6},{6,5},{7,4},{8,11},{9,10},{10,... | collective-permute-start | bytes 393224 | tf_op jit(solution)/shard_map/ppermute | solution.py:199

commit v4 on v3

v4 whole, which is shorter than its diff:
```python
import functools

import jax
import jax.numpy as jnp
from jax import lax
from jax.experimental import pallas as pl
from jax.experimental.pallas import tpu as pltpu
from jax.sharding import PartitionSpec as P

BLK = 128
OWN = 4
HALO = 4
PAIR = 2 * BLK
FIRST_OUT = 9
EVERY = ("row", "col", "depth")

BEFORE_ONLY = [(0, s) for s in range(4)] + [(1, s) for s in range(3)]
BOTH = [(0, 4), (1, 3), (1, 4), (2, 0), (2, 1), (3, 0)]
AFTER_ONLY = [(2, s) for s in range(2, 5)] + [(3, s) for s in range(1, 5)]
EARLY_SIDE = 1
INNER = BEFORE_ONLY[7 - EARLY_SIDE :] + BOTH + AFTER_ONLY[:EARLY_SIDE]
OUTER = BEFORE_ONLY[: 7 - EARLY_SIDE] + AFTER_ONLY[EARLY_SIDE:]
INNER_TO_BEFORE, INNER_TO_AFTER = slice(0, 6 + EARLY_SIDE), slice(EARLY_SIDE, 6 + 2 * EARLY_SIDE)
OUTER_TO_BEFORE, OUTER_TO_AFTER = slice(0, 7 - EARLY_SIDE), slice(7 - EARLY_SIDE, 14 - 2 * EARLY_SIDE)


def ranks(row, col, depth):
    core, z_half = row & 1, (row >> 1) & 1
    return col ^ (3 * (core ^ z_half)), depth ^ (3 * core)


def place():
    return tuple(lax.axis_index(axis) for axis in EVERY)


def pack_kernel(last_row, density, mask, *outs):
    row, col, depth = place()
    col_rank, depth_rank = ranks(row, col, depth)

    def weight(rank, block_row, slot):
        value = mask[slot, rank * OWN + block_row].astype(jnp.float32)
        if block_row + slot < 2:
            value = jnp.where((row == 0) & (rank == 0), 0.0, value)
        if block_row + slot > OWN + 1:
            value = jnp.where((row == last_row) & (rank == 15), 0.0, value)
        return value

    for k in range(4):
        for other in range(4):
            rank = (col_rank ^ k) * 4 + other
            for index, (block_row, slot) in enumerate(INNER):
                outs[k][0, other, index] = density[rank * OWN + block_row, slot] * weight(rank, block_row, slot)
            rank = other * 4 + (depth_rank ^ k)
            for index, (block_row, slot) in enumerate(OUTER):
                outs[4 + k][other, 0, index] = density[rank * OWN + block_row, slot] * weight(rank, block_row, slot)


def pack(density, mask):
    vmem = pl.BlockSpec(memory_space=pltpu.VMEM)
    smem = pl.BlockSpec(memory_space=pltpu.SMEM)
    inner = jax.ShapeDtypeStruct((1, 4, len(INNER), 8, BLK), jnp.float32)
    outer = jax.ShapeDtypeStruct((4, 1, len(OUTER), 8, BLK), jnp.float32)
    outs = pl.pallas_call(
        functools.partial(pack_kernel, lax.axis_size("row") - 1),
        out_shape=[inner] * 4 + [outer] * 4,
        in_specs=[vmem, smem],
        out_specs=[vmem] * 8,
        compiler_params=pltpu.CompilerParams(vmem_limit_bytes=16 * 1024 * 1024),
        cost_estimate=pl.CostEstimate(flops=10**6, bytes_accessed=4 * 1024 * 1024, transcendentals=0),
    )(density, mask)
    return list(outs[:4]), list(outs[4:])


EARLY_AFTER = [(row + OWN, slot) for row, slot in INNER[INNER_TO_BEFORE]]
EARLY_BEFORE = [(row - OWN, slot) for row, slot in INNER[INNER_TO_AFTER]]
LATE_AFTER = [(row + OWN, slot) for row, slot in OUTER[OUTER_TO_BEFORE]]
LATE_BEFORE = [(row - OWN, slot) for row, slot in OUTER[OUTER_TO_AFTER]]
TILES = [(0, 1), (5, 4)] + [(pair, column) for pair in range(1, 5) for column in range(pair - 1, pair + 2)]
MINE = (2, 3)


def at(row, slot):
    return row + 4, row + slot + 2


def split_block(value):
    rounded = value.astype(jnp.bfloat16)
    return rounded, (value - rounded.astype(jnp.float32)).astype(jnp.bfloat16)


def put_block(row, column, parts, high, low):
    rows, columns = slice(row * BLK, (row + 1) * BLK), slice(column * BLK, (column + 1) * BLK)
    high[rows, columns], low[rows, columns] = parts


def product(left_high, left_low, right_high, right_low):
    def dot(a, b):
        return jnp.dot(a, b, preferred_element_type=jnp.float32)

    return dot(left_high, right_high) + (dot(left_high, right_low) + dot(left_low, right_high))


def tile(first, end):
    return slice(first * PAIR, end * PAIR)


def early_kernel(outer, inner, inner_after, inner_before, high, low, square):
    there = set()
    for source, blocks in ((outer, OUTER), (inner, INNER), (inner_after, EARLY_AFTER), (inner_before, EARLY_BEFORE)):
        for index, block in enumerate(blocks):
            put_block(*at(*block), split_block(source[:, index].reshape(BLK, BLK)), high, low)
            there.add(at(*block))
    zero = jnp.zeros((BLK, BLK), jnp.bfloat16)
    for pair, outside in TILES:
        for row in (2 * pair, 2 * pair + 1):
            for column in (2 * outside, 2 * outside + 1):
                if (row, column) not in there:
                    put_block(row, column, (zero, zero), high, low)
    for pair in MINE:
        mine = tile(pair, pair + 1)
        for column in range(pair - 2, pair + 3):
            inside, outside = tile(max(pair, column) - 1, min(pair, column) + 2), tile(column, column + 1)
            square[pair - MINE[0], :, tile(column - pair + 2, column - pair + 3)] = product(
                high[mine, inside], low[mine, inside], high[inside, outside], low[inside, outside]
            )


def early_part(*operands):
    vmem = pl.BlockSpec(memory_space=pltpu.VMEM)
    window = 12 * BLK
    part = jax.ShapeDtypeStruct((window, window), jnp.bfloat16)
    return pl.pallas_call(
        early_kernel,
        out_shape=(part, part, jax.ShapeDtypeStruct((2, PAIR, 5 * PAIR), jnp.float32)),
        in_specs=[vmem] * 4,
        out_specs=(vmem, vmem, vmem),
        compiler_params=pltpu.CompilerParams(vmem_limit_bytes=24 * 1024 * 1024),
        cost_estimate=pl.CostEstimate(flops=2 * 3 * 18 * PAIR**3, bytes_accessed=16 * 1024 * 1024, transcendentals=0),
    )(*operands)


def late_kernel(after, before, high_in, low_in, square, square_mask, out_mask, *refs):
    *outs, high, low, late_high, late_low, square_high, square_low = refs
    col_rank, depth_rank = ranks(*place())
    first = (col_rank * 4 + depth_rank) * OWN
    late = {}
    for side, (source, blocks) in enumerate(((before, LATE_BEFORE), (after, LATE_AFTER))):
        there = set()
        pair = 1 + 3 * side
        for index, block in enumerate(blocks):
            row, column = at(*block)
            parts = split_block(source[:, index].reshape(BLK, BLK))
            put_block(row, column, parts, high, low)
            put_block(2 * side + row - 2 * pair, column - 2 * pair + 2, parts, late_high, late_low)
            there.add((row, column))
        zero = jnp.zeros((BLK, BLK), jnp.bfloat16)
        late[pair + 1 - 2 * side] = (pair, side, {column // 2 for _, column in there})
        for row in (2 * pair, 2 * pair + 1):
            for column in range(2 * pair - 2, 2 * pair + 4):
                if (row, column) not in there:
                    put_block(2 * side + row - 2 * pair, column - 2 * pair + 2, (zero, zero), late_high, late_low)
    for pair in MINE:
        mine = tile(pair, pair + 1)
        kept = {}
        source, side, touched = late[pair]
        for column in range(pair - 2, pair + 3):
            value = square[pair - MINE[0], :, tile(column - pair + 2, column - pair + 3)]
            if column in touched:
                inside, rows, outside = tile(source, source + 1), tile(side, side + 1), tile(column - source + 1, column - source + 2)
                value += product(high[mine, inside], low[mine, inside], late_high[rows, outside], late_low[rows, outside])
            for half in range(2):
                for part in range(2):
                    slot = 2 * (column - pair) + part - half + 4
                    block = value[half * BLK : (half + 1) * BLK, part * BLK : (part + 1) * BLK]
                    row = 2 * (pair - MINE[0]) + half
                    if 0 <= slot < 9:
                        block = block * square_mask[slot, first + row].astype(jnp.float32)
                    if 2 <= slot < 7:
                        kept[half, slot - 2] = block
                    put_block(half, 2 * column + part, split_block(block), square_high, square_low)
        for column in range(pair - 1, pair + 2):
            inside, outside = tile(column - 1, column + 2), tile(column, column + 1)
            cube = product(square_high[:, inside], square_low[:, inside], high[inside, outside], low[inside, outside])
            for half in range(2):
                for part in range(2):
                    slot = 2 * (column - pair) + part - half + 2
                    row = 2 * (pair - MINE[0]) + half
                    if 0 <= slot < 5:
                        block = cube[half * BLK : (half + 1) * BLK, part * BLK : (part + 1) * BLK]
                        gate = out_mask[slot, first + row].astype(jnp.float32)
                        value = (gate * (3.0 * kept[half, slot] - 2.0 * block)).reshape(16, 8, BLK)
                        index = row * 5 + slot
                        if index < FIRST_OUT:
                            outs[0][:, index] = value
                        else:
                            outs[1][:, index - FIRST_OUT] = value


def late_part(*operands):
    vmem = pl.BlockSpec(memory_space=pltpu.VMEM)
    smem = pl.BlockSpec(memory_space=pltpu.SMEM)
    window = 12 * BLK
    part = jax.ShapeDtypeStruct((window, window), jnp.bfloat16)
    return pl.pallas_call(
        late_kernel,
        out_shape=[jax.ShapeDtypeStruct((16, count, 8, BLK), jnp.float32) for count in (FIRST_OUT, 20 - FIRST_OUT)] + [part] * 2,
        in_specs=[vmem] * 5 + [smem] * 2,
        out_specs=[vmem] * 4,
        scratch_shapes=[pltpu.VMEM((2 * PAIR, 3 * PAIR), jnp.bfloat16)] * 2 + [pltpu.VMEM((PAIR, window), jnp.bfloat16)] * 2,
        input_output_aliases={2: 2, 3: 3},
        compiler_params=pltpu.CompilerParams(vmem_limit_bytes=24 * 1024 * 1024),
        cost_estimate=pl.CostEstimate(flops=2 * 3 * 22 * PAIR**3, bytes_accessed=4 * 1024 * 1024, transcendentals=0),
    )(*operands)[:2]


def send(pieces, axis):
    size = lax.axis_size(axis)
    return pieces[:1] + [lax.ppermute(pieces[k], axis, [(i, i ^ k) for i in range(size)]) for k in range(1, size)]


def cut(value, dim, far):
    return [lax.dynamic_slice_in_dim(value, far ^ k, 1, dim) for k in range(value.shape[dim])]


def join(pieces, dim, near):
    stack = jnp.concatenate(pieces[::-1], axis=dim)
    last = len(pieces) - 1
    return jnp.concatenate([lax.dynamic_slice_in_dim(stack, near ^ j ^ last, 1, dim) for j in range(len(pieces))], axis=dim)


def swap(value, axis, dim, near, far):
    return join(send(cut(value, dim, far), axis), dim, near)


def chain(rows):
    places = [(row, col, depth) for row in range(rows) for col in range(4) for depth in range(4)]
    places.sort(key=lambda at: (at[0], *ranks(*at)))
    return [row * 16 + col * 4 + depth for row, col, depth in places]


def on_device(density, mask_band, mask_square, mask_out):
    row, col, depth = place()
    col_rank, depth_rank = ranks(row, col, depth)
    order = chain(lax.axis_size("row"))
    up = list(zip(order[:-1], order[1:]))
    down = list(zip(order[1:], order[:-1]))

    def halo(group, before_part, after_part):
        after = lax.ppermute(group[:, before_part], EVERY, down)
        before = lax.ppermute(group[:, after_part], EVERY, up)
        return after, before

    inner, outer = pack(density, mask_band.T)
    inner = join(send(inner, "col"), 0, col)
    outer = join(send(outer, "depth"), 1, depth)
    outer = swap(outer, "col", 0, col, col_rank)
    inner = swap(inner, "depth", 1, depth, depth_rank)
    inner = inner.reshape(16, len(INNER), 8, BLK)
    outer = outer.reshape(16, len(OUTER), 8, BLK)
    early = early_part(outer, inner, *halo(inner, INNER_TO_BEFORE, INNER_TO_AFTER))
    late = halo(outer, OUTER_TO_BEFORE, OUTER_TO_AFTER)
    lower, upper = late_part(*late, *early, mask_square.T, mask_out.T)
    lower = lower.reshape(4, 4, FIRST_OUT, 8, BLK)
    upper = upper.reshape(4, 4, 20 - FIRST_OUT, 8, BLK)
    lower = swap(lower, "col", 0, col_rank, col)
    upper = swap(upper, "depth", 1, depth_rank, depth)
    upper = send(cut(upper, 0, col), "col")
    upper[1], lower = lax.optimization_barrier((upper[1], lower))
    upper = join(upper, 0, col_rank)
    lower = swap(lower, "depth", 1, depth_rank, depth)
    return jnp.concatenate([lower, upper], axis=2).reshape(density.shape)


def solution(mesh):
    return jax.shard_map(
        on_device,
        mesh=mesh,
        in_specs=(
            P("row", None, ("col", "depth"), None),
            P("row", None),
            P("row", None),
            P("row", None),
        ),
        out_specs=P("row", None, ("col", "depth"), None),
        check_vma=False,
    )
```

time: 107 us -> 104 us (0.972)
  starting transfers between devices: 53.2 us -> 49.4 us
  local copies, waits for them, and re-layouts: 3.01 us -> 4.73 us
    ppermute x24, starting transfers between devices: 41.5 us -> 33.9 us  [send(): lax.ppermute(pieces[k], axis, [(i, i ^ k) for i in range(size)])]
    ppermute x2, starting transfers between devices: 3.84 us -> 10 us  [halo(): after = lax.ppermute(group[:, before_part], EVERY, down)]
    ppermute x2, starting transfers between devices: 7.84 us -> 5.49 us  [halo(): before = lax.ppermute(group[:, after_part], EVERY, up)]
    ppermute x2, waiting for transfers between devices: 2.97 us -> 1.24 us  [halo(): before = lax.ppermute(group[:, after_part], EVERY, up)]
    slice x2, local copies, waits for them, and re-layouts: 0.11 us -> 1.78 us  [halo(): before = lax.ppermute(group[:, after_part], EVERY, up)]
    ppermute x24, waiting for transfers between devices: 32.2 us -> 33.8 us  [send(): lax.ppermute(pieces[k], axis, [(i, i ^ k) for i in range(size)])]
    pallas_call x3 -> x2, Pallas kernels: 6.71 us -> 5.95 us  [the longest x1 3.7 us: late_part(): pl.pallas_call(late_kernel, out_shape=[jax.ShapeDtypeStruct((16, count, 8...]
  transfers between devices with their start and end apart: 28 -> 28, of which waited for: 12 -> 13; matrix products, arithmetic and copies ran while one was open for 1% -> 3% of each run, Pallas kernels for 3% -> 2%
where the time goes in v4:
time: 104 us; the launch traced here: 103 us
  starting transfers between devices  49.4 us (48%)
  waiting for transfers between devices  39.4 us (38%)
  Pallas kernels  7.04 us (7%)
  local copies, waits for them, and re-layouts  4.73 us (5%)
  other arithmetic  1.74 us (2%)
    ppermute x24, starting transfers between devices, send(): lax.ppermute(pieces[k], axis, [(i, i ^ k) for i in range(size)])  33.9 us
    ppermute x24, waiting for transfers between devices, send(): lax.ppermute(pieces[k], axis, [(i, i ^ k) for i in range(size)])  33.8 us
    ppermute x2, starting transfers between devices, halo(): after = lax.ppermute(group[:, before_part], EVERY, down)  10 us
    ppermute x2, starting transfers between devices, halo(): before = lax.ppermute(group[:, after_part], EVERY, up)  5.49 us
    ppermute x2, waiting for transfers between devices, halo(): after = lax.ppermute(group[:, before_part], EVERY, down)  4.41 us
    pallas_call x1, Pallas kernels, late_part(): pl.pallas_call(late_kernel, out_shape=[jax.ShapeDtypeStruct((16, count, 8...  3.7 us
    pallas_call x1, Pallas kernels, early_part(): pl.pallas_call(early_kernel, out_shape=(part, part, jax.ShapeDtypeStruct(...  2.25 us
    unnamed x14, local copies, waits for them, and re-layouts  2.09 us
  transfers between devices with their start and end apart: 28, of which 13 were waited for; matrix products, arithmetic and copies ran while one was open for 3% of the time, Pallas kernels for 2%

profile of v4, /device:TPU:2, one launch (start us, length us, event | category | flops | bytes accessed | tf_op | source)
XLA Modules:
  0.0 102.8 jit_solution(16008436476641968692)
XLA Ops:
  0.0 1.3 %copy-done = f32[64,5,8,128]{3,2,1,0:T(8,128)S(1)} copy-done((f32[64,5,8,128]{3,2,1,0:T(8,128)S(1)}, f32[64,5,8,128]{3,2,1,0:T(8,128)}, u32[]{:S(2)}) %copy-start) | copy-done | bytes 1310744
  1.3 0.7 copy-done.3
  2.0 1.1 %shard_map.46 = (f32[1,4,8,8,128]{4,3,2,1,0:T(8,128)S(1)}, f32[1,4,8,8,128]{4,3,2,1,0:T(8,128)S(1)}, f32[1,4,8,8,128]{4,3,2,1,0:T(8,128)S(1)}, f32[1,4,8,8,128]{...) custom-call(f32[64,5,8,128]{3,2,1,0:T(8,128)S(1)} %copy-done, ...), custom_call_target="tpu_custom_call" | custom-call | flops 1000000 | bytes 4194304 | tf_op jit(solution)/shard_map/pallas_call | solution.py:63
  3.1 4.7 %collective-permute-start.8 = (f32[1,4,8,8,128]{4,3,2,1,0:T(8,128)S(1)}, f32[1,4,8,8,128]{4,3,2,1,0:T(8,128)S(1)}, u32[]{:S(2)}, u32[]{:S(2)}) collective-permute-start(f32[1,4,8,8,128]{4,3,2,1,0:T(8,128)S(1)} %get-tuple-element.24), channel_id=1, source_target_pairs={{0,12},{4,8},{8,4},{12,0},{1,13},{5,9},{9,5},{13,1},{2,14},{6,10},... | collective-permute-start | bytes 393224 | tf_op jit(solution)/shard_map/ppermute | solution.py:218
  7.8 0.7 collective-permute-start.10
  8.5 3.0 %collective-permute-start = (f32[4,1,12,8,128]{4,3,2,1,0:T(8,128)S(1)}, f32[4,1,12,8,128]{4,3,2,1,0:T(8,128)S(1)}, u32[]{:S(2)}, u32[]{:S(2)}) collective-permute-start(f32[4,1,12,8,128]{4,3,2,1,0:T(8,128)S(1)} %get-tuple-element.20), channel_id=1, source_target_pairs={{0,3},{1,2},{2,1},{3,0},{4,7},{5,6},{6,5},{7,4},{8,11},{9,10},{10,... | collective-permute-start | bytes 589832 | tf_op jit(solution)/shard_map/ppermute | solution.py:218
  11.5 0.6 collective-permute-start.1
  12.1 0.1 collective-permute-done.8
  12.2 1.6 %collective-permute-start.2 = (f32[4,1,12,8,128]{4,3,2,1,0:T(8,128)S(1)}, f32[4,1,12,8,128]{4,3,2,1,0:T(8,128)S(1)}, u32[]{:S(2)}, u32[]{:S(2)}) collective-permute-start(f32[4,1,12,8,128]{4,3,2,1,0:T(8,128)S(1)} %get-tuple-element.22), channel_id=1, source_target_pairs={{0,1},{1,0},{2,3},{3,2},{4,5},{5,4},{6,7},{7,6},{8,9},{9,8},{10,11... | collective-permute-start | bytes 589832 | tf_op jit(solution)/shard_map/ppermute | solution.py:218
  13.8 4.6 %collective-permute-done.9 = f32[1,4,8,8,128]{4,3,2,1,0:T(8,128)S(1)} collective-permute-done((f32[1,4,8,8,128]{4,3,2,1,0:T(8,128)S(1)}, f32[1,4,8,8,128]{4,3,2,1,0:T(8,128)S(1)}, u32[]{:S(2)}, u32[]{:S(2)}) %collective-permute-start.9) | collective-permute-done | bytes 131104 | tf_op jit(solution)/shard_map/ppermute | solution.py:218
  18.6 3.1 %collective-permute-start.11 = (f32[4,1,8,8,128]{4,3,2,1,0:T(8,128)S(1)}, f32[4,1,8,8,128]{4,3,2,1,0:T(8,128)S(1)}, u32[]{:S(2)}, u32[]{:S(2)}) collective-permute-start(f32[4,1,8,8,128]{4,3,2,1,0:T(8,128)S(1)} %get-tuple-element.87), channel_id=1, source_target_pairs={{0,3},{1,2},{2,1},{3,0},{4,7},{5,6},{6,5},{7,4},{8,11},{9,10},{10,... | collective-permute-start | bytes 393224 | tf_op jit(solution)/shard_map/ppermute | solution.py:218
  21.7 0.1 collective-permute-start.13
  21.9 1.5 %collective-permute-start.12 = (f32[4,1,8,8,128]{4,3,2,1,0:T(8,128)S(1)}, f32[4,1,8,8,128]{4,3,2,1,0:T(8,128)S(1)}, u32[]{:S(2)}, u32[]{:S(2)}) collective-permute-start(f32[4,1,8,8,128]{4,3,2,1,0:T(8,128)S(1)} %get-tuple-element.90), channel_id=1, source_target_pairs={{0,2},{1,3},{2,0},{3,1},{4,6},{5,7},{6,4},{7,5},{8,10},{9,11},{10,... | collective-permute-start | bytes 393224 | tf_op jit(solution)/shard_map/ppermute | solution.py:218
  23.7 2.7 %collective-permute-start.3 = (f32[1,4,12,8,128]{4,3,2,1,0:T(8,128)S(1)}, f32[1,4,12,8,128]{4,3,2,1,0:T(8,128)S(1)}, u32[]{:S(2)}, u32[]{:S(2)}) collective-permute-start(f32[1,4,12,8,128]{4,3,2,1,0:T(8,128)S(1)} %get-tuple-element.41), channel_id=1, source_target_pairs={{0,12},{4,8},{8,4},{12,0},{1,13},{5,9},{9,5},{13,1},{2,14},{6,10},... | collective-permute-start | bytes 589832 | tf_op jit(solution)/shard_map/ppermute | solution.py:218
  26.5 1.7 %collective-permute-start.4 = (f32[1,4,12,8,128]{4,3,2,1,0:T(8,128)S(1)}, f32[1,4,12,8,128]{4,3,2,1,0:T(8,128)S(1)}, u32[]{:S(2)}, u32[]{:S(2)}) collective-permute-start(f32[1,4,12,8,128]{4,3,2,1,0:T(8,128)S(1)} %get-tuple-element.44), channel_id=1, source_target_pairs={{0,8},{4,12},{8,0},{12,4},{1,9},{5,13},{9,1},{13,5},{2,10},{6,14},... | collective-permute-start | bytes 589832 | tf_op jit(solution)/shard_map/ppermute | solution.py:218
  28.2 0.7 collective-permute-done.12
  29.1 0.8 fusion.1
  29.9 3.2 %collective-permute-start.15 = (f32[16,7,8,128]{3,2,1,0:T(8,128)}, f32[16,7,8,128]{3,2,1,0:T(8,128)S(1)}, u32[]{:S(2)}, u32[]{:S(2)}) collective-permute-start(f32[16,7,8,128]{3,2,1,0:T(8,128)} %get-tuple-element.81), channel_id=1, source_target_pairs={{0,1},{1,2},{2,3},{3,4},{4,5},{5,6},{6,7},{7,8},{8,9},{9,10},{10,1... | collective-permute-start | bytes 1376264 | tf_op jit(solution)/shard_map/ppermute | solution.py:250
  33.1 4.5 %collective-permute-start.14 = (f32[16,7,8,128]{3,2,1,0:T(8,128)S(1)}, f32[16,7,8,128]{3,2,1,0:T(8,128)S(1)}, u32[]{:S(2)}, u32[]{:S(2)}) collective-permute-start(f32[16,7,8,128]{3,2,1,0:T(8,128)S(1)} %get-tuple-element.82), channel_id=1, source_target_pairs={{1,0},{2,1},{3,2},{4,3},{5,4},{6,5},{7,6},{8,7},{9,8},{10,9},{11,1... | collective-permute-start | bytes 1376264 | tf_op jit(solution)/shard_map/ppermute | solution.py:249
  37.6 0.5 collective-permute-done.5
  38.1 5.4 %collective-permute-done.4 = f32[1,4,12,8,128]{4,3,2,1,0:T(8,128)S(1)} collective-permute-done((f32[1,4,12,8,128]{4,3,2,1,0:T(8,128)S(1)}, f32[1,4,12,8,128]{4,3,2,1,0:T(8,128)S(1)}, u32[]{:S(2)}, u32[]{:S(2)}) %collective-permute-start.4) | collective-permute-done | bytes 196640 | tf_op jit(solution)/shard_map/ppermute | solution.py:218
  43.7 1.0 fusion
  44.6 2.3 %collective-permute-start.7 = (f32[16,6,8,128]{3,2,1,0:T(8,128)}, f32[16,6,8,128]{3,2,1,0:T(8,128)S(1)}, u32[]{:S(2)}, u32[]{:S(2)}) collective-permute-start(f32[16,6,8,128]{3,2,1,0:T(8,128)} %get-tuple-element.35), channel_id=1, source_target_pairs={{0,1},{1,2},{2,3},{3,4},{4,5},{5,6},{6,7},{7,8},{8,9},{9,10},{10,1... | collective-permute-start | bytes 1179656 | tf_op jit(solution)/shard_map/ppermute | solution.py:250
  46.9 5.5 %collective-permute-start.6 = (f32[16,6,8,128]{3,2,1,0:T(8,128)}, f32[16,6,8,128]{3,2,1,0:T(8,128)S(1)}, u32[]{:S(2)}, u32[]{:S(2)}) collective-permute-start(f32[16,6,8,128]{3,2,1,0:T(8,128)} %get-tuple-element.36), channel_id=1, source_target_pairs={{1,0},{2,1},{3,2},{4,3},{5,4},{6,5},{7,6},{8,7},{9,8},{10,9},{11,1... | collective-permute-start | bytes 1179656 | tf_op jit(solution)/shard_map/ppermute | solution.py:249
  52.6 2.2 %shard_map.47 = (bf16[1536,1536]{1,0:T(8,128)(2,1)S(1)}, bf16[1536,1536]{1,0:T(8,128)(2,1)S(1)}, f32[2,256,1280]{2,1,0:T(8,128)S(1)}) custom-call(f32[16,12,8,128]{3,2,1,0:T(8,128)S(1)} %bitcast.11, f32[16,8,8,128]{3,2,1,0:T(8,128)S(1)} %bitcast.9, f32[16,7,8,128]{3,2,1,0:T(8,128)S(1)} %collective-permute-done.14.inner_after, ...), custom_call_target="tpu_custom_call" | custom-call | flops 1811939328 | bytes 16777216 | tf_op jit(solution)/shard_map/pallas_call | solution.py:132
  54.8 1.2 %collective-permute-done.7.before = f32[16,6,8,128]{3,2,1,0:T(8,128)S(1)} collective-permute-done((f32[16,6,8,128]{3,2,1,0:T(8,128)}, f32[16,6,8,128]{3,2,1,0:T(8,128)S(1)}, u32[]{:S(2)}, u32[]{:S(2)}) %collective-permute-start.7) | collective-permute-done | bytes 393248 | tf_op jit(solution)/shard_map/ppermute | solution.py:250
  56.0 4.4 %collective-permute-done.6.after = f32[16,6,8,128]{3,2,1,0:T(8,128)S(1)} collective-permute-done((f32[16,6,8,128]{3,2,1,0:T(8,128)}, f32[16,6,8,128]{3,2,1,0:T(8,128)S(1)}, u32[]{:S(2)}, u32[]{:S(2)}) %collective-permute-start.6) | collective-permute-done | bytes 393248 | tf_op jit(solution)/shard_map/ppermute | solution.py:249
  60.5 3.7 %shard_map.48 = (f32[16,9,8,128]{3,2,1,0:T(8,128)S(1)}, f32[16,11,8,128]{3,2,1,0:T(8,128)S(1)}, bf16[1536,1536]{1,0:T(8,128)(2,1)S(1)}, bf16[1536,1536]{1,0:T(8,128)(2,1)S(1)}) custom-call(f32[16,6,8,128]{3,2,1,0:T(8,128)S(1)} %collective-permute-done.6.after, ...), custom_call_target="tpu_custom_call", output_to_operand_aliasing={{2}: (2, {}), {3}: (3, {})} | custom-call | flops 2214592512 | bytes 4194304 | tf_op jit(solution)/shard_map/pallas_call | solution.py:204
  64.2 1.0 collective-permute-start.20
  65.2 2.8 %collective-permute-start.22 = (f32[1,4,9,8,128]{4,3,2,1,0:T(8,128)S(1)}, f32[1,4,9,8,128]{4,3,2,1,0:T(8,128)S(1)}, u32[]{:S(2)}, u32[]{:S(2)}) collective-permute-start(f32[1,4,9,8,128]{4,3,2,1,0:T(8,128)S(1)} %get-tuple-element.79), channel_id=1, source_target_pairs={{0,4},{4,0},{8,12},{12,8},{1,5},{5,1},{9,13},{13,9},{2,6},{6,2},{1... | collective-permute-start | bytes 442376 | tf_op jit(solution)/shard_map/ppermute | solution.py:218
  68.0 0.7 collective-permute-start.21
  68.8 0.1 collective-permute-start.16
  68.9 0.1 collective-permute-start.18
  69.0 3.6 %collective-permute-done.20 = f32[1,4,9,8,128]{4,3,2,1,0:T(8,128)S(1)} collective-permute-done((f32[1,4,9,8,128]{4,3,2,1,0:T(8,128)S(1)}, f32[1,4,9,8,128]{4,3,2,1,0:T(8,128)S(1)}, u32[]{:S(2)}, u32[]{:S(2)}) %collective-permute-start.20) | collective-permute-done | bytes 147488 | tf_op jit(solution)/shard_map/ppermute | solution.py:218
  72.6 0.9 collective-permute-start.17
  73.6 3.6 %collective-permute-done.22 = f32[1,4,9,8,128]{4,3,2,1,0:T(8,128)S(1)} collective-permute-done((f32[1,4,9,8,128]{4,3,2,1,0:T(8,128)S(1)}, f32[1,4,9,8,128]{4,3,2,1,0:T(8,128)S(1)}, u32[]{:S(2)}, u32[]{:S(2)}) %collective-permute-start.22) | collective-permute-done | bytes 147488 | tf_op jit(solution)/shard_map/ppermute | solution.py:218
  77.2 2.9 %collective-permute-done.21 = f32[1,4,9,8,128]{4,3,2,1,0:T(8,128)S(1)} collective-permute-done((f32[1,4,9,8,128]{4,3,2,1,0:T(8,128)S(1)}, f32[1,4,9,8,128]{4,3,2,1,0:T(8,128)S(1)}, u32[]{:S(2)}, u32[]{:S(2)}) %collective-permute-start.21) | collective-permute-done | bytes 147488 | tf_op jit(solution)/shard_map/ppermute | solution.py:218
  80.1 2.0 %collective-permute-done.17 = f32[4,1,11,8,128]{4,3,2,1,0:T(8,128)S(1)} collective-permute-done((f32[4,1,11,8,128]{4,3,2,1,0:T(8,128)S(1)}, f32[4,1,11,8,128]{4,3,2,1,0:T(8,128)S(1)}, u32[]{:S(2)}, u32[]{:S(2)}) %collective-permute-start.17) | collective-permute-done | bytes 180256 | tf_op jit(solution)/shard_map/ppermute | solution.py:218
  82.2 0.1 constant_dynamic-slice_fusion.27
  82.4 0.4 collective-permute-start.19
  82.8 2.0 %collective-permute-start.26 = (f32[1,4,11,8,128]{4,3,2,1,0:T(8,128)S(1)}, f32[1,4,11,8,128]{4,3,2,1,0:T(8,128)S(1)}, u32[]{:S(2)}, u32[]{:S(2)}) collective-permute-start(f32[1,4,11,8,128]{4,3,2,1,0:T(8,128)S(1)} %get-tuple-element.53), channel_id=1, source_target_pairs={{0,12},{4,8},{8,4},{12,0},{1,13},{5,9},{9,5},{13,1},{2,14},{6,10},... | collective-permute-start | bytes 540680 | tf_op jit(solution)/shard_map/ppermute | solution.py:218
  84.8 1.3 %collective-permute-start.27 = (f32[1,4,11,8,128]{4,3,2,1,0:T(8,128)S(1)}, f32[1,4,11,8,128]{4,3,2,1,0:T(8,128)S(1)}, u32[]{:S(2)}, u32[]{:S(2)}) collective-permute-start(f32[1,4,11,8,128]{4,3,2,1,0:T(8,128)S(1)} %get-tuple-element.55), channel_id=1, source_target_pairs={{0,8},{4,12},{8,0},{12,4},{1,9},{5,13},{9,1},{13,5},{2,10},{6,14},... | collective-permute-start | bytes 540680 | tf_op jit(solution)/shard_map/ppermute | solution.py:218
  86.2 4.6 %collective-permute-done.19 = f32[1,4,11,8,128]{4,3,2,1,0:T(8,128)S(1)} collective-permute-done((f32[1,4,11,8,128]{4,3,2,1,0:T(8,128)S(1)}, f32[1,4,11,8,128]{4,3,2,1,0:T(8,128)S(1)}, u32[]{:S(2)}, u32[]{:S(2)}) %collective-permute-start.19) | collective-permute-done | bytes 180256 | tf_op jit(solution)/shard_map/ppermute | solution.py:218
  90.9 0.4 collective-permute-start.23
  91.2 1.3 %collective-permute-start.25 = (f32[4,1,9,8,128]{4,3,2,1,0:T(8,128)S(1)}, f32[4,1,9,8,128]{4,3,2,1,0:T(8,128)S(1)}, u32[]{:S(2)}, u32[]{:S(2)}) collective-permute-start(f32[4,1,9,8,128]{4,3,2,1,0:T(8,128)S(1)} %get-tuple-element.71), channel_id=1, source_target_pairs={{0,1},{1,0},{2,3},{3,2},{4,5},{5,4},{6,7},{7,6},{8,9},{9,8},{10,11... | collective-permute-start | bytes 442376 | tf_op jit(solution)/shard_map/ppermute | solution.py:218
  92.6 3.1 %collective-permute-start.24 = (f32[4,1,9,8,128]{4,3,2,1,0:T(8,128)S(1)}, f32[4,1,9,8,128]{4,3,2,1,0:T(8,128)S(1)}, u32[]{:S(2)}, u32[]{:S(2)}) collective-permute-start(f32[4,1,9,8,128]{4,3,2,1,0:T(8,128)S(1)} %get-tuple-element.72), channel_id=1, source_target_pairs={{0,2},{1,3},{2,0},{3,1},{4,6},{5,7},{6,4},{7,5},{8,10},{9,11},{10,... | collective-permute-start | bytes 442376 | tf_op jit(solution)/shard_map/ppermute | solution.py:218
  95.7 5.6 %collective-permute-done.27 = f32[1,4,11,8,128]{4,3,2,1,0:T(8,128)S(1)} collective-permute-done((f32[1,4,11,8,128]{4,3,2,1,0:T(8,128)S(1)}, f32[1,4,11,8,128]{4,3,2,1,0:T(8,128)S(1)}, u32[]{:S(2)}, u32[]{:S(2)}) %collective-permute-start.27) | collective-permute-done | bytes 180256 | tf_op jit(solution)/shard_map/ppermute | solution.py:218
  101.6 1.2 %maximum_maximum_fusion = f32[4,4,20,8,128]{4,3,2,1,0:T(8,128)} fusion(f32[1,4,11,8,128]{4,3,2,1,0:T(8,128)S(1)} %get-tuple-element.50, f32[1,4,11,8,128]{4,3,2,1,0:T(8,128)S(1)} %get-tuple-element.51, f32[1,4,11,8,128]{4,3,2,1,0:T(8,128)S(1)} %get-tuple-element.52, f32[1,4,11,8,128]{4,3,2,1,0:T(8,128)S(1)} %get-tuple-element.49, ...), kind=kLoop, calls=%fused_computation | loop fusion | flops 2293760 | bytes 2621440 | tf_op jit(solution)/shard_map/concatenate | solution.py:271
  (56 shorter events, 1.5 us)
Async XLA Ops:
  0.0 1.3 %copy-start = (f32[64,5,8,128]{3,2,1,0:T(8,128)S(1)}, f32[64,5,8,128]{3,2,1,0:T(8,128)}, u32[]{:S(2)}) copy-start(f32[64,5,8,128]{3,2,1,0:T(8,128)} %density.1) | copy-start | bytes 3932164
  1.3 0.7 copy-start.3
  3.1 9.1 %collective-permute-start.8 = (f32[1,4,8,8,128]{4,3,2,1,0:T(8,128)S(1)}, f32[1,4,8,8,128]{4,3,2,1,0:T(8,128)S(1)}, u32[]{:S(2)}, u32[]{:S(2)}) collective-permute-start(f32[1,4,8,8,128]{4,3,2,1,0:T(8,128)S(1)} %get-tuple-element.24), channel_id=1, source_target_pairs={{0,12},{4,8},{8,4},{12,0},{1,13},{5,9},{9,5},{13,1},{2,14},{6,10},... | collective-permute-start | bytes 393224 | tf_op jit(solution)/shard_map/ppermute | solution.py:218
  7.8 10.6 %collective-permute-start.9 = (f32[1,4,8,8,128]{4,3,2,1,0:T(8,128)S(1)}, f32[1,4,8,8,128]{4,3,2,1,0:T(8,128)S(1)}, u32[]{:S(2)}, u32[]{:S(2)}) collective-permute-start(f32[1,4,8,8,128]{4,3,2,1,0:T(8,128)S(1)} %get-tuple-element.25), channel_id=1, source_target_pairs={{0,8},{4,12},{8,0},{12,4},{1,9},{5,13},{9,1},{13,5},{2,10},{6,14},... | collective-permute-start | bytes 393224 | tf_op jit(solution)/shard_map/ppermute | solution.py:218
  7.8 10.6 %collective-permute-start.10 = (f32[1,4,8,8,128]{4,3,2,1,0:T(8,128)S(1)}, f32[1,4,8,8,128]{4,3,2,1,0:T(8,128)S(1)}, u32[]{:S(2)}, u32[]{:S(2)}) collective-permute-start(f32[1,4,8,8,128]{4,3,2,1,0:T(8,128)S(1)} %get-tuple-element.26), channel_id=1, source_target_pairs={{0,4},{4,0},{8,12},{12,8},{1,5},{5,1},{9,13},{13,9},{2,6},{6,2},{1... | collective-permute-start | bytes 393224 | tf_op jit(solution)/shard_map/ppermute | solution.py:218
  8.5 13.4 %collective-permute-start = (f32[4,1,12,8,128]{4,3,2,1,0:T(8,128)S(1)}, f32[4,1,12,8,128]{4,3,2,1,0:T(8,128)S(1)}, u32[]{:S(2)}, u32[]{:S(2)}) collective-permute-start(f32[4,1,12,8,128]{4,3,2,1,0:T(8,128)S(1)} %get-tuple-element.20), channel_id=1, source_target_pairs={{0,3},{1,2},{2,1},{3,0},{4,7},{5,6},{6,5},{7,4},{8,11},{9,10},{10,... | collective-permute-start | bytes 589832 | tf_op jit(solution)/shard_map/ppermute | solution.py:218
  11.5 11.9 %collective-permute-start.1 = (f32[4,1,12,8,128]{4,3,2,1,0:T(8,128)S(1)}, f32[4,1,12,8,128]{4,3,2,1,0:T(8,128)S(1)}, u32[]{:S(2)}, u32[]{:S(2)}) collective-permute-start(f32[4,1,12,8,128]{4,3,2,1,0:T(8,128)S(1)} %get-tuple-element.21), channel_id=1, source_target_pairs={{0,2},{1,3},{2,0},{3,1},{4,6},{5,7},{6,4},{7,5},{8,10},{9,11},{10,... | collective-permute-start | bytes 589832 | tf_op jit(solution)/shard_map/ppermute | solution.py:218
  12.2 11.2 %collective-permute-start.2 = (f32[4,1,12,8,128]{4,3,2,1,0:T(8,128)S(1)}, f32[4,1,12,8,128]{4,3,2,1,0:T(8,128)S(1)}, u32[]{:S(2)}, u32[]{:S(2)}) collective-permute-start(f32[4,1,12,8,128]{4,3,2,1,0:T(8,128)S(1)} %get-tuple-element.22), channel_id=1, source_target_pairs={{0,1},{1,0},{2,3},{3,2},{4,5},{5,4},{6,7},{7,6},{8,9},{9,8},{10,11... | collective-permute-start | bytes 589832 | tf_op jit(solution)/shard_map/ppermute | solution.py:218
  18.6 7.8 %collective-permute-start.11 = (f32[4,1,8,8,128]{4,3,2,1,0:T(8,128)S(1)}, f32[4,1,8,8,128]{4,3,2,1,0:T(8,128)S(1)}, u32[]{:S(2)}, u32[]{:S(2)}) collective-permute-start(f32[4,1,8,8,128]{4,3,2,1,0:T(8,128)S(1)} %get-tuple-element.87), channel_id=1, source_target_pairs={{0,3},{1,2},{2,1},{3,0},{4,7},{5,6},{6,5},{7,4},{8,11},{9,10},{10,... | collective-permute-start | bytes 393224 | tf_op jit(solution)/shard_map/ppermute | solution.py:218
  21.7 6.5 %collective-permute-start.13 = (f32[4,1,8,8,128]{4,3,2,1,0:T(8,128)S(1)}, f32[4,1,8,8,128]{4,3,2,1,0:T(8,128)S(1)}, u32[]{:S(2)}, u32[]{:S(2)}) collective-permute-start(f32[4,1,8,8,128]{4,3,2,1,0:T(8,128)S(1)} %get-tuple-element.89), channel_id=1, source_target_pairs={{0,1},{1,0},{2,3},{3,2},{4,5},{5,4},{6,7},{7,6},{8,9},{9,8},{10,11... | collective-permute-start | bytes 393224 | tf_op jit(solution)/shard_map/ppermute | solution.py:218
  21.9 7.1 %collective-permute-start.12 = (f32[4,1,8,8,128]{4,3,2,1,0:T(8,128)S(1)}, f32[4,1,8,8,128]{4,3,2,1,0:T(8,128)S(1)}, u32[]{:S(2)}, u32[]{:S(2)}) collective-permute-start(f32[4,1,8,8,128]{4,3,2,1,0:T(8,128)S(1)} %get-tuple-element.90), channel_id=1, source_target_pairs={{0,2},{1,3},{2,0},{3,1},{4,6},{5,7},{6,4},{7,5},{8,10},{9,11},{10,... | collective-permute-start | bytes 393224 | tf_op jit(solution)/shard_map/ppermute | solution.py:218
  23.7 13.8 %collective-permute-start.3 = (f32[1,4,12,8,128]{4,3,2,1,0:T(8,128)S(1)}, f32[1,4,12,8,128]{4,3,2,1,0:T(8,128)S(1)}, u32[]{:S(2)}, u32[]{:S(2)}) collective-permute-start(f32[1,4,12,8,128]{4,3,2,1,0:T(8,128)S(1)} %get-tuple-element.41), channel_id=1, source_target_pairs={{0,12},{4,8},{8,4},{12,0},{1,13},{5,9},{9,5},{13,1},{2,14},{6,10},... | collective-permute-start | bytes 589832 | tf_op jit(solution)/shard_map/ppermute | solution.py:218
  26.5 11.6 %collective-permute-start.5 = (f32[1,4,12,8,128]{4,3,2,1,0:T(8,128)S(1)}, f32[1,4,12,8,128]{4,3,2,1,0:T(8,128)S(1)}, u32[]{:S(2)}, u32[]{:S(2)}) collective-permute-start(f32[1,4,12,8,128]{4,3,2,1,0:T(8,128)S(1)} %get-tuple-element.43), channel_id=1, source_target_pairs={{0,4},{4,0},{8,12},{12,8},{1,5},{5,1},{9,13},{13,9},{2,6},{6,2},{1... | collective-permute-start | bytes 589832 | tf_op jit(solution)/shard_map/ppermute | solution.py:218
  26.5 17.0 %collective-permute-start.4 = (f32[1,4,12,8,128]{4,3,2,1,0:T(8,128)S(1)}, f32[1,4,12,8,128]{4,3,2,1,0:T(8,128)S(1)}, u32[]{:S(2)}, u32[]{:S(2)}) collective-permute-start(f32[1,4,12,8,128]{4,3,2,1,0:T(8,128)S(1)} %get-tuple-element.44), channel_id=1, source_target_pairs={{0,8},{4,12},{8,0},{12,4},{1,9},{5,13},{9,1},{13,5},{2,10},{6,14},... | collective-permute-start | bytes 589832 | tf_op jit(solution)/shard_map/ppermute | solution.py:218
  29.9 22.6 %collective-permute-start.15 = (f32[16,7,8,128]{3,2,1,0:T(8,128)}, f32[16,7,8,128]{3,2,1,0:T(8,128)S(1)}, u32[]{:S(2)}, u32[]{:S(2)}) collective-permute-start(f32[16,7,8,128]{3,2,1,0:T(8,128)} %get-tuple-element.81), channel_id=1, source_target_pairs={{0,1},{1,2},{2,3},{3,4},{4,5},{5,6},{6,7},{7,8},{8,9},{9,10},{10,1... | collective-permute-start | bytes 1376264 | tf_op jit(solution)/shard_map/ppermute | solution.py:250
  33.1 19.4 %collective-permute-start.14 = (f32[16,7,8,128]{3,2,1,0:T(8,128)S(1)}, f32[16,7,8,128]{3,2,1,0:T(8,128)S(1)}, u32[]{:S(2)}, u32[]{:S(2)}) collective-permute-start(f32[16,7,8,128]{3,2,1,0:T(8,128)S(1)} %get-tuple-element.82), channel_id=1, source_target_pairs={{1,0},{2,1},{3,2},{4,3},{5,4},{6,5},{7,6},{8,7},{9,8},{10,9},{11,1... | collective-permute-start | bytes 1376264 | tf_op jit(solution)/shard_map/ppermute | solution.py:249
  44.6 11.4 %collective-permute-start.7 = (f32[16,6,8,128]{3,2,1,0:T(8,128)}, f32[16,6,8,128]{3,2,1,0:T(8,128)S(1)}, u32[]{:S(2)}, u32[]{:S(2)}) collective-permute-start(f32[16,6,8,128]{3,2,1,0:T(8,128)} %get-tuple-element.35), channel_id=1, source_target_pairs={{0,1},{1,2},{2,3},{3,4},{4,5},{5,6},{6,7},{7,8},{8,9},{9,10},{10,1... | collective-permute-start | bytes 1179656 | tf_op jit(solution)/shard_map/ppermute | solution.py:250
  46.9 13.5 %collective-permute-start.6 = (f32[16,6,8,128]{3,2,1,0:T(8,128)}, f32[16,6,8,128]{3,2,1,0:T(8,128)S(1)}, u32[]{:S(2)}, u32[]{:S(2)}) collective-permute-start(f32[16,6,8,128]{3,2,1,0:T(8,128)} %get-tuple-element.36), channel_id=1, source_target_pairs={{1,0},{2,1},{3,2},{4,3},{5,4},{6,5},{7,6},{8,7},{9,8},{10,9},{11,1... | collective-permute-start | bytes 1179656 | tf_op jit(solution)/shard_map/ppermute | solution.py:249
  52.5 7.9 %copy-start.1 = (s32[64,9]{0,1:T(8,128)S(1)}, s32[64,9]{0,1:T(8,128)}, u32[]{:S(2)}) copy-start(s32[64,9]{0,1:T(8,128)} %param.6) | copy-start | bytes 6916
  52.5 7.9 %copy-start.2 = (s32[64,5]{0,1:T(8,128)S(1)}, s32[64,5]{0,1:T(8,128)}, u32[]{:S(2)}) copy-start(s32[64,5]{0,1:T(8,128)} %param.7) | copy-start | bytes 3844
  64.2 8.4 %collective-permute-start.20 = (f32[1,4,9,8,128]{4,3,2,1,0:T(8,128)S(1)}, f32[1,4,9,8,128]{4,3,2,1,0:T(8,128)S(1)}, u32[]{:S(2)}, u32[]{:S(2)}) collective-permute-start(f32[1,4,9,8,128]{4,3,2,1,0:T(8,128)S(1)} %get-tuple-element.77), channel_id=1, source_target_pairs={{0,12},{4,8},{8,4},{12,0},{1,13},{5,9},{9,5},{13,1},{2,14},{6,10},... | collective-permute-start | bytes 442376 | tf_op jit(solution)/shard_map/ppermute | solution.py:218
  65.2 12.0 %collective-permute-start.22 = (f32[1,4,9,8,128]{4,3,2,1,0:T(8,128)S(1)}, f32[1,4,9,8,128]{4,3,2,1,0:T(8,128)S(1)}, u32[]{:S(2)}, u32[]{:S(2)}) collective-permute-start(f32[1,4,9,8,128]{4,3,2,1,0:T(8,128)S(1)} %get-tuple-element.79), channel_id=1, source_target_pairs={{0,4},{4,0},{8,12},{12,8},{1,5},{5,1},{9,13},{13,9},{2,6},{6,2},{1... | collective-permute-start | bytes 442376 | tf_op jit(solution)/shard_map/ppermute | solution.py:218
  68.0 12.0 %collective-permute-start.21 = (f32[1,4,9,8,128]{4,3,2,1,0:T(8,128)S(1)}, f32[1,4,9,8,128]{4,3,2,1,0:T(8,128)S(1)}, u32[]{:S(2)}, u32[]{:S(2)}) collective-permute-start(f32[1,4,9,8,128]{4,3,2,1,0:T(8,128)S(1)} %get-tuple-element.80), channel_id=1, source_target_pairs={{0,8},{4,12},{8,0},{12,4},{1,9},{5,13},{9,1},{13,5},{2,10},{6,14},... | collective-permute-start | bytes 442376 | tf_op jit(solution)/shard_map/ppermute | solution.py:218
  68.8 11.3 %collective-permute-start.16 = (f32[4,1,11,8,128]{4,3,2,1,0:T(8,128)S(1)}, f32[4,1,11,8,128]{4,3,2,1,0:T(8,128)S(1)}, u32[]{:S(2)}, u32[]{:S(2)}) collective-permute-start(f32[4,1,11,8,128]{4,3,2,1,0:T(8,128)S(1)} %get-tuple-element.61), channel_id=1, source_target_pairs={{0,3},{1,2},{2,1},{3,0},{4,7},{5,6},{6,5},{7,4},{8,11},{9,10},{10,... | collective-permute-start | bytes 540680 | tf_op jit(solution)/shard_map/ppermute | solution.py:218
  68.9 11.2 %collective-permute-start.18 = (f32[4,1,11,8,128]{4,3,2,1,0:T(8,128)S(1)}, f32[4,1,11,8,128]{4,3,2,1,0:T(8,128)S(1)}, u32[]{:S(2)}, u32[]{:S(2)}) collective-permute-start(f32[4,1,11,8,128]{4,3,2,1,0:T(8,128)S(1)} %get-tuple-element.63), channel_id=1, source_target_pairs={{0,1},{1,0},{2,3},{3,2},{4,5},{5,4},{6,7},{7,6},{8,9},{9,8},{10,11... | collective-permute-start | bytes 540680 | tf_op jit(solution)/shard_map/ppermute | solution.py:218
  72.6 9.5 %collective-permute-start.17 = (f32[4,1,11,8,128]{4,3,2,1,0:T(8,128)S(1)}, f32[4,1,11,8,128]{4,3,2,1,0:T(8,128)S(1)}, u32[]{:S(2)}, u32[]{:S(2)}) collective-permute-start(f32[4,1,11,8,128]{4,3,2,1,0:T(8,128)S(1)} %get-tuple-element.64), channel_id=1, source_target_pairs={{0,2},{1,3},{2,0},{3,1},{4,6},{5,7},{6,4},{7,5},{8,10},{9,11},{10,... | collective-permute-start | bytes 540680 | tf_op jit(solution)/shard_map/ppermute | solution.py:218
  82.4 8.4 %collective-permute-start.19 = (f32[1,4,11,8,128]{4,3,2,1,0:T(8,128)S(1)}, f32[1,4,11,8,128]{4,3,2,1,0:T(8,128)S(1)}, u32[]{:S(2)}, u32[]{:S(2)}) collective-permute-start(f32[1,4,11,8,128]{4,3,2,1,0:T(8,128)S(1)} %get-tuple-element.56), channel_id=1, source_target_pairs={{0,4},{4,0},{8,12},{12,8},{1,5},{5,1},{9,13},{13,9},{2,6},{6,2},{1... | collective-permute-start | bytes 540680 | tf_op jit(solution)/shard_map/ppermute | solution.py:218
  82.8 12.8 %collective-permute-start.26 = (f32[1,4,11,8,128]{4,3,2,1,0:T(8,128)S(1)}, f32[1,4,11,8,128]{4,3,2,1,0:T(8,128)S(1)}, u32[]{:S(2)}, u32[]{:S(2)}) collective-permute-start(f32[1,4,11,8,128]{4,3,2,1,0:T(8,128)S(1)} %get-tuple-element.53), channel_id=1, source_target_pairs={{0,12},{4,8},{8,4},{12,0},{1,13},{5,9},{9,5},{13,1},{2,14},{6,10},... | collective-permute-start | bytes 540680 | tf_op jit(solution)/shard_map/ppermute | solution.py:218
  84.8 16.5 %collective-permute-start.27 = (f32[1,4,11,8,128]{4,3,2,1,0:T(8,128)S(1)}, f32[1,4,11,8,128]{4,3,2,1,0:T(8,128)S(1)}, u32[]{:S(2)}, u32[]{:S(2)}) collective-permute-start(f32[1,4,11,8,128]{4,3,2,1,0:T(8,128)S(1)} %get-tuple-element.55), channel_id=1, source_target_pairs={{0,8},{4,12},{8,0},{12,4},{1,9},{5,13},{9,1},{13,5},{2,10},{6,14},... | collective-permute-start | bytes 540680 | tf_op jit(solution)/shard_map/ppermute | solution.py:218
  90.9 10.6 %collective-permute-start.23 = (f32[4,1,9,8,128]{4,3,2,1,0:T(8,128)S(1)}, f32[4,1,9,8,128]{4,3,2,1,0:T(8,128)S(1)}, u32[]{:S(2)}, u32[]{:S(2)}) collective-permute-start(f32[4,1,9,8,128]{4,3,2,1,0:T(8,128)S(1)} %get-tuple-element.69), channel_id=1, source_target_pairs={{0,3},{1,2},{2,1},{3,0},{4,7},{5,6},{6,5},{7,4},{8,11},{9,10},{10,... | collective-permute-start | bytes 442376 | tf_op jit(solution)/shard_map/ppermute | solution.py:218
  91.2 10.2 %collective-permute-start.25 = (f32[4,1,9,8,128]{4,3,2,1,0:T(8,128)S(1)}, f32[4,1,9,8,128]{4,3,2,1,0:T(8,128)S(1)}, u32[]{:S(2)}, u32[]{:S(2)}) collective-permute-start(f32[4,1,9,8,128]{4,3,2,1,0:T(8,128)S(1)} %get-tuple-element.71), channel_id=1, source_target_pairs={{0,1},{1,0},{2,3},{3,2},{4,5},{5,4},{6,7},{7,6},{8,9},{9,8},{10,11... | collective-permute-start | bytes 442376 | tf_op jit(solution)/shard_map/ppermute | solution.py:218
  92.6 8.9 %collective-permute-start.24 = (f32[4,1,9,8,128]{4,3,2,1,0:T(8,128)S(1)}, f32[4,1,9,8,128]{4,3,2,1,0:T(8,128)S(1)}, u32[]{:S(2)}, u32[]{:S(2)}) collective-permute-start(f32[4,1,9,8,128]{4,3,2,1,0:T(8,128)S(1)} %get-tuple-element.72), channel_id=1, source_target_pairs={{0,2},{1,3},{2,0},{3,1},{4,6},{5,7},{6,4},{7,5},{8,10},{9,11},{10,... | collective-permute-start | bytes 442376 | tf_op jit(solution)/shard_map/ppermute | solution.py:218

commit v5 on v4

--- a/solution.py
+++ b/solution.py
@@ -26,7 +26,8 @@
 
 def ranks(row, col, depth):
     core, z_half = row & 1, (row >> 1) & 1
-    return col ^ (3 * (core ^ z_half)), depth ^ (3 * core)
+    col_rank = col ^ (3 * (core ^ z_half))
+    return col_rank, depth ^ (3 * (col_rank & 1))
 
 
 def place():
@@ -50,7 +51,7 @@
             rank = (col_rank ^ k) * 4 + other
             for index, (block_row, slot) in enumerate(INNER):
                 outs[k][0, other, index] = density[rank * OWN + block_row, slot] * weight(rank, block_row, slot)
-            rank = other * 4 + (depth_rank ^ k)
+            rank = other * 4 + (depth ^ (3 * (other & 1)) ^ k)
             for index, (block_row, slot) in enumerate(OUTER):
                 outs[4 + k][other, 0, index] = density[rank * OWN + block_row, slot] * weight(rank, block_row, slot)
 
@@ -267,7 +268,9 @@
     upper = send(cut(upper, 0, col), "col")
     upper[1], lower = lax.optimization_barrier((upper[1], lower))
     upper = join(upper, 0, col_rank)
-    lower = swap(lower, "depth", 1, depth_rank, depth)
+    lower = send(cut(lower, 1, depth), "depth")
+    turns = [join([piece[turn::2] for piece in lower], 1, depth ^ (3 * turn)) for turn in range(2)]
+    lower = jnp.stack(turns, axis=1).reshape(4, 4, FIRST_OUT, 8, BLK)
     return jnp.concatenate([lower, upper], axis=2).reshape(density.shape)
 
 

time: 104 us -> 101 us (0.971)
  starting transfers between devices: 49.4 us -> 44.4 us
  waiting for transfers between devices: 39.4 us -> 41.4 us
    ppermute x2, starting transfers between devices: 10 us -> 5.02 us  [halo(): after = lax.ppermute(group[:, before_part], EVERY, down)]
    ppermute x2, waiting for transfers between devices: 1.24 us -> 3.71 us  [halo(): before = lax.ppermute(group[:, after_part], EVERY, up)]
    ppermute x24, starting transfers between devices: 33.9 us -> 32.6 us  [send(): lax.ppermute(pieces[k], axis, [(i, i ^ k) for i in range(size)])]
    ppermute x2, starting transfers between devices: 5.49 us -> 6.82 us  [halo(): before = lax.ppermute(group[:, after_part], EVERY, up)]
  transfers between devices with their start and end apart: 28 -> 28, of which waited for: 13 -> 12; matrix products, arithmetic and copies ran while one was open for 3% -> 3% of each run, Pallas kernels for 2% -> 2%
where the time goes in v5:
time: 101 us; the launch traced here: 100 us
  starting transfers between devices  44.4 us (44%)
  waiting for transfers between devices  41.4 us (41%)
  Pallas kernels  7.05 us (7%)
  local copies, waits for them, and re-layouts  4.81 us (5%)
  other arithmetic  1.84 us (2%)
    ppermute x24, waiting for transfers between devices, send(): lax.ppermute(pieces[k], axis, [(i, i ^ k) for i in range(size)])  33.1 us
    ppermute x24, starting transfers between devices, send(): lax.ppermute(pieces[k], axis, [(i, i ^ k) for i in range(size)])  32.6 us
    ppermute x2, starting transfers between devices, halo(): before = lax.ppermute(group[:, after_part], EVERY, up)  6.82 us
    ppermute x2, starting transfers between devices, halo(): after = lax.ppermute(group[:, before_part], EVERY, down)  5.02 us
    ppermute x2, waiting for transfers between devices, halo(): after = lax.ppermute(group[:, before_part], EVERY, down)  4.59 us
    ppermute x2, waiting for transfers between devices, halo(): before = lax.ppermute(group[:, after_part], EVERY, up)  3.71 us
    pallas_call x1, Pallas kernels, late_part(): pl.pallas_call(late_kernel, out_shape=[jax.ShapeDtypeStruct((16, count, 8...  3.7 us
    pallas_call x1, Pallas kernels, early_part(): pl.pallas_call(early_kernel, out_shape=(part, part, jax.ShapeDtypeStruct(...  2.25 us
  transfers between devices with their start and end apart: 28, of which 12 were waited for; matrix products, arithmetic and copies ran while one was open for 3% of the time, Pallas kernels for 2%

profile of v5, /device:TPU:2, one launch (start us, length us, event | category | flops | bytes accessed | tf_op | source)
XLA Modules:
  0.0 100.0 jit_solution(10760823069421245148)
XLA Ops:
  0.0 1.3 %copy-done = f32[64,5,8,128]{3,2,1,0:T(8,128)S(1)} copy-done((f32[64,5,8,128]{3,2,1,0:T(8,128)S(1)}, f32[64,5,8,128]{3,2,1,0:T(8,128)}, u32[]{:S(2)}) %copy-start) | copy-done | bytes 1310744
  1.3 0.7 copy-done.3
  2.0 1.1 %shard_map.46 = (f32[1,4,8,8,128]{4,3,2,1,0:T(8,128)S(1)}, f32[1,4,8,8,128]{4,3,2,1,0:T(8,128)S(1)}, f32[1,4,8,8,128]{4,3,2,1,0:T(8,128)S(1)}, f32[1,4,8,8,128]{...) custom-call(f32[64,5,8,128]{3,2,1,0:T(8,128)S(1)} %copy-done, ...), custom_call_target="tpu_custom_call" | custom-call | flops 1000000 | bytes 4194304 | tf_op jit(solution)/shard_map/pallas_call | solution.py:64
  3.1 4.7 %collective-permute-start.8 = (f32[1,4,8,8,128]{4,3,2,1,0:T(8,128)S(1)}, f32[1,4,8,8,128]{4,3,2,1,0:T(8,128)S(1)}, u32[]{:S(2)}, u32[]{:S(2)}) collective-permute-start(f32[1,4,8,8,128]{4,3,2,1,0:T(8,128)S(1)} %get-tuple-element.24), channel_id=1, source_target_pairs={{0,12},{4,8},{8,4},{12,0},{1,13},{5,9},{9,5},{13,1},{2,14},{6,10},... | collective-permute-start | bytes 393224 | tf_op jit(solution)/shard_map/ppermute | solution.py:219
  7.8 0.7 collective-permute-start.10
  8.5 3.0 %collective-permute-start = (f32[4,1,12,8,128]{4,3,2,1,0:T(8,128)S(1)}, f32[4,1,12,8,128]{4,3,2,1,0:T(8,128)S(1)}, u32[]{:S(2)}, u32[]{:S(2)}) collective-permute-start(f32[4,1,12,8,128]{4,3,2,1,0:T(8,128)S(1)} %get-tuple-element.20), channel_id=1, source_target_pairs={{0,3},{1,2},{2,1},{3,0},{4,7},{5,6},{6,5},{7,4},{8,11},{9,10},{10,... | collective-permute-start | bytes 589832 | tf_op jit(solution)/shard_map/ppermute | solution.py:219
  11.5 0.6 collective-permute-start.1
  12.1 0.1 collective-permute-done.8
  12.3 1.6 %collective-permute-start.2 = (f32[4,1,12,8,128]{4,3,2,1,0:T(8,128)S(1)}, f32[4,1,12,8,128]{4,3,2,1,0:T(8,128)S(1)}, u32[]{:S(2)}, u32[]{:S(2)}) collective-permute-start(f32[4,1,12,8,128]{4,3,2,1,0:T(8,128)S(1)} %get-tuple-element.22), channel_id=1, source_target_pairs={{0,1},{1,0},{2,3},{3,2},{4,5},{5,4},{6,7},{7,6},{8,9},{9,8},{10,11... | collective-permute-start | bytes 589832 | tf_op jit(solution)/shard_map/ppermute | solution.py:219
  13.8 4.6 %collective-permute-done.9 = f32[1,4,8,8,128]{4,3,2,1,0:T(8,128)S(1)} collective-permute-done((f32[1,4,8,8,128]{4,3,2,1,0:T(8,128)S(1)}, f32[1,4,8,8,128]{4,3,2,1,0:T(8,128)S(1)}, u32[]{:S(2)}, u32[]{:S(2)}) %collective-permute-start.9) | collective-permute-done | bytes 131104 | tf_op jit(solution)/shard_map/ppermute | solution.py:219
  18.6 3.1 %collective-permute-start.11 = (f32[4,1,8,8,128]{4,3,2,1,0:T(8,128)S(1)}, f32[4,1,8,8,128]{4,3,2,1,0:T(8,128)S(1)}, u32[]{:S(2)}, u32[]{:S(2)}) collective-permute-start(f32[4,1,8,8,128]{4,3,2,1,0:T(8,128)S(1)} %get-tuple-element.83), channel_id=1, source_target_pairs={{0,3},{1,2},{2,1},{3,0},{4,7},{5,6},{6,5},{7,4},{8,11},{9,10},{10,... | collective-permute-start | bytes 393224 | tf_op jit(solution)/shard_map/ppermute | solution.py:219
  21.7 0.6 collective-permute-start.12
  22.4 0.5 collective-permute-start.13
  23.1 2.7 %collective-permute-start.3 = (f32[1,4,12,8,128]{4,3,2,1,0:T(8,128)S(1)}, f32[1,4,12,8,128]{4,3,2,1,0:T(8,128)S(1)}, u32[]{:S(2)}, u32[]{:S(2)}) collective-permute-start(f32[1,4,12,8,128]{4,3,2,1,0:T(8,128)S(1)} %get-tuple-element.41), channel_id=1, source_target_pairs={{0,12},{4,8},{8,4},{12,0},{1,13},{5,9},{9,5},{13,1},{2,14},{6,10},... | collective-permute-start | bytes 589832 | tf_op jit(solution)/shard_map/ppermute | solution.py:219
  25.9 0.8 collective-permute-start.4
  26.7 0.9 collective-permute-start.5
  27.6 1.4 %collective-permute-done.12 = f32[4,1,8,8,128]{4,3,2,1,0:T(8,128)S(1)} collective-permute-done((f32[4,1,8,8,128]{4,3,2,1,0:T(8,128)S(1)}, f32[4,1,8,8,128]{4,3,2,1,0:T(8,128)S(1)}, u32[]{:S(2)}, u32[]{:S(2)}) %collective-permute-start.12) | collective-permute-done | bytes 131104 | tf_op jit(solution)/shard_map/ppermute | solution.py:219
  29.1 0.8 fusion.1
  29.9 3.1 %collective-permute-start.14 = (f32[16,7,8,128]{3,2,1,0:T(8,128)}, f32[16,7,8,128]{3,2,1,0:T(8,128)S(1)}, u32[]{:S(2)}, u32[]{:S(2)}) collective-permute-start(f32[16,7,8,128]{3,2,1,0:T(8,128)} %get-tuple-element.78), channel_id=1, source_target_pairs={{1,0},{2,1},{3,2},{7,3},{6,7},{5,6},{4,5},{8,4},{9,8},{10,9},{11,1... | collective-permute-start | bytes 1376264 | tf_op jit(solution)/shard_map/ppermute | solution.py:250
  33.1 2.7 %collective-permute-start.15 = (f32[16,7,8,128]{3,2,1,0:T(8,128)S(1)}, f32[16,7,8,128]{3,2,1,0:T(8,128)S(1)}, u32[]{:S(2)}, u32[]{:S(2)}) collective-permute-start(f32[16,7,8,128]{3,2,1,0:T(8,128)S(1)} %get-tuple-element.77), channel_id=1, source_target_pairs={{0,1},{1,2},{2,3},{3,7},{7,6},{6,5},{5,4},{4,8},{8,9},{9,10},{10,1... | collective-permute-start | bytes 1376264 | tf_op jit(solution)/shard_map/ppermute | solution.py:251
  35.8 7.2 %collective-permute-done.4 = f32[1,4,12,8,128]{4,3,2,1,0:T(8,128)S(1)} collective-permute-done((f32[1,4,12,8,128]{4,3,2,1,0:T(8,128)S(1)}, f32[1,4,12,8,128]{4,3,2,1,0:T(8,128)S(1)}, u32[]{:S(2)}, u32[]{:S(2)}) %collective-permute-start.4) | collective-permute-done | bytes 196640 | tf_op jit(solution)/shard_map/ppermute | solution.py:219
  43.2 0.9 fusion
  44.2 1.9 %collective-permute-start.6 = (f32[16,6,8,128]{3,2,1,0:T(8,128)}, f32[16,6,8,128]{3,2,1,0:T(8,128)S(1)}, u32[]{:S(2)}, u32[]{:S(2)}) collective-permute-start(f32[16,6,8,128]{3,2,1,0:T(8,128)} %get-tuple-element.36), channel_id=1, source_target_pairs={{1,0},{2,1},{3,2},{7,3},{6,7},{5,6},{4,5},{8,4},{9,8},{10,9},{11,1... | collective-permute-start | bytes 1179656 | tf_op jit(solution)/shard_map/ppermute | solution.py:250
  46.1 4.1 %collective-permute-start.7 = (f32[16,6,8,128]{3,2,1,0:T(8,128)}, f32[16,6,8,128]{3,2,1,0:T(8,128)S(1)}, u32[]{:S(2)}, u32[]{:S(2)}) collective-permute-start(f32[16,6,8,128]{3,2,1,0:T(8,128)} %get-tuple-element.35), channel_id=1, source_target_pairs={{0,1},{1,2},{2,3},{3,7},{7,6},{6,5},{5,4},{4,8},{8,9},{9,10},{10,1... | collective-permute-start | bytes 1179656 | tf_op jit(solution)/shard_map/ppermute | solution.py:251
  50.2 2.2 %shard_map.47 = (bf16[1536,1536]{1,0:T(8,128)(2,1)S(1)}, bf16[1536,1536]{1,0:T(8,128)(2,1)S(1)}, f32[2,256,1280]{2,1,0:T(8,128)S(1)}) custom-call(f32[16,12,8,128]{3,2,1,0:T(8,128)S(1)} %bitcast.16, f32[16,8,8,128]{3,2,1,0:T(8,128)S(1)} %bitcast.14, f32[16,7,8,128]{3,2,1,0:T(8,128)S(1)} %collective-permute-done.14.inner_after, ...), custom_call_target="tpu_custom_call" | custom-call | flops 1811939328 | bytes 16777216 | tf_op jit(solution)/shard_map/pallas_call | solution.py:133
  52.5 4.6 %collective-permute-done.6.after = f32[16,6,8,128]{3,2,1,0:T(8,128)S(1)} collective-permute-done((f32[16,6,8,128]{3,2,1,0:T(8,128)}, f32[16,6,8,128]{3,2,1,0:T(8,128)S(1)}, u32[]{:S(2)}, u32[]{:S(2)}) %collective-permute-start.6) | collective-permute-done | bytes 393248 | tf_op jit(solution)/shard_map/ppermute | solution.py:250
  57.1 3.7 %collective-permute-done.7.before = f32[16,6,8,128]{3,2,1,0:T(8,128)S(1)} collective-permute-done((f32[16,6,8,128]{3,2,1,0:T(8,128)}, f32[16,6,8,128]{3,2,1,0:T(8,128)S(1)}, u32[]{:S(2)}, u32[]{:S(2)}) %collective-permute-start.7) | collective-permute-done | bytes 393248 | tf_op jit(solution)/shard_map/ppermute | solution.py:251
  60.8 3.7 %shard_map.48 = (f32[16,9,8,128]{3,2,1,0:T(8,128)S(1)}, f32[16,11,8,128]{3,2,1,0:T(8,128)S(1)}, bf16[1536,1536]{1,0:T(8,128)(2,1)S(1)}, bf16[1536,1536]{1,0:T(8,128)(2,1)S(1)}) custom-call(f32[16,6,8,128]{3,2,1,0:T(8,128)S(1)} %collective-permute-done.6.after, ...), custom_call_target="tpu_custom_call", output_to_operand_aliasing={{2}: (2, {}), {3}: (3, {})} | custom-call | flops 2214592512 | bytes 4194304 | tf_op jit(solution)/shard_map/pallas_call | solution.py:205
  64.6 0.1 collective-permute-start.20
  64.7 0.3 collective-permute-start.21
  65.0 4.0 %collective-permute-start.22 = (f32[1,4,9,8,128]{4,3,2,1,0:T(8,128)S(1)}, f32[1,4,9,8,128]{4,3,2,1,0:T(8,128)S(1)}, u32[]{:S(2)}, u32[]{:S(2)}) collective-permute-start(f32[1,4,9,8,128]{4,3,2,1,0:T(8,128)S(1)} %get-tuple-element.75), channel_id=1, source_target_pairs={{0,4},{4,0},{8,12},{12,8},{1,5},{5,1},{9,13},{13,9},{2,6},{6,2},{1... | collective-permute-start | bytes 442376 | tf_op jit(solution)/shard_map/ppermute | solution.py:219
  69.0 0.1 constant_dynamic-slice_fusion.35
  69.1 0.1 collective-permute-start.16
  69.2 0.1 collective-permute-start.17
  69.3 3.9 %collective-permute-done.20 = f32[1,4,9,8,128]{4,3,2,1,0:T(8,128)S(1)} collective-permute-done((f32[1,4,9,8,128]{4,3,2,1,0:T(8,128)S(1)}, f32[1,4,9,8,128]{4,3,2,1,0:T(8,128)S(1)}, u32[]{:S(2)}, u32[]{:S(2)}) %collective-permute-start.20) | collective-permute-done | bytes 147488 | tf_op jit(solution)/shard_map/ppermute | solution.py:219
  73.2 0.1 collective-permute-start.18
  73.3 4.3 %collective-permute-done.21 = f32[1,4,9,8,128]{4,3,2,1,0:T(8,128)S(1)} collective-permute-done((f32[1,4,9,8,128]{4,3,2,1,0:T(8,128)S(1)}, f32[1,4,9,8,128]{4,3,2,1,0:T(8,128)S(1)}, u32[]{:S(2)}, u32[]{:S(2)}) %collective-permute-start.21) | collective-permute-done | bytes 147488 | tf_op jit(solution)/shard_map/ppermute | solution.py:219
  77.6 1.5 %collective-permute-done.16 = f32[4,1,11,8,128]{4,3,2,1,0:T(8,128)S(1)} collective-permute-done((f32[4,1,11,8,128]{4,3,2,1,0:T(8,128)S(1)}, f32[4,1,11,8,128]{4,3,2,1,0:T(8,128)S(1)}, u32[]{:S(2)}, u32[]{:S(2)}) %collective-permute-start.16) | collective-permute-done | bytes 180256 | tf_op jit(solution)/shard_map/ppermute | solution.py:219
  79.1 0.6 collective-permute-done.18
  79.8 0.1 constant_dynamic-slice_fusion.31
  80.0 0.9 collective-permute-start.19
  81.1 3.5 %collective-permute-start.26 = (f32[1,4,11,8,128]{4,3,2,1,0:T(8,128)S(1)}, f32[1,4,11,8,128]{4,3,2,1,0:T(8,128)S(1)}, u32[]{:S(2)}, u32[]{:S(2)}) collective-permute-start(f32[1,4,11,8,128]{4,3,2,1,0:T(8,128)S(1)} %get-tuple-element.53), channel_id=1, source_target_pairs={{0,12},{4,8},{8,4},{12,0},{1,13},{5,9},{9,5},{13,1},{2,14},{6,10},... | collective-permute-start | bytes 540680 | tf_op jit(solution)/shard_map/ppermute | solution.py:219
  84.6 3.0 %collective-permute-done.19 = f32[1,4,11,8,128]{4,3,2,1,0:T(8,128)S(1)} collective-permute-done((f32[1,4,11,8,128]{4,3,2,1,0:T(8,128)S(1)}, f32[1,4,11,8,128]{4,3,2,1,0:T(8,128)S(1)}, u32[]{:S(2)}, u32[]{:S(2)}) %collective-permute-start.19) | collective-permute-done | bytes 180256 | tf_op jit(solution)/shard_map/ppermute | solution.py:219
  87.6 0.1 collective-permute-start.24
  87.7 1.1 %collective-permute-start.25 = (f32[4,1,9,8,128]{4,3,2,1,0:T(8,128)S(1)}, f32[4,1,9,8,128]{4,3,2,1,0:T(8,128)S(1)}, u32[]{:S(2)}, u32[]{:S(2)}) collective-permute-start(f32[4,1,9,8,128]{4,3,2,1,0:T(8,128)S(1)} %get-tuple-element.67), channel_id=1, source_target_pairs={{0,1},{1,0},{2,3},{3,2},{4,5},{5,4},{6,7},{7,6},{8,9},{9,8},{10,11... | collective-permute-start | bytes 442376 | tf_op jit(solution)/shard_map/ppermute | solution.py:219
  88.8 3.0 %collective-permute-start.23 = (f32[4,1,9,8,128]{4,3,2,1,0:T(8,128)S(1)}, f32[4,1,9,8,128]{4,3,2,1,0:T(8,128)S(1)}, u32[]{:S(2)}, u32[]{:S(2)}) collective-permute-start(f32[4,1,9,8,128]{4,3,2,1,0:T(8,128)S(1)} %get-tuple-element.65), channel_id=1, source_target_pairs={{0,3},{1,2},{2,1},{3,0},{4,7},{5,6},{6,5},{7,4},{8,11},{9,10},{10,... | collective-permute-start | bytes 442376 | tf_op jit(solution)/shard_map/ppermute | solution.py:219
  91.8 6.5 %collective-permute-done.27 = f32[1,4,11,8,128]{4,3,2,1,0:T(8,128)S(1)} collective-permute-done((f32[1,4,11,8,128]{4,3,2,1,0:T(8,128)S(1)}, f32[1,4,11,8,128]{4,3,2,1,0:T(8,128)S(1)}, u32[]{:S(2)}, u32[]{:S(2)}) %collective-permute-start.27) | collective-permute-done | bytes 180256 | tf_op jit(solution)/shard_map/ppermute | solution.py:219
  98.8 1.2 %maximum_maximum_fusion = f32[4,4,20,8,128]{4,3,2,1,0:T(8,128)} fusion(f32[1,4,11,8,128]{4,3,2,1,0:T(8,128)S(1)} %get-tuple-element.50, f32[1,4,11,8,128]{4,3,2,1,0:T(8,128)S(1)} %get-tuple-element.51, f32[1,4,11,8,128]{4,3,2,1,0:T(8,128)S(1)} %get-tuple-element.52, f32[1,4,11,8,128]{4,3,2,1,0:T(8,128)S(1)} %get-tuple-element.49, ...), kind=kLoop, calls=%fused_computation | loop fusion | flops 1310720 | bytes 2621440 | tf_op jit(solution)/shard_map/concatenate | solution.py:274
  (65 shorter events, 1.6 us)
Async XLA Ops:
  0.0 1.3 %copy-start = (f32[64,5,8,128]{3,2,1,0:T(8,128)S(1)}, f32[64,5,8,128]{3,2,1,0:T(8,128)}, u32[]{:S(2)}) copy-start(f32[64,5,8,128]{3,2,1,0:T(8,128)} %density.1) | copy-start | bytes 3932164
  1.3 0.7 copy-start.3
  3.1 9.1 %collective-permute-start.8 = (f32[1,4,8,8,128]{4,3,2,1,0:T(8,128)S(1)}, f32[1,4,8,8,128]{4,3,2,1,0:T(8,128)S(1)}, u32[]{:S(2)}, u32[]{:S(2)}) collective-permute-start(f32[1,4,8,8,128]{4,3,2,1,0:T(8,128)S(1)} %get-tuple-element.24), channel_id=1, source_target_pairs={{0,12},{4,8},{8,4},{12,0},{1,13},{5,9},{9,5},{13,1},{2,14},{6,10},... | collective-permute-start | bytes 393224 | tf_op jit(solution)/shard_map/ppermute | solution.py:219
  7.8 10.6 %collective-permute-start.9 = (f32[1,4,8,8,128]{4,3,2,1,0:T(8,128)S(1)}, f32[1,4,8,8,128]{4,3,2,1,0:T(8,128)S(1)}, u32[]{:S(2)}, u32[]{:S(2)}) collective-permute-start(f32[1,4,8,8,128]{4,3,2,1,0:T(8,128)S(1)} %get-tuple-element.25), channel_id=1, source_target_pairs={{0,8},{4,12},{8,0},{12,4},{1,9},{5,13},{9,1},{13,5},{2,10},{6,14},... | collective-permute-start | bytes 393224 | tf_op jit(solution)/shard_map/ppermute | solution.py:219
  7.8 10.6 %collective-permute-start.10 = (f32[1,4,8,8,128]{4,3,2,1,0:T(8,128)S(1)}, f32[1,4,8,8,128]{4,3,2,1,0:T(8,128)S(1)}, u32[]{:S(2)}, u32[]{:S(2)}) collective-permute-start(f32[1,4,8,8,128]{4,3,2,1,0:T(8,128)S(1)} %get-tuple-element.26), channel_id=1, source_target_pairs={{0,4},{4,0},{8,12},{12,8},{1,5},{5,1},{9,13},{13,9},{2,6},{6,2},{1... | collective-permute-start | bytes 393224 | tf_op jit(solution)/shard_map/ppermute | solution.py:219
  8.5 13.9 %collective-permute-start = (f32[4,1,12,8,128]{4,3,2,1,0:T(8,128)S(1)}, f32[4,1,12,8,128]{4,3,2,1,0:T(8,128)S(1)}, u32[]{:S(2)}, u32[]{:S(2)}) collective-permute-start(f32[4,1,12,8,128]{4,3,2,1,0:T(8,128)S(1)} %get-tuple-element.20), channel_id=1, source_target_pairs={{0,3},{1,2},{2,1},{3,0},{4,7},{5,6},{6,5},{7,4},{8,11},{9,10},{10,... | collective-permute-start | bytes 589832 | tf_op jit(solution)/shard_map/ppermute | solution.py:219
  11.5 11.3 %collective-permute-start.1 = (f32[4,1,12,8,128]{4,3,2,1,0:T(8,128)S(1)}, f32[4,1,12,8,128]{4,3,2,1,0:T(8,128)S(1)}, u32[]{:S(2)}, u32[]{:S(2)}) collective-permute-start(f32[4,1,12,8,128]{4,3,2,1,0:T(8,128)S(1)} %get-tuple-element.21), channel_id=1, source_target_pairs={{0,2},{1,3},{2,0},{3,1},{4,6},{5,7},{6,4},{7,5},{8,10},{9,11},{10,... | collective-permute-start | bytes 589832 | tf_op jit(solution)/shard_map/ppermute | solution.py:219
  12.3 10.6 %collective-permute-start.2 = (f32[4,1,12,8,128]{4,3,2,1,0:T(8,128)S(1)}, f32[4,1,12,8,128]{4,3,2,1,0:T(8,128)S(1)}, u32[]{:S(2)}, u32[]{:S(2)}) collective-permute-start(f32[4,1,12,8,128]{4,3,2,1,0:T(8,128)S(1)} %get-tuple-element.22), channel_id=1, source_target_pairs={{0,1},{1,0},{2,3},{3,2},{4,5},{5,4},{6,7},{7,6},{8,9},{9,8},{10,11... | collective-permute-start | bytes 589832 | tf_op jit(solution)/shard_map/ppermute | solution.py:219
  18.6 8.1 %collective-permute-start.11 = (f32[4,1,8,8,128]{4,3,2,1,0:T(8,128)S(1)}, f32[4,1,8,8,128]{4,3,2,1,0:T(8,128)S(1)}, u32[]{:S(2)}, u32[]{:S(2)}) collective-permute-start(f32[4,1,8,8,128]{4,3,2,1,0:T(8,128)S(1)} %get-tuple-element.83), channel_id=1, source_target_pairs={{0,3},{1,2},{2,1},{3,0},{4,7},{5,6},{6,5},{7,4},{8,11},{9,10},{10,... | collective-permute-start | bytes 393224 | tf_op jit(solution)/shard_map/ppermute | solution.py:219
  21.7 7.2 %collective-permute-start.12 = (f32[4,1,8,8,128]{4,3,2,1,0:T(8,128)S(1)}, f32[4,1,8,8,128]{4,3,2,1,0:T(8,128)S(1)}, u32[]{:S(2)}, u32[]{:S(2)}) collective-permute-start(f32[4,1,8,8,128]{4,3,2,1,0:T(8,128)S(1)} %get-tuple-element.86), channel_id=1, source_target_pairs={{0,2},{1,3},{2,0},{3,1},{4,6},{5,7},{6,4},{7,5},{8,10},{9,11},{10,... | collective-permute-start | bytes 393224 | tf_op jit(solution)/shard_map/ppermute | solution.py:219
  22.4 6.6 %collective-permute-start.13 = (f32[4,1,8,8,128]{4,3,2,1,0:T(8,128)S(1)}, f32[4,1,8,8,128]{4,3,2,1,0:T(8,128)S(1)}, u32[]{:S(2)}, u32[]{:S(2)}) collective-permute-start(f32[4,1,8,8,128]{4,3,2,1,0:T(8,128)S(1)} %get-tuple-element.85), channel_id=1, source_target_pairs={{0,1},{1,0},{2,3},{3,2},{4,5},{5,4},{6,7},{7,6},{8,9},{9,8},{10,11... | collective-permute-start | bytes 393224 | tf_op jit(solution)/shard_map/ppermute | solution.py:219
  23.1 12.7 %collective-permute-start.3 = (f32[1,4,12,8,128]{4,3,2,1,0:T(8,128)S(1)}, f32[1,4,12,8,128]{4,3,2,1,0:T(8,128)S(1)}, u32[]{:S(2)}, u32[]{:S(2)}) collective-permute-start(f32[1,4,12,8,128]{4,3,2,1,0:T(8,128)S(1)} %get-tuple-element.41), channel_id=1, source_target_pairs={{0,12},{4,8},{8,4},{12,0},{1,13},{5,9},{9,5},{13,1},{2,14},{6,10},... | collective-permute-start | bytes 589832 | tf_op jit(solution)/shard_map/ppermute | solution.py:219
  25.9 17.2 %collective-permute-start.4 = (f32[1,4,12,8,128]{4,3,2,1,0:T(8,128)S(1)}, f32[1,4,12,8,128]{4,3,2,1,0:T(8,128)S(1)}, u32[]{:S(2)}, u32[]{:S(2)}) collective-permute-start(f32[1,4,12,8,128]{4,3,2,1,0:T(8,128)S(1)} %get-tuple-element.44), channel_id=1, source_target_pairs={{0,8},{4,12},{8,0},{12,4},{1,9},{5,13},{9,1},{13,5},{2,10},{6,14},... | collective-permute-start | bytes 589832 | tf_op jit(solution)/shard_map/ppermute | solution.py:219
  26.7 16.3 %collective-permute-start.5 = (f32[1,4,12,8,128]{4,3,2,1,0:T(8,128)S(1)}, f32[1,4,12,8,128]{4,3,2,1,0:T(8,128)S(1)}, u32[]{:S(2)}, u32[]{:S(2)}) collective-permute-start(f32[1,4,12,8,128]{4,3,2,1,0:T(8,128)S(1)} %get-tuple-element.43), channel_id=1, source_target_pairs={{0,4},{4,0},{8,12},{12,8},{1,5},{5,1},{9,13},{13,9},{2,6},{6,2},{1... | collective-permute-start | bytes 589832 | tf_op jit(solution)/shard_map/ppermute | solution.py:219
  29.9 20.3 %collective-permute-start.14 = (f32[16,7,8,128]{3,2,1,0:T(8,128)}, f32[16,7,8,128]{3,2,1,0:T(8,128)S(1)}, u32[]{:S(2)}, u32[]{:S(2)}) collective-permute-start(f32[16,7,8,128]{3,2,1,0:T(8,128)} %get-tuple-element.78), channel_id=1, source_target_pairs={{1,0},{2,1},{3,2},{7,3},{6,7},{5,6},{4,5},{8,4},{9,8},{10,9},{11,1... | collective-permute-start | bytes 1376264 | tf_op jit(solution)/shard_map/ppermute | solution.py:250
  33.1 17.2 %collective-permute-start.15 = (f32[16,7,8,128]{3,2,1,0:T(8,128)S(1)}, f32[16,7,8,128]{3,2,1,0:T(8,128)S(1)}, u32[]{:S(2)}, u32[]{:S(2)}) collective-permute-start(f32[16,7,8,128]{3,2,1,0:T(8,128)S(1)} %get-tuple-element.77), channel_id=1, source_target_pairs={{0,1},{1,2},{2,3},{3,7},{7,6},{6,5},{5,4},{4,8},{8,9},{9,10},{10,1... | collective-permute-start | bytes 1376264 | tf_op jit(solution)/shard_map/ppermute | solution.py:251
  44.2 12.9 %collective-permute-start.6 = (f32[16,6,8,128]{3,2,1,0:T(8,128)}, f32[16,6,8,128]{3,2,1,0:T(8,128)S(1)}, u32[]{:S(2)}, u32[]{:S(2)}) collective-permute-start(f32[16,6,8,128]{3,2,1,0:T(8,128)} %get-tuple-element.36), channel_id=1, source_target_pairs={{1,0},{2,1},{3,2},{7,3},{6,7},{5,6},{4,5},{8,4},{9,8},{10,9},{11,1... | collective-permute-start | bytes 1179656 | tf_op jit(solution)/shard_map/ppermute | solution.py:250
  46.1 14.7 %collective-permute-start.7 = (f32[16,6,8,128]{3,2,1,0:T(8,128)}, f32[16,6,8,128]{3,2,1,0:T(8,128)S(1)}, u32[]{:S(2)}, u32[]{:S(2)}) collective-permute-start(f32[16,6,8,128]{3,2,1,0:T(8,128)} %get-tuple-element.35), channel_id=1, source_target_pairs={{0,1},{1,2},{2,3},{3,7},{7,6},{6,5},{5,4},{4,8},{8,9},{9,10},{10,1... | collective-permute-start | bytes 1179656 | tf_op jit(solution)/shard_map/ppermute | solution.py:251
  50.2 10.6 %copy-start.1 = (s32[64,9]{0,1:T(8,128)S(1)}, s32[64,9]{0,1:T(8,128)}, u32[]{:S(2)}) copy-start(s32[64,9]{0,1:T(8,128)} %param.6) | copy-start | bytes 6916
  50.2 10.6 %copy-start.2 = (s32[64,5]{0,1:T(8,128)S(1)}, s32[64,5]{0,1:T(8,128)}, u32[]{:S(2)}) copy-start(s32[64,5]{0,1:T(8,128)} %param.7) | copy-start | bytes 3844
  64.6 8.7 %collective-permute-start.20 = (f32[1,4,9,8,128]{4,3,2,1,0:T(8,128)S(1)}, f32[1,4,9,8,128]{4,3,2,1,0:T(8,128)S(1)}, u32[]{:S(2)}, u32[]{:S(2)}) collective-permute-start(f32[1,4,9,8,128]{4,3,2,1,0:T(8,128)S(1)} %get-tuple-element.73), channel_id=1, source_target_pairs={{0,12},{4,8},{8,4},{12,0},{1,13},{5,9},{9,5},{13,1},{2,14},{6,10},... | collective-permute-start | bytes 442376 | tf_op jit(solution)/shard_map/ppermute | solution.py:219
  64.7 12.9 %collective-permute-start.21 = (f32[1,4,9,8,128]{4,3,2,1,0:T(8,128)S(1)}, f32[1,4,9,8,128]{4,3,2,1,0:T(8,128)S(1)}, u32[]{:S(2)}, u32[]{:S(2)}) collective-permute-start(f32[1,4,9,8,128]{4,3,2,1,0:T(8,128)S(1)} %get-tuple-element.76), channel_id=1, source_target_pairs={{0,8},{4,12},{8,0},{12,4},{1,9},{5,13},{9,1},{13,5},{2,10},{6,14},... | collective-permute-start | bytes 442376 | tf_op jit(solution)/shard_map/ppermute | solution.py:219
  65.0 12.6 %collective-permute-start.22 = (f32[1,4,9,8,128]{4,3,2,1,0:T(8,128)S(1)}, f32[1,4,9,8,128]{4,3,2,1,0:T(8,128)S(1)}, u32[]{:S(2)}, u32[]{:S(2)}) collective-permute-start(f32[1,4,9,8,128]{4,3,2,1,0:T(8,128)S(1)} %get-tuple-element.75), channel_id=1, source_target_pairs={{0,4},{4,0},{8,12},{12,8},{1,5},{5,1},{9,13},{13,9},{2,6},{6,2},{1... | collective-permute-start | bytes 442376 | tf_op jit(solution)/shard_map/ppermute | solution.py:219
  69.1 10.0 %collective-permute-start.16 = (f32[4,1,11,8,128]{4,3,2,1,0:T(8,128)S(1)}, f32[4,1,11,8,128]{4,3,2,1,0:T(8,128)S(1)}, u32[]{:S(2)}, u32[]{:S(2)}) collective-permute-start(f32[4,1,11,8,128]{4,3,2,1,0:T(8,128)S(1)} %get-tuple-element.61), channel_id=1, source_target_pairs={{0,3},{1,2},{2,1},{3,0},{4,7},{5,6},{6,5},{7,4},{8,11},{9,10},{10,... | collective-permute-start | bytes 540680 | tf_op jit(solution)/shard_map/ppermute | solution.py:219
  69.2 9.9 %collective-permute-start.17 = (f32[4,1,11,8,128]{4,3,2,1,0:T(8,128)S(1)}, f32[4,1,11,8,128]{4,3,2,1,0:T(8,128)S(1)}, u32[]{:S(2)}, u32[]{:S(2)}) collective-permute-start(f32[4,1,11,8,128]{4,3,2,1,0:T(8,128)S(1)} %get-tuple-element.64), channel_id=1, source_target_pairs={{0,2},{1,3},{2,0},{3,1},{4,6},{5,7},{6,4},{7,5},{8,10},{9,11},{10,... | collective-permute-start | bytes 540680 | tf_op jit(solution)/shard_map/ppermute | solution.py:219
  73.2 6.5 %collective-permute-start.18 = (f32[4,1,11,8,128]{4,3,2,1,0:T(8,128)S(1)}, f32[4,1,11,8,128]{4,3,2,1,0:T(8,128)S(1)}, u32[]{:S(2)}, u32[]{:S(2)}) collective-permute-start(f32[4,1,11,8,128]{4,3,2,1,0:T(8,128)S(1)} %get-tuple-element.63), channel_id=1, source_target_pairs={{0,1},{1,0},{2,3},{3,2},{4,5},{5,4},{6,7},{7,6},{8,9},{9,8},{10,11... | collective-permute-start | bytes 540680 | tf_op jit(solution)/shard_map/ppermute | solution.py:219
  80.0 7.5 %collective-permute-start.19 = (f32[1,4,11,8,128]{4,3,2,1,0:T(8,128)S(1)}, f32[1,4,11,8,128]{4,3,2,1,0:T(8,128)S(1)}, u32[]{:S(2)}, u32[]{:S(2)}) collective-permute-start(f32[1,4,11,8,128]{4,3,2,1,0:T(8,128)S(1)} %get-tuple-element.56), channel_id=1, source_target_pairs={{0,4},{4,0},{8,12},{12,8},{1,5},{5,1},{9,13},{13,9},{2,6},{6,2},{1... | collective-permute-start | bytes 540680 | tf_op jit(solution)/shard_map/ppermute | solution.py:219
  81.1 10.7 %collective-permute-start.26 = (f32[1,4,11,8,128]{4,3,2,1,0:T(8,128)S(1)}, f32[1,4,11,8,128]{4,3,2,1,0:T(8,128)S(1)}, u32[]{:S(2)}, u32[]{:S(2)}) collective-permute-start(f32[1,4,11,8,128]{4,3,2,1,0:T(8,128)S(1)} %get-tuple-element.53), channel_id=1, source_target_pairs={{0,12},{4,8},{8,4},{12,0},{1,13},{5,9},{9,5},{13,1},{2,14},{6,10},... | collective-permute-start | bytes 540680 | tf_op jit(solution)/shard_map/ppermute | solution.py:219
  84.6 13.8 %collective-permute-start.27 = (f32[1,4,11,8,128]{4,3,2,1,0:T(8,128)S(1)}, f32[1,4,11,8,128]{4,3,2,1,0:T(8,128)S(1)}, u32[]{:S(2)}, u32[]{:S(2)}) collective-permute-start(f32[1,4,11,8,128]{4,3,2,1,0:T(8,128)S(1)} %get-tuple-element.55), channel_id=1, source_target_pairs={{0,8},{4,12},{8,0},{12,4},{1,9},{5,13},{9,1},{13,5},{2,10},{6,14},... | collective-permute-start | bytes 540680 | tf_op jit(solution)/shard_map/ppermute | solution.py:219
  87.6 10.8 %collective-permute-start.24 = (f32[4,1,9,8,128]{4,3,2,1,0:T(8,128)S(1)}, f32[4,1,9,8,128]{4,3,2,1,0:T(8,128)S(1)}, u32[]{:S(2)}, u32[]{:S(2)}) collective-permute-start(f32[4,1,9,8,128]{4,3,2,1,0:T(8,128)S(1)} %get-tuple-element.68), channel_id=1, source_target_pairs={{0,2},{1,3},{2,0},{3,1},{4,6},{5,7},{6,4},{7,5},{8,10},{9,11},{10,... | collective-permute-start | bytes 442376 | tf_op jit(solution)/shard_map/ppermute | solution.py:219
  87.7 10.8 %collective-permute-start.25 = (f32[4,1,9,8,128]{4,3,2,1,0:T(8,128)S(1)}, f32[4,1,9,8,128]{4,3,2,1,0:T(8,128)S(1)}, u32[]{:S(2)}, u32[]{:S(2)}) collective-permute-start(f32[4,1,9,8,128]{4,3,2,1,0:T(8,128)S(1)} %get-tuple-element.67), channel_id=1, source_target_pairs={{0,1},{1,0},{2,3},{3,2},{4,5},{5,4},{6,7},{7,6},{8,9},{9,8},{10,11... | collective-permute-start | bytes 442376 | tf_op jit(solution)/shard_map/ppermute | solution.py:219
  88.8 9.7 %collective-permute-start.23 = (f32[4,1,9,8,128]{4,3,2,1,0:T(8,128)S(1)}, f32[4,1,9,8,128]{4,3,2,1,0:T(8,128)S(1)}, u32[]{:S(2)}, u32[]{:S(2)}) collective-permute-start(f32[4,1,9,8,128]{4,3,2,1,0:T(8,128)S(1)} %get-tuple-element.65), channel_id=1, source_target_pairs={{0,3},{1,2},{2,1},{3,0},{4,7},{5,6},{6,5},{7,4},{8,11},{9,10},{10,... | collective-permute-start | bytes 442376 | tf_op jit(solution)/shard_map/ppermute | solution.py:219

commit v6 on v5

--- a/solution.py
+++ b/solution.py
@@ -223,14 +223,42 @@
     return [lax.dynamic_slice_in_dim(value, far ^ k, 1, dim) for k in range(value.shape[dim])]
 
 
-def join(pieces, dim, near):
-    stack = jnp.concatenate(pieces[::-1], axis=dim)
-    last = len(pieces) - 1
+def join(pieces, dim, near, early_first=True):
+    stack = jnp.concatenate(pieces[::-1] if early_first else pieces, axis=dim)
+    last = (len(pieces) - 1) * early_first
     return jnp.concatenate([lax.dynamic_slice_in_dim(stack, near ^ j ^ last, 1, dim) for j in range(len(pieces))], axis=dim)
 
 
 def swap(value, axis, dim, near, far):
     return join(send(cut(value, dim, far), axis), dim, near)
+
+
+def gather_kernel(by_col, before_part, after_part, *refs):
+    pieces, (whole, to_before, to_after) = refs[:4], refs[4:]
+    row, col, depth = place()
+    for k, piece in enumerate(pieces):
+        for other in range(4):
+            if by_col:
+                value, layer = piece[0, other], (col ^ k) * 4 + other
+            else:
+                value, layer = piece[other, 0], other * 4 + (depth ^ k)
+            whole[layer] = value
+            to_before[layer] = value[before_part]
+            to_after[layer] = value[after_part]
+
+
+def gather(pieces, by_col, before_part, after_part):
+    vmem = pl.BlockSpec(memory_space=pltpu.VMEM)
+    count = pieces[0].shape[2]
+    counts = (count, before_part.stop - before_part.start, after_part.stop - after_part.start)
+    return pl.pallas_call(
+        functools.partial(gather_kernel, by_col, before_part, after_part),
+        out_shape=[jax.ShapeDtypeStruct((16, n, 8, BLK), jnp.float32) for n in counts],
+        in_specs=[vmem] * 4,
+        out_specs=[vmem] * 3,
+        compiler_params=pltpu.CompilerParams(vmem_limit_bytes=16 * 1024 * 1024),
+        cost_estimate=pl.CostEstimate(flops=0, bytes_accessed=0, transcendentals=0),
+    )(*pieces)
 
 
 def chain(rows):
@@ -246,24 +274,24 @@
     up = list(zip(order[:-1], order[1:]))
     down = list(zip(order[1:], order[:-1]))
 
-    def halo(group, before_part, after_part):
-        after = lax.ppermute(group[:, before_part], EVERY, down)
-        before = lax.ppermute(group[:, after_part], EVERY, up)
+    def halo(to_before, to_after):
+        after = lax.ppermute(to_before, EVERY, down)
+        before = lax.ppermute(to_after, EVERY, up)
         return after, before
 
     inner, outer = pack(density, mask_band.T)
     inner = join(send(inner, "col"), 0, col)
     outer = join(send(outer, "depth"), 1, depth)
-    outer = swap(outer, "col", 0, col, col_rank)
-    inner = swap(inner, "depth", 1, depth, depth_rank)
-    inner = inner.reshape(16, len(INNER), 8, BLK)
-    outer = outer.reshape(16, len(OUTER), 8, BLK)
-    early = early_part(outer, inner, *halo(inner, INNER_TO_BEFORE, INNER_TO_AFTER))
-    late = halo(outer, OUTER_TO_BEFORE, OUTER_TO_AFTER)
+    outer = swap(outer, "col", 0, col, col_rank).reshape(16, len(OUTER), 8, BLK)
+    inner = send(cut(inner, 1, depth_rank), "depth")
+    inner, *inner_halo = gather(inner, False, INNER_TO_BEFORE, INNER_TO_AFTER)
+    outer_halo = outer[:, OUTER_TO_BEFORE], outer[:, OUTER_TO_AFTER]
+    early = early_part(outer, inner, *halo(*inner_halo))
+    late = halo(*outer_halo)
     lower, upper = late_part(*late, *early, mask_square.T, mask_out.T)
     lower = lower.reshape(4, 4, FIRST_OUT, 8, BLK)
     upper = upper.reshape(4, 4, 20 - FIRST_OUT, 8, BLK)
-    lower = swap(lower, "col", 0, col_rank, col)
+    lower = join(send(cut(lower, 0, col), "col"), 0, col_rank, False)
     upper = swap(upper, "depth", 1, depth_rank, depth)
     upper = send(cut(upper, 0, col), "col")
     upper[1], lower = lax.optimization_barrier((upper[1], lower))

time: 101 us -> 100 us (0.990)
  waiting for transfers between devices: 41.4 us -> 37.9 us
  starting transfers between devices: 44.4 us -> 47.5 us
  Pallas kernels: 7.05 us -> 8.21 us
    ppermute x24, waiting for transfers between devices: 33.1 us -> 28.6 us  [send(): lax.ppermute(pieces[k], axis, [(i, i ^ k) for i in range(size)])]
    ppermute x24, starting transfers between devices: 32.6 us -> 35.7 us  [send(): lax.ppermute(pieces[k], axis, [(i, i ^ k) for i in range(size)])]
    pallas_call x1, Pallas kernels: 2.25 us -> 3.31 us  [early_part(): pl.pallas_call(early_kernel, out_shape=(part, part, jax.ShapeDtypeStruct(...]
    ppermute x4, waiting for transfers between devices: 8.3 us -> 9.32 us  [the longest x2 9.32 us: halo(): before = lax.ppermute(to_after, EVERY, up)]
  transfers between devices with their start and end apart: 28 -> 28, of which waited for: 12 -> 14; matrix products, arithmetic and copies ran while one was open for 3% -> 2% of each run, Pallas kernels for 2% -> 3%
where the time goes in v6:
time: 100 us; the launch traced here: 99.8 us
  starting transfers between devices  47.5 us (48%)
  waiting for transfers between devices  37.9 us (38%)
  Pallas kernels  8.21 us (8%)
  local copies, waits for them, and re-layouts  3.93 us (4%)
  other arithmetic  1.76 us (2%)
    ppermute x24, starting transfers between devices, send(): lax.ppermute(pieces[k], axis, [(i, i ^ k) for i in range(size)])  35.7 us
    ppermute x24, waiting for transfers between devices, send(): lax.ppermute(pieces[k], axis, [(i, i ^ k) for i in range(size)])  28.6 us
    ppermute x2, waiting for transfers between devices, halo(): before = lax.ppermute(to_after, EVERY, up)  9.32 us
    ppermute x2, starting transfers between devices, halo(): before = lax.ppermute(to_after, EVERY, up)  6.2 us
    ppermute x2, starting transfers between devices, halo(): after = lax.ppermute(to_before, EVERY, down)  5.66 us
    pallas_call x1, Pallas kernels, late_part(): pl.pallas_call(late_kernel, out_shape=[jax.ShapeDtypeStruct((16, count, 8...  3.7 us
    pallas_call x1, Pallas kernels, early_part(): pl.pallas_call(early_kernel, out_shape=(part, part, jax.ShapeDtypeStruct(...  3.31 us
    unnamed x14, local copies, waits for them, and re-layouts  2.08 us
  transfers between devices with their start and end apart: 28, of which 14 were waited for; matrix products, arithmetic and copies ran while one was open for 2% of the time, Pallas kernels for 3%

profile of v6, /device:TPU:2, one launch (start us, length us, event | category | flops | bytes accessed | tf_op | source)
XLA Modules:
  0.0 99.8 jit_solution(6384911805378984682)
XLA Ops:
  0.0 1.3 %copy-done = f32[64,5,8,128]{3,2,1,0:T(8,128)S(1)} copy-done((f32[64,5,8,128]{3,2,1,0:T(8,128)S(1)}, f32[64,5,8,128]{3,2,1,0:T(8,128)}, u32[]{:S(2)}) %copy-start) | copy-done | bytes 1310744
  1.3 0.7 copy-done.3
  2.0 1.1 %shard_map.46 = (f32[1,4,8,8,128]{4,3,2,1,0:T(8,128)S(1)}, f32[1,4,8,8,128]{4,3,2,1,0:T(8,128)S(1)}, f32[1,4,8,8,128]{4,3,2,1,0:T(8,128)S(1)}, f32[1,4,8,8,128]{...) custom-call(f32[64,5,8,128]{3,2,1,0:T(8,128)S(1)} %copy-done, ...), custom_call_target="tpu_custom_call" | custom-call | flops 1000000 | bytes 4194304 | tf_op jit(solution)/shard_map/pallas_call | solution.py:64
  3.1 4.7 %collective-permute-start.8 = (f32[1,4,8,8,128]{4,3,2,1,0:T(8,128)S(1)}, f32[1,4,8,8,128]{4,3,2,1,0:T(8,128)S(1)}, u32[]{:S(2)}, u32[]{:S(2)}) collective-permute-start(f32[1,4,8,8,128]{4,3,2,1,0:T(8,128)S(1)} %get-tuple-element.27), channel_id=1, source_target_pairs={{0,12},{4,8},{8,4},{12,0},{1,13},{5,9},{9,5},{13,1},{2,14},{6,10},... | collective-permute-start | bytes 393224 | tf_op jit(solution)/shard_map/ppermute | solution.py:219
  7.8 0.7 collective-permute-start.10
  8.5 3.0 %collective-permute-start = (f32[4,1,12,8,128]{4,3,2,1,0:T(8,128)S(1)}, f32[4,1,12,8,128]{4,3,2,1,0:T(8,128)S(1)}, u32[]{:S(2)}, u32[]{:S(2)}) collective-permute-start(f32[4,1,12,8,128]{4,3,2,1,0:T(8,128)S(1)} %get-tuple-element.23), channel_id=1, source_target_pairs={{0,3},{1,2},{2,1},{3,0},{4,7},{5,6},{6,5},{7,4},{8,11},{9,10},{10,... | collective-permute-start | bytes 589832 | tf_op jit(solution)/shard_map/ppermute | solution.py:219
  11.5 0.6 collective-permute-start.1
  12.1 0.1 collective-permute-done.8
  12.3 1.6 %collective-permute-start.2 = (f32[4,1,12,8,128]{4,3,2,1,0:T(8,128)S(1)}, f32[4,1,12,8,128]{4,3,2,1,0:T(8,128)S(1)}, u32[]{:S(2)}, u32[]{:S(2)}) collective-permute-start(f32[4,1,12,8,128]{4,3,2,1,0:T(8,128)S(1)} %get-tuple-element.25), channel_id=1, source_target_pairs={{0,1},{1,0},{2,3},{3,2},{4,5},{5,4},{6,7},{7,6},{8,9},{9,8},{10,11... | collective-permute-start | bytes 589832 | tf_op jit(solution)/shard_map/ppermute | solution.py:219
  13.8 4.6 %collective-permute-done.9 = f32[1,4,8,8,128]{4,3,2,1,0:T(8,128)S(1)} collective-permute-done((f32[1,4,8,8,128]{4,3,2,1,0:T(8,128)S(1)}, f32[1,4,8,8,128]{4,3,2,1,0:T(8,128)S(1)}, u32[]{:S(2)}, u32[]{:S(2)}) %collective-permute-start.9) | collective-permute-done | bytes 131104 | tf_op jit(solution)/shard_map/ppermute | solution.py:219
  18.6 1.7 %collective-permute-start.11 = (f32[4,1,8,8,128]{4,3,2,1,0:T(8,128)S(1)}, f32[4,1,8,8,128]{4,3,2,1,0:T(8,128)S(1)}, u32[]{:S(2)}, u32[]{:S(2)}) collective-permute-start(f32[4,1,8,8,128]{4,3,2,1,0:T(8,128)S(1)} %get-tuple-element.85), channel_id=1, source_target_pairs={{0,1},{1,0},{2,3},{3,2},{4,5},{5,4},{6,7},{7,6},{8,9},{9,8},{10,11... | collective-permute-start | bytes 393224 | tf_op jit(solution)/shard_map/ppermute | solution.py:219
  20.3 0.5 collective-permute-done.1
  21.1 4.5 %collective-permute-start.3 = (f32[1,4,12,8,128]{4,3,2,1,0:T(8,128)S(1)}, f32[1,4,12,8,128]{4,3,2,1,0:T(8,128)S(1)}, u32[]{:S(2)}, u32[]{:S(2)}) collective-permute-start(f32[1,4,12,8,128]{4,3,2,1,0:T(8,128)S(1)} %get-tuple-element.47), channel_id=1, source_target_pairs={{0,12},{4,8},{8,4},{12,0},{1,13},{5,9},{9,5},{13,1},{2,14},{6,10},... | collective-permute-start | bytes 589832 | tf_op jit(solution)/shard_map/ppermute | solution.py:219
  25.6 0.3 collective-permute-start.4
  25.9 0.3 collective-permute-start.5
  26.3 3.1 %collective-permute-start.12 = (f32[4,1,8,8,128]{4,3,2,1,0:T(8,128)S(1)}, f32[4,1,8,8,128]{4,3,2,1,0:T(8,128)S(1)}, u32[]{:S(2)}, u32[]{:S(2)}) collective-permute-start(f32[4,1,8,8,128]{4,3,2,1,0:T(8,128)S(1)} %get-tuple-element.84), channel_id=1, source_target_pairs={{0,2},{1,3},{2,0},{3,1},{4,6},{5,7},{6,4},{7,5},{8,10},{9,11},{10,... | collective-permute-start | bytes 393224 | tf_op jit(solution)/shard_map/ppermute | solution.py:219
  29.3 1.1 %collective-permute-start.13 = (f32[4,1,8,8,128]{4,3,2,1,0:T(8,128)S(1)}, f32[4,1,8,8,128]{4,3,2,1,0:T(8,128)S(1)}, u32[]{:S(2)}, u32[]{:S(2)}) collective-permute-start(f32[4,1,8,8,128]{4,3,2,1,0:T(8,128)S(1)} %get-tuple-element.83), channel_id=1, source_target_pairs={{0,3},{1,2},{2,1},{3,0},{4,7},{5,6},{6,5},{7,4},{8,11},{9,10},{10,... | collective-permute-start | bytes 393224 | tf_op jit(solution)/shard_map/ppermute | solution.py:219
  30.4 2.3 %collective-permute-done.12.refs_2_ = f32[4,1,8,8,128]{4,3,2,1,0:T(8,128)S(1)} collective-permute-done((f32[4,1,8,8,128]{4,3,2,1,0:T(8,128)S(1)}, f32[4,1,8,8,128]{4,3,2,1,0:T(8,128)S(1)}, u32[]{:S(2)}, u32[]{:S(2)}) %collective-permute-start.12) | collective-permute-done | bytes 131104 | tf_op jit(solution)/shard_map/ppermute | solution.py:219
  32.7 2.8 %collective-permute-done.13.refs_3_ = f32[4,1,8,8,128]{4,3,2,1,0:T(8,128)S(1)} collective-permute-done((f32[4,1,8,8,128]{4,3,2,1,0:T(8,128)S(1)}, f32[4,1,8,8,128]{4,3,2,1,0:T(8,128)S(1)}, u32[]{:S(2)}, u32[]{:S(2)}) %collective-permute-start.13) | collective-permute-done | bytes 131104 | tf_op jit(solution)/shard_map/ppermute | solution.py:219
  35.5 0.1 shard_map.47
  35.6 1.9 %collective-permute-start.14 = (f32[16,7,8,128]{3,2,1,0:T(8,128)S(1)}, f32[16,7,8,128]{3,2,1,0:T(8,128)S(1)}, u32[]{:S(2)}, u32[]{:S(2)}) collective-permute-start(f32[16,7,8,128]{3,2,1,0:T(8,128)S(1)} %get-tuple-element.32), channel_id=1, source_target_pairs={{1,0},{2,1},{3,2},{7,3},{6,7},{5,6},{4,5},{8,4},{9,8},{10,9},{11,1... | collective-permute-start | bytes 1376264 | tf_op jit(solution)/shard_map/ppermute | solution.py:278
  37.6 3.9 %collective-permute-start.15 = (f32[16,7,8,128]{3,2,1,0:T(8,128)S(1)}, f32[16,7,8,128]{3,2,1,0:T(8,128)}, u32[]{:S(2)}, u32[]{:S(2)}) collective-permute-start(f32[16,7,8,128]{3,2,1,0:T(8,128)S(1)} %get-tuple-element.33), channel_id=1, source_target_pairs={{0,1},{1,2},{2,3},{3,7},{7,6},{6,5},{5,4},{4,8},{8,9},{9,10},{10,1... | collective-permute-start | bytes 1376264 | tf_op jit(solution)/shard_map/ppermute | solution.py:279
  41.7 0.9 fusion
  42.7 3.7 %collective-permute-start.6 = (f32[16,6,8,128]{3,2,1,0:T(8,128)}, f32[16,6,8,128]{3,2,1,0:T(8,128)S(1)}, u32[]{:S(2)}, u32[]{:S(2)}) collective-permute-start(f32[16,6,8,128]{3,2,1,0:T(8,128)} %get-tuple-element.42), channel_id=1, source_target_pairs={{1,0},{2,1},{3,2},{7,3},{6,7},{5,6},{4,5},{8,4},{9,8},{10,9},{11,1... | collective-permute-start | bytes 1179656 | tf_op jit(solution)/shard_map/ppermute | solution.py:278
  46.4 2.3 %collective-permute-start.7 = (f32[16,6,8,128]{3,2,1,0:T(8,128)}, f32[16,6,8,128]{3,2,1,0:T(8,128)S(1)}, u32[]{:S(2)}, u32[]{:S(2)}) collective-permute-start(f32[16,6,8,128]{3,2,1,0:T(8,128)} %get-tuple-element.41), channel_id=1, source_target_pairs={{0,1},{1,2},{2,3},{3,7},{7,6},{6,5},{5,4},{4,8},{8,9},{9,10},{10,1... | collective-permute-start | bytes 1179656 | tf_op jit(solution)/shard_map/ppermute | solution.py:279
  48.7 5.8 %collective-permute-done.15.inner_before = f32[16,7,8,128]{3,2,1,0:T(8,128)} collective-permute-done((f32[16,7,8,128]{3,2,1,0:T(8,128)S(1)}, f32[16,7,8,128]{3,2,1,0:T(8,128)}, u32[]{:S(2)}, u32[]{:S(2)}) %collective-permute-start.15) | collective-permute-done | bytes 458784 | tf_op jit(solution)/shard_map/ppermute | solution.py:279
  54.6 3.3 %shard_map.48 = (bf16[1536,1536]{1,0:T(8,128)(2,1)S(1)}, bf16[1536,1536]{1,0:T(8,128)(2,1)S(1)}, f32[2,256,1280]{2,1,0:T(8,128)S(1)}) custom-call(f32[16,12,8,128]{3,2,1,0:T(8,128)S(1)} %bitcast.13, f32[16,8,8,128]{3,2,1,0:T(8,128)S(1)} %get-tuple-element.31.inner, f32[16,7,8,128]{3,2,1,0:T(8,128)S(1)} %collective-permute-done.14.inner_after, ...), custom_call_target="tpu_custom_call" | custom-call | flops 1811939328 | bytes 16777216 | tf_op jit(solution)/shard_map/pallas_call | solution.py:133
  57.9 3.5 %collective-permute-done.7.before = f32[16,6,8,128]{3,2,1,0:T(8,128)S(1)} collective-permute-done((f32[16,6,8,128]{3,2,1,0:T(8,128)}, f32[16,6,8,128]{3,2,1,0:T(8,128)S(1)}, u32[]{:S(2)}, u32[]{:S(2)}) %collective-permute-start.7) | collective-permute-done | bytes 393248 | tf_op jit(solution)/shard_map/ppermute | solution.py:279
  61.4 3.7 %shard_map.49 = (f32[16,9,8,128]{3,2,1,0:T(8,128)S(1)}, f32[16,11,8,128]{3,2,1,0:T(8,128)S(1)}, bf16[1536,1536]{1,0:T(8,128)(2,1)S(1)}, bf16[1536,1536]{1,0:T(8,128)(2,1)S(1)}) custom-call(f32[16,6,8,128]{3,2,1,0:T(8,128)S(1)} %collective-permute-done.6.after, ...), custom_call_target="tpu_custom_call", output_to_operand_aliasing={{2}: (2, {}), {3}: (3, {})} | custom-call | flops 2214592512 | bytes 4194304 | tf_op jit(solution)/shard_map/pallas_call | solution.py:205
  65.1 0.1 collective-permute-start.20
  65.3 0.1 collective-permute-start.21
  65.4 4.3 %collective-permute-start.22 = (f32[1,4,9,8,128]{4,3,2,1,0:T(8,128)S(1)}, f32[1,4,9,8,128]{4,3,2,1,0:T(8,128)S(1)}, u32[]{:S(2)}, u32[]{:S(2)}) collective-permute-start(f32[1,4,9,8,128]{4,3,2,1,0:T(8,128)S(1)} %get-tuple-element.80), channel_id=1, source_target_pairs={{0,12},{4,8},{8,4},{12,0},{1,13},{5,9},{9,5},{13,1},{2,14},{6,10},... | collective-permute-start | bytes 442376 | tf_op jit(solution)/shard_map/ppermute | solution.py:219
  69.7 0.3 collective-permute-start.16
  70.0 2.3 %collective-permute-done.20 = f32[1,4,9,8,128]{4,3,2,1,0:T(8,128)S(1)} collective-permute-done((f32[1,4,9,8,128]{4,3,2,1,0:T(8,128)S(1)}, f32[1,4,9,8,128]{4,3,2,1,0:T(8,128)S(1)}, u32[]{:S(2)}, u32[]{:S(2)}) %collective-permute-start.20) | collective-permute-done | bytes 147488 | tf_op jit(solution)/shard_map/ppermute | solution.py:219
  72.3 1.6 %collective-permute-start.18 = (f32[4,1,11,8,128]{4,3,2,1,0:T(8,128)S(1)}, f32[4,1,11,8,128]{4,3,2,1,0:T(8,128)S(1)}, u32[]{:S(2)}, u32[]{:S(2)}) collective-permute-start(f32[4,1,11,8,128]{4,3,2,1,0:T(8,128)S(1)} %get-tuple-element.69), channel_id=1, source_target_pairs={{0,1},{1,0},{2,3},{3,2},{4,5},{5,4},{6,7},{7,6},{8,9},{9,8},{10,11... | collective-permute-start | bytes 540680 | tf_op jit(solution)/shard_map/ppermute | solution.py:219
  73.9 4.5 %collective-permute-done.21 = f32[1,4,9,8,128]{4,3,2,1,0:T(8,128)S(1)} collective-permute-done((f32[1,4,9,8,128]{4,3,2,1,0:T(8,128)S(1)}, f32[1,4,9,8,128]{4,3,2,1,0:T(8,128)S(1)}, u32[]{:S(2)}, u32[]{:S(2)}) %collective-permute-start.21) | collective-permute-done | bytes 147488 | tf_op jit(solution)/shard_map/ppermute | solution.py:219
  78.5 0.7 collective-permute-done.16
  79.1 0.7 collective-permute-done.18
  80.1 1.1 %collective-permute-start.19 = (f32[1,4,11,8,128]{4,3,2,1,0:T(8,128)S(1)}, f32[1,4,11,8,128]{4,3,2,1,0:T(8,128)S(1)}, u32[]{:S(2)}, u32[]{:S(2)}) collective-permute-start(f32[1,4,11,8,128]{4,3,2,1,0:T(8,128)S(1)} %get-tuple-element.62), channel_id=1, source_target_pairs={{0,4},{4,0},{8,12},{12,8},{1,5},{5,1},{9,13},{13,9},{2,6},{6,2},{1... | collective-permute-start | bytes 540680 | tf_op jit(solution)/shard_map/ppermute | solution.py:219
  81.2 1.4 %collective-permute-start.26 = (f32[1,4,11,8,128]{4,3,2,1,0:T(8,128)S(1)}, f32[1,4,11,8,128]{4,3,2,1,0:T(8,128)S(1)}, u32[]{:S(2)}, u32[]{:S(2)}) collective-permute-start(f32[1,4,11,8,128]{4,3,2,1,0:T(8,128)S(1)} %get-tuple-element.59), channel_id=1, source_target_pairs={{0,12},{4,8},{8,4},{12,0},{1,13},{5,9},{9,5},{13,1},{2,14},{6,10},... | collective-permute-start | bytes 540680 | tf_op jit(solution)/shard_map/ppermute | solution.py:219
  82.7 1.1 %collective-permute-start.27 = (f32[1,4,11,8,128]{4,3,2,1,0:T(8,128)S(1)}, f32[1,4,11,8,128]{4,3,2,1,0:T(8,128)S(1)}, u32[]{:S(2)}, u32[]{:S(2)}) collective-permute-start(f32[1,4,11,8,128]{4,3,2,1,0:T(8,128)S(1)} %get-tuple-element.61), channel_id=1, source_target_pairs={{0,8},{4,12},{8,0},{12,4},{1,9},{5,13},{9,1},{13,5},{2,10},{6,14},... | collective-permute-start | bytes 540680 | tf_op jit(solution)/shard_map/ppermute | solution.py:219
  83.8 5.9 %collective-permute-done.19 = f32[1,4,11,8,128]{4,3,2,1,0:T(8,128)S(1)} collective-permute-done((f32[1,4,11,8,128]{4,3,2,1,0:T(8,128)S(1)}, f32[1,4,11,8,128]{4,3,2,1,0:T(8,128)S(1)}, u32[]{:S(2)}, u32[]{:S(2)}) %collective-permute-start.19) | collective-permute-done | bytes 180256 | tf_op jit(solution)/shard_map/ppermute | solution.py:219
  89.8 0.1 collective-permute-start.24
  89.9 2.0 %collective-permute-start.25 = (f32[4,1,9,8,128]{4,3,2,1,0:T(8,128)S(1)}, f32[4,1,9,8,128]{4,3,2,1,0:T(8,128)S(1)}, u32[]{:S(2)}, u32[]{:S(2)}) collective-permute-start(f32[4,1,9,8,128]{4,3,2,1,0:T(8,128)S(1)} %get-tuple-element.73), channel_id=1, source_target_pairs={{0,1},{1,0},{2,3},{3,2},{4,5},{5,4},{6,7},{7,6},{8,9},{9,8},{10,11... | collective-permute-start | bytes 442376 | tf_op jit(solution)/shard_map/ppermute | solution.py:219
  91.9 2.0 %collective-permute-start.23 = (f32[4,1,9,8,128]{4,3,2,1,0:T(8,128)S(1)}, f32[4,1,9,8,128]{4,3,2,1,0:T(8,128)S(1)}, u32[]{:S(2)}, u32[]{:S(2)}) collective-permute-start(f32[4,1,9,8,128]{4,3,2,1,0:T(8,128)S(1)} %get-tuple-element.71), channel_id=1, source_target_pairs={{0,3},{1,2},{2,1},{3,0},{4,7},{5,6},{6,5},{7,4},{8,11},{9,10},{10,... | collective-permute-start | bytes 442376 | tf_op jit(solution)/shard_map/ppermute | solution.py:219
  94.0 3.7 %collective-permute-done.27 = f32[1,4,11,8,128]{4,3,2,1,0:T(8,128)S(1)} collective-permute-done((f32[1,4,11,8,128]{4,3,2,1,0:T(8,128)S(1)}, f32[1,4,11,8,128]{4,3,2,1,0:T(8,128)S(1)}, u32[]{:S(2)}, u32[]{:S(2)}) %collective-permute-start.27) | collective-permute-done | bytes 180256 | tf_op jit(solution)/shard_map/ppermute | solution.py:219
  97.9 0.4 collective-permute-done.23
  98.6 1.2 %maximum_maximum_fusion = f32[4,4,20,8,128]{4,3,2,1,0:T(8,128)} fusion(f32[1,4,11,8,128]{4,3,2,1,0:T(8,128)S(1)} %get-tuple-element.56, f32[1,4,11,8,128]{4,3,2,1,0:T(8,128)S(1)} %get-tuple-element.57, f32[1,4,11,8,128]{4,3,2,1,0:T(8,128)S(1)} %get-tuple-element.58, f32[1,4,11,8,128]{4,3,2,1,0:T(8,128)S(1)} %get-tuple-element.55, ...), kind=kLoop, calls=%fused_computation | loop fusion | flops 1310720 | bytes 2621440 | tf_op jit(solution)/shard_map/concatenate | solution.py:302
  (62 shorter events, 1.6 us)
Async XLA Ops:
  0.0 1.3 %copy-start = (f32[64,5,8,128]{3,2,1,0:T(8,128)S(1)}, f32[64,5,8,128]{3,2,1,0:T(8,128)}, u32[]{:S(2)}) copy-start(f32[64,5,8,128]{3,2,1,0:T(8,128)} %density.1) | copy-start | bytes 3932164
  1.3 0.7 copy-start.3
  3.1 9.1 %collective-permute-start.8 = (f32[1,4,8,8,128]{4,3,2,1,0:T(8,128)S(1)}, f32[1,4,8,8,128]{4,3,2,1,0:T(8,128)S(1)}, u32[]{:S(2)}, u32[]{:S(2)}) collective-permute-start(f32[1,4,8,8,128]{4,3,2,1,0:T(8,128)S(1)} %get-tuple-element.27), channel_id=1, source_target_pairs={{0,12},{4,8},{8,4},{12,0},{1,13},{5,9},{9,5},{13,1},{2,14},{6,10},... | collective-permute-start | bytes 393224 | tf_op jit(solution)/shard_map/ppermute | solution.py:219
  7.8 10.6 %collective-permute-start.9 = (f32[1,4,8,8,128]{4,3,2,1,0:T(8,128)S(1)}, f32[1,4,8,8,128]{4,3,2,1,0:T(8,128)S(1)}, u32[]{:S(2)}, u32[]{:S(2)}) collective-permute-start(f32[1,4,8,8,128]{4,3,2,1,0:T(8,128)S(1)} %get-tuple-element.28), channel_id=1, source_target_pairs={{0,8},{4,12},{8,0},{12,4},{1,9},{5,13},{9,1},{13,5},{2,10},{6,14},... | collective-permute-start | bytes 393224 | tf_op jit(solution)/shard_map/ppermute | solution.py:219
  7.8 10.6 %collective-permute-start.10 = (f32[1,4,8,8,128]{4,3,2,1,0:T(8,128)S(1)}, f32[1,4,8,8,128]{4,3,2,1,0:T(8,128)S(1)}, u32[]{:S(2)}, u32[]{:S(2)}) collective-permute-start(f32[1,4,8,8,128]{4,3,2,1,0:T(8,128)S(1)} %get-tuple-element.29), channel_id=1, source_target_pairs={{0,4},{4,0},{8,12},{12,8},{1,5},{5,1},{9,13},{13,9},{2,6},{6,2},{1... | collective-permute-start | bytes 393224 | tf_op jit(solution)/shard_map/ppermute | solution.py:219
  8.5 11.8 %collective-permute-start = (f32[4,1,12,8,128]{4,3,2,1,0:T(8,128)S(1)}, f32[4,1,12,8,128]{4,3,2,1,0:T(8,128)S(1)}, u32[]{:S(2)}, u32[]{:S(2)}) collective-permute-start(f32[4,1,12,8,128]{4,3,2,1,0:T(8,128)S(1)} %get-tuple-element.23), channel_id=1, source_target_pairs={{0,3},{1,2},{2,1},{3,0},{4,7},{5,6},{6,5},{7,4},{8,11},{9,10},{10,... | collective-permute-start | bytes 589832 | tf_op jit(solution)/shard_map/ppermute | solution.py:219
  11.5 9.3 %collective-permute-start.1 = (f32[4,1,12,8,128]{4,3,2,1,0:T(8,128)S(1)}, f32[4,1,12,8,128]{4,3,2,1,0:T(8,128)S(1)}, u32[]{:S(2)}, u32[]{:S(2)}) collective-permute-start(f32[4,1,12,8,128]{4,3,2,1,0:T(8,128)S(1)} %get-tuple-element.24), channel_id=1, source_target_pairs={{0,2},{1,3},{2,0},{3,1},{4,6},{5,7},{6,4},{7,5},{8,10},{9,11},{10,... | collective-permute-start | bytes 589832 | tf_op jit(solution)/shard_map/ppermute | solution.py:219
  12.3 8.6 %collective-permute-start.2 = (f32[4,1,12,8,128]{4,3,2,1,0:T(8,128)S(1)}, f32[4,1,12,8,128]{4,3,2,1,0:T(8,128)S(1)}, u32[]{:S(2)}, u32[]{:S(2)}) collective-permute-start(f32[4,1,12,8,128]{4,3,2,1,0:T(8,128)S(1)} %get-tuple-element.25), channel_id=1, source_target_pairs={{0,1},{1,0},{2,3},{3,2},{4,5},{5,4},{6,7},{7,6},{8,9},{9,8},{10,11... | collective-permute-start | bytes 589832 | tf_op jit(solution)/shard_map/ppermute | solution.py:219
  18.6 10.7 %collective-permute-start.11 = (f32[4,1,8,8,128]{4,3,2,1,0:T(8,128)S(1)}, f32[4,1,8,8,128]{4,3,2,1,0:T(8,128)S(1)}, u32[]{:S(2)}, u32[]{:S(2)}) collective-permute-start(f32[4,1,8,8,128]{4,3,2,1,0:T(8,128)S(1)} %get-tuple-element.85), channel_id=1, source_target_pairs={{0,1},{1,0},{2,3},{3,2},{4,5},{5,4},{6,7},{7,6},{8,9},{9,8},{10,11... | collective-permute-start | bytes 393224 | tf_op jit(solution)/shard_map/ppermute | solution.py:219
  21.1 20.4 %collective-permute-start.3 = (f32[1,4,12,8,128]{4,3,2,1,0:T(8,128)S(1)}, f32[1,4,12,8,128]{4,3,2,1,0:T(8,128)S(1)}, u32[]{:S(2)}, u32[]{:S(2)}) collective-permute-start(f32[1,4,12,8,128]{4,3,2,1,0:T(8,128)S(1)} %get-tuple-element.47), channel_id=1, source_target_pairs={{0,12},{4,8},{8,4},{12,0},{1,13},{5,9},{9,5},{13,1},{2,14},{6,10},... | collective-permute-start | bytes 589832 | tf_op jit(solution)/shard_map/ppermute | solution.py:219
  25.6 15.9 %collective-permute-start.4 = (f32[1,4,12,8,128]{4,3,2,1,0:T(8,128)S(1)}, f32[1,4,12,8,128]{4,3,2,1,0:T(8,128)S(1)}, u32[]{:S(2)}, u32[]{:S(2)}) collective-permute-start(f32[1,4,12,8,128]{4,3,2,1,0:T(8,128)S(1)} %get-tuple-element.50), channel_id=1, source_target_pairs={{0,8},{4,12},{8,0},{12,4},{1,9},{5,13},{9,1},{13,5},{2,10},{6,14},... | collective-permute-start | bytes 589832 | tf_op jit(solution)/shard_map/ppermute | solution.py:219
  25.9 15.6 %collective-permute-start.5 = (f32[1,4,12,8,128]{4,3,2,1,0:T(8,128)S(1)}, f32[1,4,12,8,128]{4,3,2,1,0:T(8,128)S(1)}, u32[]{:S(2)}, u32[]{:S(2)}) collective-permute-start(f32[1,4,12,8,128]{4,3,2,1,0:T(8,128)S(1)} %get-tuple-element.49), channel_id=1, source_target_pairs={{0,4},{4,0},{8,12},{12,8},{1,5},{5,1},{9,13},{13,9},{2,6},{6,2},{1... | collective-permute-start | bytes 589832 | tf_op jit(solution)/shard_map/ppermute | solution.py:219
  26.3 6.5 %collective-permute-start.12 = (f32[4,1,8,8,128]{4,3,2,1,0:T(8,128)S(1)}, f32[4,1,8,8,128]{4,3,2,1,0:T(8,128)S(1)}, u32[]{:S(2)}, u32[]{:S(2)}) collective-permute-start(f32[4,1,8,8,128]{4,3,2,1,0:T(8,128)S(1)} %get-tuple-element.84), channel_id=1, source_target_pairs={{0,2},{1,3},{2,0},{3,1},{4,6},{5,7},{6,4},{7,5},{8,10},{9,11},{10,... | collective-permute-start | bytes 393224 | tf_op jit(solution)/shard_map/ppermute | solution.py:219
  29.3 6.2 %collective-permute-start.13 = (f32[4,1,8,8,128]{4,3,2,1,0:T(8,128)S(1)}, f32[4,1,8,8,128]{4,3,2,1,0:T(8,128)S(1)}, u32[]{:S(2)}, u32[]{:S(2)}) collective-permute-start(f32[4,1,8,8,128]{4,3,2,1,0:T(8,128)S(1)} %get-tuple-element.83), channel_id=1, source_target_pairs={{0,3},{1,2},{2,1},{3,0},{4,7},{5,6},{6,5},{7,4},{8,11},{9,10},{10,... | collective-permute-start | bytes 393224 | tf_op jit(solution)/shard_map/ppermute | solution.py:219
  35.6 13.1 %collective-permute-start.14 = (f32[16,7,8,128]{3,2,1,0:T(8,128)S(1)}, f32[16,7,8,128]{3,2,1,0:T(8,128)S(1)}, u32[]{:S(2)}, u32[]{:S(2)}) collective-permute-start(f32[16,7,8,128]{3,2,1,0:T(8,128)S(1)} %get-tuple-element.32), channel_id=1, source_target_pairs={{1,0},{2,1},{3,2},{7,3},{6,7},{5,6},{4,5},{8,4},{9,8},{10,9},{11,1... | collective-permute-start | bytes 1376264 | tf_op jit(solution)/shard_map/ppermute | solution.py:278
  37.6 17.0 %collective-permute-start.15 = (f32[16,7,8,128]{3,2,1,0:T(8,128)S(1)}, f32[16,7,8,128]{3,2,1,0:T(8,128)}, u32[]{:S(2)}, u32[]{:S(2)}) collective-permute-start(f32[16,7,8,128]{3,2,1,0:T(8,128)S(1)} %get-tuple-element.33), channel_id=1, source_target_pairs={{0,1},{1,2},{2,3},{3,7},{7,6},{6,5},{5,4},{4,8},{8,9},{9,10},{10,1... | collective-permute-start | bytes 1376264 | tf_op jit(solution)/shard_map/ppermute | solution.py:279
  42.7 15.2 %collective-permute-start.6 = (f32[16,6,8,128]{3,2,1,0:T(8,128)}, f32[16,6,8,128]{3,2,1,0:T(8,128)S(1)}, u32[]{:S(2)}, u32[]{:S(2)}) collective-permute-start(f32[16,6,8,128]{3,2,1,0:T(8,128)} %get-tuple-element.42), channel_id=1, source_target_pairs={{1,0},{2,1},{3,2},{7,3},{6,7},{5,6},{4,5},{8,4},{9,8},{10,9},{11,1... | collective-permute-start | bytes 1179656 | tf_op jit(solution)/shard_map/ppermute | solution.py:278
  46.4 15.0 %collective-permute-start.7 = (f32[16,6,8,128]{3,2,1,0:T(8,128)}, f32[16,6,8,128]{3,2,1,0:T(8,128)S(1)}, u32[]{:S(2)}, u32[]{:S(2)}) collective-permute-start(f32[16,6,8,128]{3,2,1,0:T(8,128)} %get-tuple-element.41), channel_id=1, source_target_pairs={{0,1},{1,2},{2,3},{3,7},{7,6},{6,5},{5,4},{4,8},{8,9},{9,10},{10,1... | collective-permute-start | bytes 1179656 | tf_op jit(solution)/shard_map/ppermute | solution.py:279
  54.5 6.8 %copy-start.1 = (s32[64,9]{0,1:T(8,128)S(1)}, s32[64,9]{0,1:T(8,128)}, u32[]{:S(2)}) copy-start(s32[64,9]{0,1:T(8,128)} %param.6) | copy-start | bytes 6916
  54.5 6.8 %copy-start.2 = (s32[64,5]{0,1:T(8,128)S(1)}, s32[64,5]{0,1:T(8,128)}, u32[]{:S(2)}) copy-start(s32[64,5]{0,1:T(8,128)} %param.7) | copy-start | bytes 3844
  65.1 7.2 %collective-permute-start.20 = (f32[1,4,9,8,128]{4,3,2,1,0:T(8,128)S(1)}, f32[1,4,9,8,128]{4,3,2,1,0:T(8,128)S(1)}, u32[]{:S(2)}, u32[]{:S(2)}) collective-permute-start(f32[1,4,9,8,128]{4,3,2,1,0:T(8,128)S(1)} %get-tuple-element.82), channel_id=1, source_target_pairs={{0,4},{4,0},{8,12},{12,8},{1,5},{5,1},{9,13},{13,9},{2,6},{6,2},{1... | collective-permute-start | bytes 442376 | tf_op jit(solution)/shard_map/ppermute | solution.py:219
  65.3 13.1 %collective-permute-start.21 = (f32[1,4,9,8,128]{4,3,2,1,0:T(8,128)S(1)}, f32[1,4,9,8,128]{4,3,2,1,0:T(8,128)S(1)}, u32[]{:S(2)}, u32[]{:S(2)}) collective-permute-start(f32[1,4,9,8,128]{4,3,2,1,0:T(8,128)S(1)} %get-tuple-element.81), channel_id=1, source_target_pairs={{0,8},{4,12},{8,0},{12,4},{1,9},{5,13},{9,1},{13,5},{2,10},{6,14},... | collective-permute-start | bytes 442376 | tf_op jit(solution)/shard_map/ppermute | solution.py:219
  65.4 13.1 %collective-permute-start.22 = (f32[1,4,9,8,128]{4,3,2,1,0:T(8,128)S(1)}, f32[1,4,9,8,128]{4,3,2,1,0:T(8,128)S(1)}, u32[]{:S(2)}, u32[]{:S(2)}) collective-permute-start(f32[1,4,9,8,128]{4,3,2,1,0:T(8,128)S(1)} %get-tuple-element.80), channel_id=1, source_target_pairs={{0,12},{4,8},{8,4},{12,0},{1,13},{5,9},{9,5},{13,1},{2,14},{6,10},... | collective-permute-start | bytes 442376 | tf_op jit(solution)/shard_map/ppermute | solution.py:219
  69.7 9.4 %collective-permute-start.16 = (f32[4,1,11,8,128]{4,3,2,1,0:T(8,128)S(1)}, f32[4,1,11,8,128]{4,3,2,1,0:T(8,128)S(1)}, u32[]{:S(2)}, u32[]{:S(2)}) collective-permute-start(f32[4,1,11,8,128]{4,3,2,1,0:T(8,128)S(1)} %get-tuple-element.67), channel_id=1, source_target_pairs={{0,3},{1,2},{2,1},{3,0},{4,7},{5,6},{6,5},{7,4},{8,11},{9,10},{10,... | collective-permute-start | bytes 540680 | tf_op jit(solution)/shard_map/ppermute | solution.py:219
  70.0 9.1 %collective-permute-start.17 = (f32[4,1,11,8,128]{4,3,2,1,0:T(8,128)S(1)}, f32[4,1,11,8,128]{4,3,2,1,0:T(8,128)S(1)}, u32[]{:S(2)}, u32[]{:S(2)}) collective-permute-start(f32[4,1,11,8,128]{4,3,2,1,0:T(8,128)S(1)} %get-tuple-element.70), channel_id=1, source_target_pairs={{0,2},{1,3},{2,0},{3,1},{4,6},{5,7},{6,4},{7,5},{8,10},{9,11},{10,... | collective-permute-start | bytes 540680 | tf_op jit(solution)/shard_map/ppermute | solution.py:219
  72.3 7.5 %collective-permute-start.18 = (f32[4,1,11,8,128]{4,3,2,1,0:T(8,128)S(1)}, f32[4,1,11,8,128]{4,3,2,1,0:T(8,128)S(1)}, u32[]{:S(2)}, u32[]{:S(2)}) collective-permute-start(f32[4,1,11,8,128]{4,3,2,1,0:T(8,128)S(1)} %get-tuple-element.69), channel_id=1, source_target_pairs={{0,1},{1,0},{2,3},{3,2},{4,5},{5,4},{6,7},{7,6},{8,9},{9,8},{10,11... | collective-permute-start | bytes 540680 | tf_op jit(solution)/shard_map/ppermute | solution.py:219
  80.1 9.7 %collective-permute-start.19 = (f32[1,4,11,8,128]{4,3,2,1,0:T(8,128)S(1)}, f32[1,4,11,8,128]{4,3,2,1,0:T(8,128)S(1)}, u32[]{:S(2)}, u32[]{:S(2)}) collective-permute-start(f32[1,4,11,8,128]{4,3,2,1,0:T(8,128)S(1)} %get-tuple-element.62), channel_id=1, source_target_pairs={{0,4},{4,0},{8,12},{12,8},{1,5},{5,1},{9,13},{13,9},{2,6},{6,2},{1... | collective-permute-start | bytes 540680 | tf_op jit(solution)/shard_map/ppermute | solution.py:219
  81.2 12.7 %collective-permute-start.26 = (f32[1,4,11,8,128]{4,3,2,1,0:T(8,128)S(1)}, f32[1,4,11,8,128]{4,3,2,1,0:T(8,128)S(1)}, u32[]{:S(2)}, u32[]{:S(2)}) collective-permute-start(f32[1,4,11,8,128]{4,3,2,1,0:T(8,128)S(1)} %get-tuple-element.59), channel_id=1, source_target_pairs={{0,12},{4,8},{8,4},{12,0},{1,13},{5,9},{9,5},{13,1},{2,14},{6,10},... | collective-permute-start | bytes 540680 | tf_op jit(solution)/shard_map/ppermute | solution.py:219
  82.7 15.0 %collective-permute-start.27 = (f32[1,4,11,8,128]{4,3,2,1,0:T(8,128)S(1)}, f32[1,4,11,8,128]{4,3,2,1,0:T(8,128)S(1)}, u32[]{:S(2)}, u32[]{:S(2)}) collective-permute-start(f32[1,4,11,8,128]{4,3,2,1,0:T(8,128)S(1)} %get-tuple-element.61), channel_id=1, source_target_pairs={{0,8},{4,12},{8,0},{12,4},{1,9},{5,13},{9,1},{13,5},{2,10},{6,14},... | collective-permute-start | bytes 540680 | tf_op jit(solution)/shard_map/ppermute | solution.py:219
  89.8 8.1 %collective-permute-start.24 = (f32[4,1,9,8,128]{4,3,2,1,0:T(8,128)S(1)}, f32[4,1,9,8,128]{4,3,2,1,0:T(8,128)S(1)}, u32[]{:S(2)}, u32[]{:S(2)}) collective-permute-start(f32[4,1,9,8,128]{4,3,2,1,0:T(8,128)S(1)} %get-tuple-element.74), channel_id=1, source_target_pairs={{0,2},{1,3},{2,0},{3,1},{4,6},{5,7},{6,4},{7,5},{8,10},{9,11},{10,... | collective-permute-start | bytes 442376 | tf_op jit(solution)/shard_map/ppermute | solution.py:219
  89.9 8.0 %collective-permute-start.25 = (f32[4,1,9,8,128]{4,3,2,1,0:T(8,128)S(1)}, f32[4,1,9,8,128]{4,3,2,1,0:T(8,128)S(1)}, u32[]{:S(2)}, u32[]{:S(2)}) collective-permute-start(f32[4,1,9,8,128]{4,3,2,1,0:T(8,128)S(1)} %get-tuple-element.73), channel_id=1, source_target_pairs={{0,1},{1,0},{2,3},{3,2},{4,5},{5,4},{6,7},{7,6},{8,9},{9,8},{10,11... | collective-permute-start | bytes 442376 | tf_op jit(solution)/shard_map/ppermute | solution.py:219
  91.9 6.4 %collective-permute-start.23 = (f32[4,1,9,8,128]{4,3,2,1,0:T(8,128)S(1)}, f32[4,1,9,8,128]{4,3,2,1,0:T(8,128)S(1)}, u32[]{:S(2)}, u32[]{:S(2)}) collective-permute-start(f32[4,1,9,8,128]{4,3,2,1,0:T(8,128)S(1)} %get-tuple-element.71), channel_id=1, source_target_pairs={{0,3},{1,2},{2,1},{3,0},{4,7},{5,6},{6,5},{7,4},{8,11},{9,10},{10,... | collective-permute-start | bytes 442376 | tf_op jit(solution)/shard_map/ppermute | solution.py:219

commit v7 on v6

--- a/solution.py
+++ b/solution.py
@@ -17,7 +17,7 @@
 BEFORE_ONLY = [(0, s) for s in range(4)] + [(1, s) for s in range(3)]
 BOTH = [(0, 4), (1, 3), (1, 4), (2, 0), (2, 1), (3, 0)]
 AFTER_ONLY = [(2, s) for s in range(2, 5)] + [(3, s) for s in range(1, 5)]
-EARLY_SIDE = 1
+EARLY_SIDE = 2
 INNER = BEFORE_ONLY[7 - EARLY_SIDE :] + BOTH + AFTER_ONLY[:EARLY_SIDE]
 OUTER = BEFORE_ONLY[: 7 - EARLY_SIDE] + AFTER_ONLY[EARLY_SIDE:]
 INNER_TO_BEFORE, INNER_TO_AFTER = slice(0, 6 + EARLY_SIDE), slice(EARLY_SIDE, 6 + 2 * EARLY_SIDE)

time: 100 us -> 100 us (level)
  waiting for transfers between devices: 37.9 us -> 36.1 us
  starting transfers between devices: 47.5 us -> 49 us
    ppermute x2, starting transfers between devices: 5.66 us -> 9.34 us  [halo(): after = lax.ppermute(to_before, EVERY, down)]
    ppermute x2, waiting for transfers between devices: 9.32 us -> 6.2 us  [halo(): before = lax.ppermute(to_after, EVERY, up)]
    ppermute x2, starting transfers between devices: 6.2 us -> 4.02 us  [halo(): before = lax.ppermute(to_after, EVERY, up)]
    ppermute x2, waiting for transfers between devices: 0.01 us -> 1.46 us  [halo(): after = lax.ppermute(to_before, EVERY, down)]
  transfers between devices with their start and end apart: 28 -> 28, of which waited for: 14 -> 16; matrix products, arithmetic and copies ran while one was open for 2% -> 2% of each run, Pallas kernels for 3% -> 4%
where the time goes in v7:
time: 100 us
  starting transfers between devices  49 us (49%)
  waiting for transfers between devices  36.1 us (36%)
  Pallas kernels  9.02 us (9%)
  local copies, waits for them, and re-layouts  3.74 us (4%)
  other arithmetic  1.73 us (2%)
    ppermute x24, starting transfers between devices, send(): lax.ppermute(pieces[k], axis, [(i, i ^ k) for i in range(size)])  35.6 us
    ppermute x24, waiting for transfers between devices, send(): lax.ppermute(pieces[k], axis, [(i, i ^ k) for i in range(size)])  28.4 us
    ppermute x2, starting transfers between devices, halo(): after = lax.ppermute(to_before, EVERY, down)  9.34 us
    ppermute x2, waiting for transfers between devices, halo(): before = lax.ppermute(to_after, EVERY, up)  6.2 us
    ppermute x2, starting transfers between devices, halo(): before = lax.ppermute(to_after, EVERY, up)  4.02 us
    pallas_call x1, Pallas kernels, late_part(): pl.pallas_call(late_kernel, out_shape=[jax.ShapeDtypeStruct((16, count, 8...  3.7 us
    pallas_call x1, Pallas kernels, early_part(): pl.pallas_call(early_kernel, out_shape=(part, part, jax.ShapeDtypeStruct(...  3.32 us
    unnamed x14, local copies, waits for them, and re-layouts  2.09 us
  transfers between devices with their start and end apart: 28, of which 16 were waited for; matrix products, arithmetic and copies ran while one was open for 2% of the time, Pallas kernels for 4%

profile of v7, /device:TPU:2, one launch (start us, length us, event | category | flops | bytes accessed | tf_op | source)
XLA Modules:
  0.0 100.0 jit_solution(1193084921430614267)
XLA Ops:
  0.0 1.3 %copy-done = f32[64,5,8,128]{3,2,1,0:T(8,128)S(1)} copy-done((f32[64,5,8,128]{3,2,1,0:T(8,128)S(1)}, f32[64,5,8,128]{3,2,1,0:T(8,128)}, u32[]{:S(2)}) %copy-start) | copy-done | bytes 1310744
  1.3 0.7 copy-done.3
  2.0 1.1 %shard_map.46 = (f32[1,4,10,8,128]{4,3,2,1,0:T(8,128)S(1)}, f32[1,4,10,8,128]{4,3,2,1,0:T(8,128)S(1)}, f32[1,4,10,8,128]{4,3,2,1,0:T(8,128)S(1)}, f32[1,4,10,8,1...) custom-call(f32[64,5,8,128]{3,2,1,0:T(8,128)S(1)} %copy-done, ...), custom_call_target="tpu_custom_call" | custom-call | flops 1000000 | bytes 4194304 | tf_op jit(solution)/shard_map/pallas_call | solution.py:64
  3.1 4.7 %collective-permute-start.8 = (f32[1,4,10,8,128]{4,3,2,1,0:T(8,128)S(1)}, f32[1,4,10,8,128]{4,3,2,1,0:T(8,128)S(1)}, u32[]{:S(2)}, u32[]{:S(2)}) collective-permute-start(f32[1,4,10,8,128]{4,3,2,1,0:T(8,128)S(1)} %get-tuple-element.27), channel_id=1, source_target_pairs={{0,12},{4,8},{8,4},{12,0},{1,13},{5,9},{9,5},{13,1},{2,14},{6,10},... | collective-permute-start | bytes 491528 | tf_op jit(solution)/shard_map/ppermute | solution.py:219
  7.8 0.7 collective-permute-start.10
  8.5 3.0 %collective-permute-start = (f32[4,1,10,8,128]{4,3,2,1,0:T(8,128)S(1)}, f32[4,1,10,8,128]{4,3,2,1,0:T(8,128)S(1)}, u32[]{:S(2)}, u32[]{:S(2)}) collective-permute-start(f32[4,1,10,8,128]{4,3,2,1,0:T(8,128)S(1)} %get-tuple-element.23), channel_id=1, source_target_pairs={{0,3},{1,2},{2,1},{3,0},{4,7},{5,6},{6,5},{7,4},{8,11},{9,10},{10,... | collective-permute-start | bytes 491528 | tf_op jit(solution)/shard_map/ppermute | solution.py:219
  11.5 0.6 collective-permute-start.1
  12.1 0.8 collective-permute-done.8
  12.9 1.6 %collective-permute-start.2 = (f32[4,1,10,8,128]{4,3,2,1,0:T(8,128)S(1)}, f32[4,1,10,8,128]{4,3,2,1,0:T(8,128)S(1)}, u32[]{:S(2)}, u32[]{:S(2)}) collective-permute-start(f32[4,1,10,8,128]{4,3,2,1,0:T(8,128)S(1)} %get-tuple-element.25), channel_id=1, source_target_pairs={{0,1},{1,0},{2,3},{3,2},{4,5},{5,4},{6,7},{7,6},{8,9},{9,8},{10,11... | collective-permute-start | bytes 491528 | tf_op jit(solution)/shard_map/ppermute | solution.py:219
  14.5 6.7 %collective-permute-done.9 = f32[1,4,10,8,128]{4,3,2,1,0:T(8,128)S(1)} collective-permute-done((f32[1,4,10,8,128]{4,3,2,1,0:T(8,128)S(1)}, f32[1,4,10,8,128]{4,3,2,1,0:T(8,128)S(1)}, u32[]{:S(2)}, u32[]{:S(2)}) %collective-permute-start.9) | collective-permute-done | bytes 163872 | tf_op jit(solution)/shard_map/ppermute | solution.py:219
  21.4 1.7 %collective-permute-start.11 = (f32[4,1,10,8,128]{4,3,2,1,0:T(8,128)S(1)}, f32[4,1,10,8,128]{4,3,2,1,0:T(8,128)S(1)}, u32[]{:S(2)}, u32[]{:S(2)}) collective-permute-start(f32[4,1,10,8,128]{4,3,2,1,0:T(8,128)S(1)} %get-tuple-element.59), channel_id=1, source_target_pairs={{0,1},{1,0},{2,3},{3,2},{4,5},{5,4},{6,7},{7,6},{8,9},{9,8},{10,11... | collective-permute-start | bytes 491528 | tf_op jit(solution)/shard_map/ppermute | solution.py:219
  23.1 2.9 %collective-permute-start.12 = (f32[4,1,10,8,128]{4,3,2,1,0:T(8,128)S(1)}, f32[4,1,10,8,128]{4,3,2,1,0:T(8,128)S(1)}, u32[]{:S(2)}, u32[]{:S(2)}) collective-permute-start(f32[4,1,10,8,128]{4,3,2,1,0:T(8,128)S(1)} %get-tuple-element.58), channel_id=1, source_target_pairs={{0,2},{1,3},{2,0},{3,1},{4,6},{5,7},{6,4},{7,5},{8,10},{9,11},{10,... | collective-permute-start | bytes 491528 | tf_op jit(solution)/shard_map/ppermute | solution.py:219
  26.0 0.2 collective-permute-start.13
  26.5 2.8 %collective-permute-start.3 = (f32[1,4,10,8,128]{4,3,2,1,0:T(8,128)S(1)}, f32[1,4,10,8,128]{4,3,2,1,0:T(8,128)S(1)}, u32[]{:S(2)}, u32[]{:S(2)}) collective-permute-start(f32[1,4,10,8,128]{4,3,2,1,0:T(8,128)S(1)} %get-tuple-element.71), channel_id=1, source_target_pairs={{0,12},{4,8},{8,4},{12,0},{1,13},{5,9},{9,5},{13,1},{2,14},{6,10},... | collective-permute-start | bytes 491528 | tf_op jit(solution)/shard_map/ppermute | solution.py:219
  29.3 1.7 %collective-permute-start.5 = (f32[1,4,10,8,128]{4,3,2,1,0:T(8,128)S(1)}, f32[1,4,10,8,128]{4,3,2,1,0:T(8,128)S(1)}, u32[]{:S(2)}, u32[]{:S(2)}) collective-permute-start(f32[1,4,10,8,128]{4,3,2,1,0:T(8,128)S(1)} %get-tuple-element.73), channel_id=1, source_target_pairs={{0,4},{4,0},{8,12},{12,8},{1,5},{5,1},{9,13},{13,9},{2,6},{6,2},{1... | collective-permute-start | bytes 491528 | tf_op jit(solution)/shard_map/ppermute | solution.py:219
  31.0 1.9 %collective-permute-done.12.refs_2_ = f32[4,1,10,8,128]{4,3,2,1,0:T(8,128)S(1)} collective-permute-done((f32[4,1,10,8,128]{4,3,2,1,0:T(8,128)S(1)}, f32[4,1,10,8,128]{4,3,2,1,0:T(8,128)S(1)}, u32[]{:S(2)}, u32[]{:S(2)}) %collective-permute-start.12) | collective-permute-done | bytes 163872 | tf_op jit(solution)/shard_map/ppermute | solution.py:219
  32.9 2.1 %collective-permute-done.13.refs_3_ = f32[4,1,10,8,128]{4,3,2,1,0:T(8,128)S(1)} collective-permute-done((f32[4,1,10,8,128]{4,3,2,1,0:T(8,128)S(1)}, f32[4,1,10,8,128]{4,3,2,1,0:T(8,128)S(1)}, u32[]{:S(2)}, u32[]{:S(2)}) %collective-permute-start.13) | collective-permute-done | bytes 163872 | tf_op jit(solution)/shard_map/ppermute | solution.py:219
  34.9 0.9 shard_map.47
  35.8 4.6 %collective-permute-start.14 = (f32[16,8,8,128]{3,2,1,0:T(8,128)}, f32[16,8,8,128]{3,2,1,0:T(8,128)S(1)}, u32[]{:S(2)}, u32[]{:S(2)}) collective-permute-start(f32[16,8,8,128]{3,2,1,0:T(8,128)} %get-tuple-element.32), channel_id=1, source_target_pairs={{1,0},{2,1},{3,2},{7,3},{6,7},{5,6},{4,5},{8,4},{9,8},{10,9},{11,1... | collective-permute-start | bytes 1572872 | tf_op jit(solution)/shard_map/ppermute | solution.py:278
  40.4 1.9 %collective-permute-start.15 = (f32[16,8,8,128]{3,2,1,0:T(8,128)S(1)}, f32[16,8,8,128]{3,2,1,0:T(8,128)}, u32[]{:S(2)}, u32[]{:S(2)}) collective-permute-start(f32[16,8,8,128]{3,2,1,0:T(8,128)S(1)} %get-tuple-element.33), channel_id=1, source_target_pairs={{0,1},{1,2},{2,3},{3,7},{7,6},{6,5},{5,4},{4,8},{8,9},{9,10},{10,1... | collective-permute-start | bytes 1572872 | tf_op jit(solution)/shard_map/ppermute | solution.py:279
  42.3 1.0 collective-permute-done.4
  43.5 0.8 fusion
  44.3 4.8 %collective-permute-start.6 = (f32[16,5,8,128]{3,2,1,0:T(8,128)}, f32[16,5,8,128]{3,2,1,0:T(8,128)S(1)}, u32[]{:S(2)}, u32[]{:S(2)}) collective-permute-start(f32[16,5,8,128]{3,2,1,0:T(8,128)} %get-tuple-element.66), channel_id=1, source_target_pairs={{1,0},{2,1},{3,2},{7,3},{6,7},{5,6},{4,5},{8,4},{9,8},{10,9},{11,1... | collective-permute-start | bytes 983048 | tf_op jit(solution)/shard_map/ppermute | solution.py:278
  49.0 2.1 %collective-permute-start.7 = (f32[16,5,8,128]{3,2,1,0:T(8,128)S(1)}, f32[16,5,8,128]{3,2,1,0:T(8,128)S(1)}, u32[]{:S(2)}, u32[]{:S(2)}) collective-permute-start(f32[16,5,8,128]{3,2,1,0:T(8,128)S(1)} %get-tuple-element.65), channel_id=1, source_target_pairs={{0,1},{1,2},{2,3},{3,7},{7,6},{6,5},{5,4},{4,8},{8,9},{9,10},{10,1... | collective-permute-start | bytes 983048 | tf_op jit(solution)/shard_map/ppermute | solution.py:279
  51.2 1.5 %collective-permute-done.14.inner_after = f32[16,8,8,128]{3,2,1,0:T(8,128)S(1)} collective-permute-done((f32[16,8,8,128]{3,2,1,0:T(8,128)}, f32[16,8,8,128]{3,2,1,0:T(8,128)S(1)}, u32[]{:S(2)}, u32[]{:S(2)}) %collective-permute-start.14) | collective-permute-done | bytes 524320 | tf_op jit(solution)/shard_map/ppermute | solution.py:278
  52.6 5.2 %collective-permute-done.15.inner_before = f32[16,8,8,128]{3,2,1,0:T(8,128)} collective-permute-done((f32[16,8,8,128]{3,2,1,0:T(8,128)S(1)}, f32[16,8,8,128]{3,2,1,0:T(8,128)}, u32[]{:S(2)}, u32[]{:S(2)}) %collective-permute-start.15) | collective-permute-done | bytes 524320 | tf_op jit(solution)/shard_map/ppermute | solution.py:279
  57.8 3.3 %shard_map.48 = (bf16[1536,1536]{1,0:T(8,128)(2,1)S(1)}, bf16[1536,1536]{1,0:T(8,128)(2,1)S(1)}, f32[2,256,1280]{2,1,0:T(8,128)S(1)}) custom-call(f32[16,10,8,128]{3,2,1,0:T(8,128)S(1)} %bitcast.13, f32[16,10,8,128]{3,2,1,0:T(8,128)S(1)} %get-tuple-element.31.inner, f32[16,8,8,128]{3,2,1,0:T(8,128)S(1)} %collective-permute-done.14.inner_after, ...), custom_call_target="tpu_custom_call" | custom-call | flops 1811939328 | bytes 16777216 | tf_op jit(solution)/shard_map/pallas_call | solution.py:133
  61.2 1.0 %collective-permute-done.7.before = f32[16,5,8,128]{3,2,1,0:T(8,128)S(1)} collective-permute-done((f32[16,5,8,128]{3,2,1,0:T(8,128)S(1)}, f32[16,5,8,128]{3,2,1,0:T(8,128)S(1)}, u32[]{:S(2)}, u32[]{:S(2)}) %collective-permute-start.7) | collective-permute-done | bytes 327712 | tf_op jit(solution)/shard_map/ppermute | solution.py:279
  62.2 3.7 %shard_map.49 = (f32[16,9,8,128]{3,2,1,0:T(8,128)S(1)}, f32[16,11,8,128]{3,2,1,0:T(8,128)S(1)}, bf16[1536,1536]{1,0:T(8,128)(2,1)S(1)}, bf16[1536,1536]{1,0:T(8,128)(2,1)S(1)}) custom-call(f32[16,5,8,128]{3,2,1,0:T(8,128)S(1)} %collective-permute-done.6.after, ...), custom_call_target="tpu_custom_call", output_to_operand_aliasing={{2}: (2, {}), {3}: (3, {})} | custom-call | flops 2214592512 | bytes 4194304 | tf_op jit(solution)/shard_map/pallas_call | solution.py:205
  65.9 0.1 collective-permute-start.20
  66.2 4.3 %collective-permute-start.22 = (f32[1,4,9,8,128]{4,3,2,1,0:T(8,128)S(1)}, f32[1,4,9,8,128]{4,3,2,1,0:T(8,128)S(1)}, u32[]{:S(2)}, u32[]{:S(2)}) collective-permute-start(f32[1,4,9,8,128]{4,3,2,1,0:T(8,128)S(1)} %get-tuple-element.88), channel_id=1, source_target_pairs={{0,12},{4,8},{8,4},{12,0},{1,13},{5,9},{9,5},{13,1},{2,14},{6,10},... | collective-permute-start | bytes 442376 | tf_op jit(solution)/shard_map/ppermute | solution.py:219
  70.5 0.2 collective-permute-start.16
  70.7 0.7 collective-permute-done.20
  71.4 3.3 %collective-permute-start.18 = (f32[4,1,11,8,128]{4,3,2,1,0:T(8,128)S(1)}, f32[4,1,11,8,128]{4,3,2,1,0:T(8,128)S(1)}, u32[]{:S(2)}, u32[]{:S(2)}) collective-permute-start(f32[4,1,11,8,128]{4,3,2,1,0:T(8,128)S(1)} %get-tuple-element.55), channel_id=1, source_target_pairs={{0,1},{1,0},{2,3},{3,2},{4,5},{5,4},{6,7},{7,6},{8,9},{9,8},{10,11... | collective-permute-start | bytes 540680 | tf_op jit(solution)/shard_map/ppermute | solution.py:219
  74.7 3.9 %collective-permute-done.21 = f32[1,4,9,8,128]{4,3,2,1,0:T(8,128)S(1)} collective-permute-done((f32[1,4,9,8,128]{4,3,2,1,0:T(8,128)S(1)}, f32[1,4,9,8,128]{4,3,2,1,0:T(8,128)S(1)}, u32[]{:S(2)}, u32[]{:S(2)}) %collective-permute-start.21) | collective-permute-done | bytes 147488 | tf_op jit(solution)/shard_map/ppermute | solution.py:219
  78.7 0.4 collective-permute-done.16
  79.1 0.3 collective-permute-done.17
  79.4 0.7 collective-permute-done.18
  80.4 0.8 collective-permute-start.19
  81.3 1.4 %collective-permute-start.26 = (f32[1,4,11,8,128]{4,3,2,1,0:T(8,128)S(1)}, f32[1,4,11,8,128]{4,3,2,1,0:T(8,128)S(1)}, u32[]{:S(2)}, u32[]{:S(2)}) collective-permute-start(f32[1,4,11,8,128]{4,3,2,1,0:T(8,128)S(1)} %get-tuple-element.45), channel_id=1, source_target_pairs={{0,12},{4,8},{8,4},{12,0},{1,13},{5,9},{9,5},{13,1},{2,14},{6,10},... | collective-permute-start | bytes 540680 | tf_op jit(solution)/shard_map/ppermute | solution.py:219
  82.7 1.4 %collective-permute-start.27 = (f32[1,4,11,8,128]{4,3,2,1,0:T(8,128)S(1)}, f32[1,4,11,8,128]{4,3,2,1,0:T(8,128)S(1)}, u32[]{:S(2)}, u32[]{:S(2)}) collective-permute-start(f32[1,4,11,8,128]{4,3,2,1,0:T(8,128)S(1)} %get-tuple-element.47), channel_id=1, source_target_pairs={{0,8},{4,12},{8,0},{12,4},{1,9},{5,13},{9,1},{13,5},{2,10},{6,14},... | collective-permute-start | bytes 540680 | tf_op jit(solution)/shard_map/ppermute | solution.py:219
  84.2 5.4 %collective-permute-done.19 = f32[1,4,11,8,128]{4,3,2,1,0:T(8,128)S(1)} collective-permute-done((f32[1,4,11,8,128]{4,3,2,1,0:T(8,128)S(1)}, f32[1,4,11,8,128]{4,3,2,1,0:T(8,128)S(1)}, u32[]{:S(2)}, u32[]{:S(2)}) %collective-permute-start.19) | collective-permute-done | bytes 180256 | tf_op jit(solution)/shard_map/ppermute | solution.py:219
  89.6 1.5 %collective-permute-start.24 = (f32[4,1,9,8,128]{4,3,2,1,0:T(8,128)S(1)}, f32[4,1,9,8,128]{4,3,2,1,0:T(8,128)S(1)}, u32[]{:S(2)}, u32[]{:S(2)}) collective-permute-start(f32[4,1,9,8,128]{4,3,2,1,0:T(8,128)S(1)} %get-tuple-element.82), channel_id=1, source_target_pairs={{0,2},{1,3},{2,0},{3,1},{4,6},{5,7},{6,4},{7,5},{8,10},{9,11},{10,... | collective-permute-start | bytes 442376 | tf_op jit(solution)/shard_map/ppermute | solution.py:219
  91.0 1.2 %collective-permute-start.25 = (f32[4,1,9,8,128]{4,3,2,1,0:T(8,128)S(1)}, f32[4,1,9,8,128]{4,3,2,1,0:T(8,128)S(1)}, u32[]{:S(2)}, u32[]{:S(2)}) collective-permute-start(f32[4,1,9,8,128]{4,3,2,1,0:T(8,128)S(1)} %get-tuple-element.81), channel_id=1, source_target_pairs={{0,1},{1,0},{2,3},{3,2},{4,5},{5,4},{6,7},{7,6},{8,9},{9,8},{10,11... | collective-permute-start | bytes 442376 | tf_op jit(solution)/shard_map/ppermute | solution.py:219
  92.2 1.6 %collective-permute-start.23 = (f32[4,1,9,8,128]{4,3,2,1,0:T(8,128)S(1)}, f32[4,1,9,8,128]{4,3,2,1,0:T(8,128)S(1)}, u32[]{:S(2)}, u32[]{:S(2)}) collective-permute-start(f32[4,1,9,8,128]{4,3,2,1,0:T(8,128)S(1)} %get-tuple-element.79), channel_id=1, source_target_pairs={{0,3},{1,2},{2,1},{3,0},{4,7},{5,6},{6,5},{7,4},{8,11},{9,10},{10,... | collective-permute-start | bytes 442376 | tf_op jit(solution)/shard_map/ppermute | solution.py:219
  93.8 3.3 %collective-permute-done.27 = f32[1,4,11,8,128]{4,3,2,1,0:T(8,128)S(1)} collective-permute-done((f32[1,4,11,8,128]{4,3,2,1,0:T(8,128)S(1)}, f32[1,4,11,8,128]{4,3,2,1,0:T(8,128)S(1)}, u32[]{:S(2)}, u32[]{:S(2)}) %collective-permute-start.27) | collective-permute-done | bytes 180256 | tf_op jit(solution)/shard_map/ppermute | solution.py:219
  97.3 1.3 %collective-permute-done.23 = f32[4,1,9,8,128]{4,3,2,1,0:T(8,128)S(1)} collective-permute-done((f32[4,1,9,8,128]{4,3,2,1,0:T(8,128)S(1)}, f32[4,1,9,8,128]{4,3,2,1,0:T(8,128)S(1)}, u32[]{:S(2)}, u32[]{:S(2)}) %collective-permute-start.23) | collective-permute-done | bytes 147488 | tf_op jit(solution)/shard_map/ppermute | solution.py:219
  98.8 1.2 %maximum_maximum_fusion = f32[4,4,20,8,128]{4,3,2,1,0:T(8,128)} fusion(f32[1,4,11,8,128]{4,3,2,1,0:T(8,128)S(1)} %get-tuple-element.42, f32[1,4,11,8,128]{4,3,2,1,0:T(8,128)S(1)} %get-tuple-element.43, f32[1,4,11,8,128]{4,3,2,1,0:T(8,128)S(1)} %get-tuple-element.44, f32[1,4,11,8,128]{4,3,2,1,0:T(8,128)S(1)} %get-tuple-element.41, ...), kind=kLoop, calls=%fused_computation | loop fusion | flops 1310720 | bytes 2621440 | tf_op jit(solution)/shard_map/concatenate | solution.py:302
  (62 shorter events, 1.6 us)
Async XLA Ops:
  0.0 1.3 %copy-start = (f32[64,5,8,128]{3,2,1,0:T(8,128)S(1)}, f32[64,5,8,128]{3,2,1,0:T(8,128)}, u32[]{:S(2)}) copy-start(f32[64,5,8,128]{3,2,1,0:T(8,128)} %density.1) | copy-start | bytes 3932164
  1.3 0.7 copy-start.3
  3.1 9.8 %collective-permute-start.8 = (f32[1,4,10,8,128]{4,3,2,1,0:T(8,128)S(1)}, f32[1,4,10,8,128]{4,3,2,1,0:T(8,128)S(1)}, u32[]{:S(2)}, u32[]{:S(2)}) collective-permute-start(f32[1,4,10,8,128]{4,3,2,1,0:T(8,128)S(1)} %get-tuple-element.27), channel_id=1, source_target_pairs={{0,12},{4,8},{8,4},{12,0},{1,13},{5,9},{9,5},{13,1},{2,14},{6,10},... | collective-permute-start | bytes 491528 | tf_op jit(solution)/shard_map/ppermute | solution.py:219
  7.8 13.4 %collective-permute-start.9 = (f32[1,4,10,8,128]{4,3,2,1,0:T(8,128)S(1)}, f32[1,4,10,8,128]{4,3,2,1,0:T(8,128)S(1)}, u32[]{:S(2)}, u32[]{:S(2)}) collective-permute-start(f32[1,4,10,8,128]{4,3,2,1,0:T(8,128)S(1)} %get-tuple-element.28), channel_id=1, source_target_pairs={{0,8},{4,12},{8,0},{12,4},{1,9},{5,13},{9,1},{13,5},{2,10},{6,14},... | collective-permute-start | bytes 491528 | tf_op jit(solution)/shard_map/ppermute | solution.py:219
  7.8 13.4 %collective-permute-start.10 = (f32[1,4,10,8,128]{4,3,2,1,0:T(8,128)S(1)}, f32[1,4,10,8,128]{4,3,2,1,0:T(8,128)S(1)}, u32[]{:S(2)}, u32[]{:S(2)}) collective-permute-start(f32[1,4,10,8,128]{4,3,2,1,0:T(8,128)S(1)} %get-tuple-element.29), channel_id=1, source_target_pairs={{0,4},{4,0},{8,12},{12,8},{1,5},{5,1},{9,13},{13,9},{2,6},{6,2},{1... | collective-permute-start | bytes 491528 | tf_op jit(solution)/shard_map/ppermute | solution.py:219
  8.5 17.5 %collective-permute-start = (f32[4,1,10,8,128]{4,3,2,1,0:T(8,128)S(1)}, f32[4,1,10,8,128]{4,3,2,1,0:T(8,128)S(1)}, u32[]{:S(2)}, u32[]{:S(2)}) collective-permute-start(f32[4,1,10,8,128]{4,3,2,1,0:T(8,128)S(1)} %get-tuple-element.23), channel_id=1, source_target_pairs={{0,3},{1,2},{2,1},{3,0},{4,7},{5,6},{6,5},{7,4},{8,11},{9,10},{10,... | collective-permute-start | bytes 491528 | tf_op jit(solution)/shard_map/ppermute | solution.py:219
  11.5 14.8 %collective-permute-start.1 = (f32[4,1,10,8,128]{4,3,2,1,0:T(8,128)S(1)}, f32[4,1,10,8,128]{4,3,2,1,0:T(8,128)S(1)}, u32[]{:S(2)}, u32[]{:S(2)}) collective-permute-start(f32[4,1,10,8,128]{4,3,2,1,0:T(8,128)S(1)} %get-tuple-element.24), channel_id=1, source_target_pairs={{0,2},{1,3},{2,0},{3,1},{4,6},{5,7},{6,4},{7,5},{8,10},{9,11},{10,... | collective-permute-start | bytes 491528 | tf_op jit(solution)/shard_map/ppermute | solution.py:219
  12.9 13.3 %collective-permute-start.2 = (f32[4,1,10,8,128]{4,3,2,1,0:T(8,128)S(1)}, f32[4,1,10,8,128]{4,3,2,1,0:T(8,128)S(1)}, u32[]{:S(2)}, u32[]{:S(2)}) collective-permute-start(f32[4,1,10,8,128]{4,3,2,1,0:T(8,128)S(1)} %get-tuple-element.25), channel_id=1, source_target_pairs={{0,1},{1,0},{2,3},{3,2},{4,5},{5,4},{6,7},{7,6},{8,9},{9,8},{10,11... | collective-permute-start | bytes 491528 | tf_op jit(solution)/shard_map/ppermute | solution.py:219
  21.4 7.8 %collective-permute-start.11 = (f32[4,1,10,8,128]{4,3,2,1,0:T(8,128)S(1)}, f32[4,1,10,8,128]{4,3,2,1,0:T(8,128)S(1)}, u32[]{:S(2)}, u32[]{:S(2)}) collective-permute-start(f32[4,1,10,8,128]{4,3,2,1,0:T(8,128)S(1)} %get-tuple-element.59), channel_id=1, source_target_pairs={{0,1},{1,0},{2,3},{3,2},{4,5},{5,4},{6,7},{7,6},{8,9},{9,8},{10,11... | collective-permute-start | bytes 491528 | tf_op jit(solution)/shard_map/ppermute | solution.py:219
  23.1 9.8 %collective-permute-start.12 = (f32[4,1,10,8,128]{4,3,2,1,0:T(8,128)S(1)}, f32[4,1,10,8,128]{4,3,2,1,0:T(8,128)S(1)}, u32[]{:S(2)}, u32[]{:S(2)}) collective-permute-start(f32[4,1,10,8,128]{4,3,2,1,0:T(8,128)S(1)} %get-tuple-element.58), channel_id=1, source_target_pairs={{0,2},{1,3},{2,0},{3,1},{4,6},{5,7},{6,4},{7,5},{8,10},{9,11},{10,... | collective-permute-start | bytes 491528 | tf_op jit(solution)/shard_map/ppermute | solution.py:219
  26.0 8.9 %collective-permute-start.13 = (f32[4,1,10,8,128]{4,3,2,1,0:T(8,128)S(1)}, f32[4,1,10,8,128]{4,3,2,1,0:T(8,128)S(1)}, u32[]{:S(2)}, u32[]{:S(2)}) collective-permute-start(f32[4,1,10,8,128]{4,3,2,1,0:T(8,128)S(1)} %get-tuple-element.57), channel_id=1, source_target_pairs={{0,3},{1,2},{2,1},{3,0},{4,7},{5,6},{6,5},{7,4},{8,11},{9,10},{10,... | collective-permute-start | bytes 491528 | tf_op jit(solution)/shard_map/ppermute | solution.py:219
  26.5 15.8 %collective-permute-start.3 = (f32[1,4,10,8,128]{4,3,2,1,0:T(8,128)S(1)}, f32[1,4,10,8,128]{4,3,2,1,0:T(8,128)S(1)}, u32[]{:S(2)}, u32[]{:S(2)}) collective-permute-start(f32[1,4,10,8,128]{4,3,2,1,0:T(8,128)S(1)} %get-tuple-element.71), channel_id=1, source_target_pairs={{0,12},{4,8},{8,4},{12,0},{1,13},{5,9},{9,5},{13,1},{2,14},{6,10},... | collective-permute-start | bytes 491528 | tf_op jit(solution)/shard_map/ppermute | solution.py:219
  29.3 14.0 %collective-permute-start.4 = (f32[1,4,10,8,128]{4,3,2,1,0:T(8,128)S(1)}, f32[1,4,10,8,128]{4,3,2,1,0:T(8,128)S(1)}, u32[]{:S(2)}, u32[]{:S(2)}) collective-permute-start(f32[1,4,10,8,128]{4,3,2,1,0:T(8,128)S(1)} %get-tuple-element.74), channel_id=1, source_target_pairs={{0,8},{4,12},{8,0},{12,4},{1,9},{5,13},{9,1},{13,5},{2,10},{6,14},... | collective-permute-start | bytes 491528 | tf_op jit(solution)/shard_map/ppermute | solution.py:219
  29.3 14.0 %collective-permute-start.5 = (f32[1,4,10,8,128]{4,3,2,1,0:T(8,128)S(1)}, f32[1,4,10,8,128]{4,3,2,1,0:T(8,128)S(1)}, u32[]{:S(2)}, u32[]{:S(2)}) collective-permute-start(f32[1,4,10,8,128]{4,3,2,1,0:T(8,128)S(1)} %get-tuple-element.73), channel_id=1, source_target_pairs={{0,4},{4,0},{8,12},{12,8},{1,5},{5,1},{9,13},{13,9},{2,6},{6,2},{1... | collective-permute-start | bytes 491528 | tf_op jit(solution)/shard_map/ppermute | solution.py:219
  35.8 16.8 %collective-permute-start.14 = (f32[16,8,8,128]{3,2,1,0:T(8,128)}, f32[16,8,8,128]{3,2,1,0:T(8,128)S(1)}, u32[]{:S(2)}, u32[]{:S(2)}) collective-permute-start(f32[16,8,8,128]{3,2,1,0:T(8,128)} %get-tuple-element.32), channel_id=1, source_target_pairs={{1,0},{2,1},{3,2},{7,3},{6,7},{5,6},{4,5},{8,4},{9,8},{10,9},{11,1... | collective-permute-start | bytes 1572872 | tf_op jit(solution)/shard_map/ppermute | solution.py:278
  40.4 17.4 %collective-permute-start.15 = (f32[16,8,8,128]{3,2,1,0:T(8,128)S(1)}, f32[16,8,8,128]{3,2,1,0:T(8,128)}, u32[]{:S(2)}, u32[]{:S(2)}) collective-permute-start(f32[16,8,8,128]{3,2,1,0:T(8,128)S(1)} %get-tuple-element.33), channel_id=1, source_target_pairs={{0,1},{1,2},{2,3},{3,7},{7,6},{6,5},{5,4},{4,8},{8,9},{9,10},{10,1... | collective-permute-start | bytes 1572872 | tf_op jit(solution)/shard_map/ppermute | solution.py:279
  44.3 16.9 %collective-permute-start.6 = (f32[16,5,8,128]{3,2,1,0:T(8,128)}, f32[16,5,8,128]{3,2,1,0:T(8,128)S(1)}, u32[]{:S(2)}, u32[]{:S(2)}) collective-permute-start(f32[16,5,8,128]{3,2,1,0:T(8,128)} %get-tuple-element.66), channel_id=1, source_target_pairs={{1,0},{2,1},{3,2},{7,3},{6,7},{5,6},{4,5},{8,4},{9,8},{10,9},{11,1... | collective-permute-start | bytes 983048 | tf_op jit(solution)/shard_map/ppermute | solution.py:278
  49.0 13.1 %collective-permute-start.7 = (f32[16,5,8,128]{3,2,1,0:T(8,128)S(1)}, f32[16,5,8,128]{3,2,1,0:T(8,128)S(1)}, u32[]{:S(2)}, u32[]{:S(2)}) collective-permute-start(f32[16,5,8,128]{3,2,1,0:T(8,128)S(1)} %get-tuple-element.65), channel_id=1, source_target_pairs={{0,1},{1,2},{2,3},{3,7},{7,6},{6,5},{5,4},{4,8},{8,9},{9,10},{10,1... | collective-permute-start | bytes 983048 | tf_op jit(solution)/shard_map/ppermute | solution.py:279
  57.8 4.4 %copy-start.1 = (s32[64,9]{0,1:T(8,128)S(1)}, s32[64,9]{0,1:T(8,128)}, u32[]{:S(2)}) copy-start(s32[64,9]{0,1:T(8,128)} %param.6) | copy-start | bytes 6916
  57.8 4.4 %copy-start.2 = (s32[64,5]{0,1:T(8,128)S(1)}, s32[64,5]{0,1:T(8,128)}, u32[]{:S(2)}) copy-start(s32[64,5]{0,1:T(8,128)} %param.7) | copy-start | bytes 3844
  65.9 5.5 %collective-permute-start.20 = (f32[1,4,9,8,128]{4,3,2,1,0:T(8,128)S(1)}, f32[1,4,9,8,128]{4,3,2,1,0:T(8,128)S(1)}, u32[]{:S(2)}, u32[]{:S(2)}) collective-permute-start(f32[1,4,9,8,128]{4,3,2,1,0:T(8,128)S(1)} %get-tuple-element.90), channel_id=1, source_target_pairs={{0,4},{4,0},{8,12},{12,8},{1,5},{5,1},{9,13},{13,9},{2,6},{6,2},{1... | collective-permute-start | bytes 442376 | tf_op jit(solution)/shard_map/ppermute | solution.py:219
  66.1 12.6 %collective-permute-start.21 = (f32[1,4,9,8,128]{4,3,2,1,0:T(8,128)S(1)}, f32[1,4,9,8,128]{4,3,2,1,0:T(8,128)S(1)}, u32[]{:S(2)}, u32[]{:S(2)}) collective-permute-start(f32[1,4,9,8,128]{4,3,2,1,0:T(8,128)S(1)} %get-tuple-element.89), channel_id=1, source_target_pairs={{0,8},{4,12},{8,0},{12,4},{1,9},{5,13},{9,1},{13,5},{2,10},{6,14},... | collective-permute-start | bytes 442376 | tf_op jit(solution)/shard_map/ppermute | solution.py:219
  66.2 12.5 %collective-permute-start.22 = (f32[1,4,9,8,128]{4,3,2,1,0:T(8,128)S(1)}, f32[1,4,9,8,128]{4,3,2,1,0:T(8,128)S(1)}, u32[]{:S(2)}, u32[]{:S(2)}) collective-permute-start(f32[1,4,9,8,128]{4,3,2,1,0:T(8,128)S(1)} %get-tuple-element.88), channel_id=1, source_target_pairs={{0,12},{4,8},{8,4},{12,0},{1,13},{5,9},{9,5},{13,1},{2,14},{6,10},... | collective-permute-start | bytes 442376 | tf_op jit(solution)/shard_map/ppermute | solution.py:219
  70.5 8.6 %collective-permute-start.16 = (f32[4,1,11,8,128]{4,3,2,1,0:T(8,128)S(1)}, f32[4,1,11,8,128]{4,3,2,1,0:T(8,128)S(1)}, u32[]{:S(2)}, u32[]{:S(2)}) collective-permute-start(f32[4,1,11,8,128]{4,3,2,1,0:T(8,128)S(1)} %get-tuple-element.53), channel_id=1, source_target_pairs={{0,3},{1,2},{2,1},{3,0},{4,7},{5,6},{6,5},{7,4},{8,11},{9,10},{10,... | collective-permute-start | bytes 540680 | tf_op jit(solution)/shard_map/ppermute | solution.py:219
  70.7 8.7 %collective-permute-start.17 = (f32[4,1,11,8,128]{4,3,2,1,0:T(8,128)S(1)}, f32[4,1,11,8,128]{4,3,2,1,0:T(8,128)S(1)}, u32[]{:S(2)}, u32[]{:S(2)}) collective-permute-start(f32[4,1,11,8,128]{4,3,2,1,0:T(8,128)S(1)} %get-tuple-element.56), channel_id=1, source_target_pairs={{0,2},{1,3},{2,0},{3,1},{4,6},{5,7},{6,4},{7,5},{8,10},{9,11},{10,... | collective-permute-start | bytes 540680 | tf_op jit(solution)/shard_map/ppermute | solution.py:219
  71.4 8.7 %collective-permute-start.18 = (f32[4,1,11,8,128]{4,3,2,1,0:T(8,128)S(1)}, f32[4,1,11,8,128]{4,3,2,1,0:T(8,128)S(1)}, u32[]{:S(2)}, u32[]{:S(2)}) collective-permute-start(f32[4,1,11,8,128]{4,3,2,1,0:T(8,128)S(1)} %get-tuple-element.55), channel_id=1, source_target_pairs={{0,1},{1,0},{2,3},{3,2},{4,5},{5,4},{6,7},{7,6},{8,9},{9,8},{10,11... | collective-permute-start | bytes 540680 | tf_op jit(solution)/shard_map/ppermute | solution.py:219
  80.4 9.1 %collective-permute-start.19 = (f32[1,4,11,8,128]{4,3,2,1,0:T(8,128)S(1)}, f32[1,4,11,8,128]{4,3,2,1,0:T(8,128)S(1)}, u32[]{:S(2)}, u32[]{:S(2)}) collective-permute-start(f32[1,4,11,8,128]{4,3,2,1,0:T(8,128)S(1)} %get-tuple-element.48), channel_id=1, source_target_pairs={{0,4},{4,0},{8,12},{12,8},{1,5},{5,1},{9,13},{13,9},{2,6},{6,2},{1... | collective-permute-start | bytes 540680 | tf_op jit(solution)/shard_map/ppermute | solution.py:219
  81.3 12.5 %collective-permute-start.26 = (f32[1,4,11,8,128]{4,3,2,1,0:T(8,128)S(1)}, f32[1,4,11,8,128]{4,3,2,1,0:T(8,128)S(1)}, u32[]{:S(2)}, u32[]{:S(2)}) collective-permute-start(f32[1,4,11,8,128]{4,3,2,1,0:T(8,128)S(1)} %get-tuple-element.45), channel_id=1, source_target_pairs={{0,12},{4,8},{8,4},{12,0},{1,13},{5,9},{9,5},{13,1},{2,14},{6,10},... | collective-permute-start | bytes 540680 | tf_op jit(solution)/shard_map/ppermute | solution.py:219
  82.7 14.4 %collective-permute-start.27 = (f32[1,4,11,8,128]{4,3,2,1,0:T(8,128)S(1)}, f32[1,4,11,8,128]{4,3,2,1,0:T(8,128)S(1)}, u32[]{:S(2)}, u32[]{:S(2)}) collective-permute-start(f32[1,4,11,8,128]{4,3,2,1,0:T(8,128)S(1)} %get-tuple-element.47), channel_id=1, source_target_pairs={{0,8},{4,12},{8,0},{12,4},{1,9},{5,13},{9,1},{13,5},{2,10},{6,14},... | collective-permute-start | bytes 540680 | tf_op jit(solution)/shard_map/ppermute | solution.py:219
  89.6 7.6 %collective-permute-start.24 = (f32[4,1,9,8,128]{4,3,2,1,0:T(8,128)S(1)}, f32[4,1,9,8,128]{4,3,2,1,0:T(8,128)S(1)}, u32[]{:S(2)}, u32[]{:S(2)}) collective-permute-start(f32[4,1,9,8,128]{4,3,2,1,0:T(8,128)S(1)} %get-tuple-element.82), channel_id=1, source_target_pairs={{0,2},{1,3},{2,0},{3,1},{4,6},{5,7},{6,4},{7,5},{8,10},{9,11},{10,... | collective-permute-start | bytes 442376 | tf_op jit(solution)/shard_map/ppermute | solution.py:219
  91.0 6.2 %collective-permute-start.25 = (f32[4,1,9,8,128]{4,3,2,1,0:T(8,128)S(1)}, f32[4,1,9,8,128]{4,3,2,1,0:T(8,128)S(1)}, u32[]{:S(2)}, u32[]{:S(2)}) collective-permute-start(f32[4,1,9,8,128]{4,3,2,1,0:T(8,128)S(1)} %get-tuple-element.81), channel_id=1, source_target_pairs={{0,1},{1,0},{2,3},{3,2},{4,5},{5,4},{6,7},{7,6},{8,9},{9,8},{10,11... | collective-permute-start | bytes 442376 | tf_op jit(solution)/shard_map/ppermute | solution.py:219
  92.2 6.4 %collective-permute-start.23 = (f32[4,1,9,8,128]{4,3,2,1,0:T(8,128)S(1)}, f32[4,1,9,8,128]{4,3,2,1,0:T(8,128)S(1)}, u32[]{:S(2)}, u32[]{:S(2)}) collective-permute-start(f32[4,1,9,8,128]{4,3,2,1,0:T(8,128)S(1)} %get-tuple-element.79), channel_id=1, source_target_pairs={{0,3},{1,2},{2,1},{3,0},{4,7},{5,6},{6,5},{7,4},{8,11},{9,10},{10,... | collective-permute-start | bytes 442376 | tf_op jit(solution)/shard_map/ppermute | solution.py:219
